TPU v7x, 32 devices: a whole 2x2x4 slice. The times are simulated.
32 devices in a mesh: seq: 4 (over y, x), dp: 8 (over z, core).
Axes of the slice: x: 2, y: 2, z: 4, core: 2. Of those that a mesh axis runs over, the one named last changes fastest.
Arguments:
- tokens: bfloat16 [8, 512, 2048], P('dp', 'seq'), may hold values from -6 to 6
- segment_ids: int32 [8, 512], P('dp', 'seq'), may hold values from 0 to 511, as said below
- pad_mask: int32 [8, 512], P('dp', 'seq'), may hold values from 0 to 1, as said below
- cotangent: bfloat16 [8, 512, 2048], P('dp', 'seq'), may hold values from -6 to 6
- first_gain: bfloat16 [2048], P(('seq', 'dp')), may hold values from 0.099609375 to 1.8984375
- first_shift: bfloat16 [2048], P(('seq', 'dp')), may hold values from -1.75 to 1.75
- query_weight: bfloat16 [2048, 2048], P(('seq', 'dp')), may hold values from -0.125 to 0.125
- key_weight: bfloat16 [2048, 2048], P(('seq', 'dp')), may hold values from -0.125 to 0.125
- value_weight: bfloat16 [2048, 2048], P(('seq', 'dp')), may hold values from -0.125 to 0.125
- query_bias: bfloat16 [2048], P(('seq', 'dp')), may hold values from -1.75 to 1.75
- value_bias: bfloat16 [2048], P(('seq', 'dp')), may hold values from -1.75 to 1.75
- output_weight: bfloat16 [2048, 2048], P(('seq', 'dp')), may hold values from -1 to 1
- output_bias: bfloat16 [2048], P(('seq', 'dp')), may hold values from -1.75 to 1.75
- second_gain: bfloat16 [2048], P(('seq', 'dp')), may hold values from 0.099609375 to 1.8984375
- second_shift: bfloat16 [2048], P(('seq', 'dp')), may hold values from -1.75 to 1.75
- up_weight: bfloat16 [2048, 8192], P(('seq', 'dp')), may hold values from -0.125 to 0.125
- up_bias: bfloat16 [8192], P(('seq', 'dp')), may hold values from -1.75 to 1.75
- down_weight: bfloat16 [8192, 2048], P(('seq', 'dp')), may hold values from -0.0625 to 0.0625
- down_bias: bfloat16 [2048], P(('seq', 'dp')), may hold values from -1.75 to 1.75
Outputs:
- block_output: bfloat16 [8, 512, 2048], P('dp', 'seq')
- input_grad: float32 [8, 512, 2048], P('dp', 'seq')
- first_gain_grad: float32 [2048], P(('seq', 'dp'))
- first_shift_grad: float32 [2048], P(('seq', 'dp'))
- query_weight_grad: float32 [2048, 2048], P(('seq', 'dp'))
- key_weight_grad: float32 [2048, 2048], P(('seq', 'dp'))
- value_weight_grad: float32 [2048, 2048], P(('seq', 'dp'))
- query_bias_grad: float32 [2048], P(('seq', 'dp'))
- value_bias_grad: float32 [2048], P(('seq', 'dp'))
- output_weight_grad: float32 [2048, 2048], P(('seq', 'dp'))
- output_bias_grad: float32 [2048], P(('seq', 'dp'))
- second_gain_grad: float32 [2048], P(('seq', 'dp'))
- second_shift_grad: float32 [2048], P(('seq', 'dp'))
- up_weight_grad: float32 [2048, 8192], P(('seq', 'dp'))
- up_bias_grad: float32 [8192], P(('seq', 'dp'))
- down_weight_grad: float32 [8192, 2048], P(('seq', 'dp'))
- down_bias_grad: float32 [2048], P(('seq', 'dp'))
Inputs may be any that keep to these rules, and one draw needn't show every extreme that they name: `segment_ids`: within each sequence the ids never fall; a real token's id is the position of its document's first token, and every padding token has id 512 - 1. `pad_mask`: each sequence ends in one or more padding tokens and has none elsewhere.
All inputs are finite; a program needn't handle non-finite values.
Results may differ from a plain program's by a relative error of at most 0.012.
Values may be sent and summed in bfloat16 or wider, within the bound.
No kernel may reach another device: no remote copies, remote signals or barrier semaphores. Data moves between devices by JAX's collectives and lax.ppermute only.
A program may use at most 448 MiB of HBM per device.

v0:
```python
import math

import jax
import jax.numpy as jnp
from jax import lax
from jax.sharding import PartitionSpec as P

H = 16
DH = 128


EPSILON = 1e-05
NEGATIVE = -1e30


def for_sending(shard):
    return jax.tree.map(lambda a: a.astype(jnp.bfloat16) if a.dtype == jnp.float32 else a, shard)


def layer_norm(values, gain_row, shift_row):
    center = values - jnp.mean(values, axis=-1, keepdims=True)
    spread = jnp.mean(center * center, axis=-1, keepdims=True)
    return center * lax.rsqrt(spread + EPSILON) * gain_row + shift_row


def gelu_exact(values):
    return jax.nn.gelu(values, approximate=False)


def matmul(form, left_side, right_side):
    return jnp.einsum(form, left_side, right_side, preferred_element_type=jnp.float32)


def split_pairs(matrix):
    extent = matrix.shape[0]
    return matrix.reshape(extent, H // 2, 2, DH).transpose(1, 2, 0, 3)


def join_pairs(stacked):
    extent = stacked.shape[2]
    return stacked.transpose(2, 0, 1, 3).reshape(extent, H * DH)


def forward(inputs, keep_rows, visible, first_weights, second_weights, fetcher):
    (
        first_gain,
        first_shift,
        query_full,
        key_full,
        value_full,
        query_bias,
        value_bias,
        output_full,
        output_bias,
    ) = first_weights
    second_gain, second_shift, up_full, up_bias, down_full, down_bias = second_weights
    score_scale = 1.0 / math.sqrt(DH)
    normed = layer_norm(
        inputs, first_gain.astype(jnp.float32), first_shift.astype(jnp.float32)
    ).astype(jnp.bfloat16)
    queries = (matmul("td,de->te", normed, query_full) + query_bias.astype(jnp.float32)).astype(
        jnp.bfloat16
    )
    keys_local = matmul("td,de->te", normed, key_full).astype(jnp.bfloat16)
    values_local = (
        matmul("td,de->te", normed, value_full) + value_bias.astype(jnp.float32)
    ).astype(jnp.bfloat16)
    keys_all, values_all = fetcher((keys_local, values_local))

    def head_forward(triple):
        query_pair, key_pair, value_pair = triple
        scores = matmul("hqd,hkd->hqk", query_pair, key_pair) * score_scale
        scores = jnp.where(visible[None], scores, NEGATIVE)
        top_score = jnp.max(scores, axis=2, keepdims=True)
        powers = jnp.exp(scores - top_score)
        totals = jnp.sum(powers, axis=2, keepdims=True)
        weights = (powers / totals).astype(jnp.bfloat16)
        output = matmul("hqk,hkd->hqd", weights, value_pair)
        return (output, (top_score + jnp.log(totals))[..., 0])

    head_outputs, log_totals = lax.map(
        head_forward, (split_pairs(queries), split_pairs(keys_all), split_pairs(values_all))
    )
    joined = join_pairs(head_outputs).astype(jnp.bfloat16)
    branch = (
        matmul("td,de->te", joined, output_full) + output_bias.astype(jnp.float32)
    ) * keep_rows[:, None]
    middle = inputs + branch
    second = layer_norm(
        middle, second_gain.astype(jnp.float32), second_shift.astype(jnp.float32)
    ).astype(jnp.bfloat16)
    hidden = matmul("td,df->tf", second, up_full) + up_bias.astype(jnp.float32)
    active = gelu_exact(hidden).astype(jnp.bfloat16)
    result = middle + matmul("tf,fd->td", active, down_full) + down_bias.astype(jnp.float32)
    return (
        normed,
        queries,
        keys_all,
        values_all,
        log_totals,
        joined,
        middle,
        second,
        hidden,
        active,
        result,
    )


def body(
    tokens,
    segment_ids,
    pad_mask,
    cotangent,
    first_gain,
    first_shift,
    query_weight,
    key_weight,
    value_weight,
    query_bias,
    value_bias,
    output_weight,
    output_bias,
    second_gain,
    second_shift,
    up_weight,
    up_bias,
    down_weight,
    down_bias,
):
    inputs = tokens[0].astype(jnp.float32)
    local_rows = tokens.shape[1]
    segments = segment_ids[0]
    keep_rows = pad_mask[0].astype(jnp.float32)
    code_local = jnp.where(pad_mask[0] == 1, segments, -1)
    key_codes = lax.all_gather(code_local, "seq", axis=0, tiled=True)
    length = key_codes.shape[0]
    query_pos = lax.axis_index("seq") * local_rows + jnp.arange(local_rows, dtype=jnp.int32)
    key_pos = jnp.arange(length, dtype=jnp.int32)
    same_doc = key_codes[None, :] == segments[:, None]
    visible = (key_pos[None, :] <= query_pos[:, None]) & (
        same_doc | (key_pos[None, :] == query_pos[:, None])
    )
    first_shards = (
        first_gain,
        first_shift,
        query_weight,
        key_weight,
        value_weight,
        query_bias,
        value_bias,
        output_weight,
        output_bias,
    )
    second_shards = (second_gain, second_shift, up_weight, up_bias, down_weight, down_bias)
    first_weights = (
        lax.all_gather(first_shards[0], ("seq", "dp"), axis=0, tiled=True),
        lax.all_gather(first_shards[1], ("seq", "dp"), axis=0, tiled=True),
        lax.all_gather(first_shards[2], ("seq", "dp"), axis=0, tiled=True),
        lax.all_gather(first_shards[3], ("seq", "dp"), axis=0, tiled=True),
        lax.all_gather(first_shards[4], ("seq", "dp"), axis=0, tiled=True),
        lax.all_gather(first_shards[5], ("seq", "dp"), axis=0, tiled=True),
        lax.all_gather(first_shards[6], ("seq", "dp"), axis=0, tiled=True),
        lax.all_gather(first_shards[7], ("seq", "dp"), axis=0, tiled=True),
        lax.all_gather(first_shards[8], ("seq", "dp"), axis=0, tiled=True),
    )
    second_weights = (
        lax.all_gather(second_shards[0], ("seq", "dp"), axis=0, tiled=True),
        lax.all_gather(second_shards[1], ("seq", "dp"), axis=0, tiled=True),
        lax.all_gather(second_shards[2], ("seq", "dp"), axis=0, tiled=True),
        lax.all_gather(second_shards[3], ("seq", "dp"), axis=0, tiled=True),
        lax.all_gather(second_shards[4], ("seq", "dp"), axis=0, tiled=True),
        lax.all_gather(second_shards[5], ("seq", "dp"), axis=0, tiled=True),
    )

    def fetch_first(couple):
        return jax.tree.map(
            lambda part, own: part.astype(own.dtype),
            lax.all_gather(for_sending(couple), "seq", axis=0, tiled=True),
            couple,
        )

    stored = forward(inputs, keep_rows, visible, first_weights, second_weights, fetch_first)
    block_output = stored[10]
    first_weights = (
        lax.all_gather(first_shards[0], ("seq", "dp"), axis=0, tiled=True),
        lax.all_gather(first_shards[1], ("seq", "dp"), axis=0, tiled=True),
        lax.all_gather(first_shards[2], ("seq", "dp"), axis=0, tiled=True),
        lax.all_gather(first_shards[3], ("seq", "dp"), axis=0, tiled=True),
        lax.all_gather(first_shards[4], ("seq", "dp"), axis=0, tiled=True),
        lax.all_gather(first_shards[5], ("seq", "dp"), axis=0, tiled=True),
        lax.all_gather(first_shards[6], ("seq", "dp"), axis=0, tiled=True),
        lax.all_gather(first_shards[7], ("seq", "dp"), axis=0, tiled=True),
        lax.all_gather(first_shards[8], ("seq", "dp"), axis=0, tiled=True),
    )
    second_weights = (
        lax.all_gather(second_shards[0], ("seq", "dp"), axis=0, tiled=True),
        lax.all_gather(second_shards[1], ("seq", "dp"), axis=0, tiled=True),
        lax.all_gather(second_shards[2], ("seq", "dp"), axis=0, tiled=True),
        lax.all_gather(second_shards[3], ("seq", "dp"), axis=0, tiled=True),
        lax.all_gather(second_shards[4], ("seq", "dp"), axis=0, tiled=True),
        lax.all_gather(second_shards[5], ("seq", "dp"), axis=0, tiled=True),
    )

    def fetch_again(couple):
        return jax.tree.map(
            lambda part, own: part.astype(own.dtype),
            lax.all_gather(for_sending(couple), "seq", axis=0, tiled=True),
            couple,
        )

    stored = forward(inputs, keep_rows, visible, first_weights, second_weights, fetch_again)
    (
        normed,
        queries,
        keys_all,
        values_all,
        log_totals,
        joined,
        middle,
        second,
        hidden,
        active,
        later_result,
    ) = stored
    (
        gain_first,
        shift_first,
        query_full,
        key_full,
        value_full,
        query_extra,
        value_extra,
        output_full,
        output_extra,
    ) = first_weights
    gain_second, shift_second, up_full, up_extra, down_full, down_extra = second_weights
    score_scale = 1.0 / math.sqrt(DH)
    upstream = cotangent[0]
    upstream_f = upstream.astype(jnp.float32)
    down_bias_grad = jnp.sum(upstream_f, axis=0)
    down_weight_grad = matmul("tf,td->fd", active, upstream)
    active_grad = matmul("td,fd->tf", upstream, down_full)
    hidden_grad = jax.vjp(gelu_exact, hidden)[1](active_grad)[0].astype(jnp.bfloat16)
    up_weight_grad = matmul("td,tf->df", second, hidden_grad)
    up_bias_grad = jnp.sum(hidden_grad.astype(jnp.float32), axis=0)
    second_grad = matmul("tf,df->td", hidden_grad, up_full)
    second_pull = jax.vjp(
        layer_norm, middle, gain_second.astype(jnp.float32), shift_second.astype(jnp.float32)
    )[1]
    middle_norm_grad, second_gain_grad, second_shift_grad = second_pull(second_grad)
    middle_grad = upstream_f + middle_norm_grad
    second_grads = (
        lax.psum_scatter(second_gain_grad, ("seq", "dp"), scatter_dimension=0, tiled=True),
        lax.psum_scatter(second_shift_grad, ("seq", "dp"), scatter_dimension=0, tiled=True),
        lax.psum_scatter(up_weight_grad, ("seq", "dp"), scatter_dimension=0, tiled=True),
        lax.psum_scatter(up_bias_grad, ("seq", "dp"), scatter_dimension=0, tiled=True),
        lax.psum_scatter(down_weight_grad, ("seq", "dp"), scatter_dimension=0, tiled=True),
        lax.psum_scatter(down_bias_grad, ("seq", "dp"), scatter_dimension=0, tiled=True),
    )
    branch_grad = (middle_grad * keep_rows[:, None]).astype(jnp.bfloat16)
    output_weight_grad = matmul("td,te->de", joined, branch_grad)
    output_bias_grad = jnp.sum(branch_grad.astype(jnp.float32), axis=0)
    heads_grad = matmul("te,de->td", branch_grad, output_full).astype(jnp.bfloat16)

    def head_backward(members):
        query_pair, key_pair, value_pair, grad_pair, log_pair = members
        scores = matmul("hqd,hkd->hqk", query_pair, key_pair) * score_scale
        scores = jnp.where(visible[None], scores, NEGATIVE)
        weights = jnp.exp(scores - log_pair[..., None])
        weight_grad = matmul("hqd,hkd->hqk", grad_pair, value_pair)
        center = jnp.sum(weights * weight_grad, axis=2, keepdims=True)
        score_grad = (weights * (weight_grad - center) * score_scale).astype(jnp.bfloat16)
        query_part = matmul("hqk,hkd->hqd", score_grad, key_pair)
        key_part = matmul("hqk,hqd->hkd", score_grad, query_pair)
        value_part = matmul("hqk,hqd->hkd", weights.astype(jnp.bfloat16), grad_pair)
        return (query_part, key_part, value_part)

    query_pairs, key_pairs, value_pairs = lax.map(
        head_backward,
        (
            split_pairs(queries),
            split_pairs(keys_all),
            split_pairs(values_all),
            split_pairs(heads_grad),
            log_totals,
        ),
    )
    query_grad = join_pairs(query_pairs).astype(jnp.bfloat16)
    key_sum, value_sum = (
        lax.psum_scatter(join_pairs(key_pairs), "seq", scatter_dimension=0, tiled=True),
        lax.psum_scatter(join_pairs(value_pairs), "seq", scatter_dimension=0, tiled=True),
    )
    key_grad = key_sum.astype(jnp.bfloat16)
    value_grad = value_sum.astype(jnp.bfloat16)
    query_weight_grad = matmul("td,te->de", normed, query_grad)
    key_weight_grad = matmul("td,te->de", normed, key_grad)
    value_weight_grad = matmul("td,te->de", normed, value_grad)
    query_bias_grad = jnp.sum(query_grad.astype(jnp.float32), axis=0)
    value_bias_grad = jnp.sum(value_grad.astype(jnp.float32), axis=0)
    normed_grad = (
        matmul("te,de->td", query_grad, query_full)
        + matmul("te,de->td", key_grad, key_full)
        + matmul("te,de->td", value_grad, value_full)
    )
    first_pull = jax.vjp(
        layer_norm, inputs, gain_first.astype(jnp.float32), shift_first.astype(jnp.float32)
    )[1]
    input_norm_grad, first_gain_grad, first_shift_grad = first_pull(normed_grad)
    input_grad = middle_grad + input_norm_grad
    first_grads = (
        lax.psum_scatter(first_gain_grad, ("seq", "dp"), scatter_dimension=0, tiled=True),
        lax.psum_scatter(first_shift_grad, ("seq", "dp"), scatter_dimension=0, tiled=True),
        lax.psum_scatter(query_weight_grad, ("seq", "dp"), scatter_dimension=0, tiled=True),
        lax.psum_scatter(key_weight_grad, ("seq", "dp"), scatter_dimension=0, tiled=True),
        lax.psum_scatter(value_weight_grad, ("seq", "dp"), scatter_dimension=0, tiled=True),
        lax.psum_scatter(query_bias_grad, ("seq", "dp"), scatter_dimension=0, tiled=True),
        lax.psum_scatter(value_bias_grad, ("seq", "dp"), scatter_dimension=0, tiled=True),
        lax.psum_scatter(output_weight_grad, ("seq", "dp"), scatter_dimension=0, tiled=True),
        lax.psum_scatter(output_bias_grad, ("seq", "dp"), scatter_dimension=0, tiled=True),
    )
    return (
        (block_output.astype(jnp.bfloat16)[None], input_grad[None])
        + tuple(first_grads)
        + tuple(second_grads)
    )


def solution(mesh):
    placed = (
        P("dp", "seq", None),
        P("dp", "seq"),
        P("dp", "seq"),
        P("dp", "seq", None),
        P(("seq", "dp")),
        P(("seq", "dp")),
        P(("seq", "dp"), None),
        P(("seq", "dp"), None),
        P(("seq", "dp"), None),
        P(("seq", "dp")),
        P(("seq", "dp")),
        P(("seq", "dp"), None),
        P(("seq", "dp")),
        P(("seq", "dp")),
        P(("seq", "dp")),
        P(("seq", "dp"), None),
        P(("seq", "dp")),
        P(("seq", "dp"), None),
        P(("seq", "dp")),
    )
    return jax.shard_map(
        body,
        mesh=mesh,
        in_specs=placed,
        out_specs=(
            P("dp", "seq", None),
            P("dp", "seq", None),
            P(("seq", "dp")),
            P(("seq", "dp")),
            P(("seq", "dp"), None),
            P(("seq", "dp"), None),
            P(("seq", "dp"), None),
            P(("seq", "dp")),
            P(("seq", "dp")),
            P(("seq", "dp"), None),
            P(("seq", "dp")),
            P(("seq", "dp")),
            P(("seq", "dp")),
            P(("seq", "dp"), None),
            P(("seq", "dp")),
            P(("seq", "dp"), None),
            P(("seq", "dp")),
        ),
        check_vma=False,
    )
```

profile of v0, /device:TPU:0, one launch (start us, length us, event | category | flops | bytes accessed | tf_op | source)
XLA Modules:
  0.0 3336.4 jit_solution(10601575912461802471)
XLA Ops:
  16.2 43.0 %all-reduce.18 = (bf16[2048]{0:T(1024)(128)(2,1)S(1)}, bf16[2048]{0:T(1024)(128)(2,1)S(1)}, bf16[2048]{0:T(1024)(128)(2,1)S(1)}, bf16[2048]{0:T(1024)(128)(2,1)S...) all-reduce(bf16[2048]{0:T(1024)(128)(2,1)S(1)} %dynamic-update-slic, ...), channel_id=1, replica_groups=mesh['seq'=4,'dp'=8] {'seq','dp'}, use_global_device_ids=true, to_apply=%add.2 | all-reduce | flops 16384 | bytes 65536
  61.8 29.5 all-gather.17.cloned.1.call-done
  97.2 73.1 %all-gather.13.cloned.1.call-done = bf16[2048,2048]{1,0:T(8,128)(2,1)} async-done(((bf16[64,2048]{1,0:T(8,128)(2,1)}), bf16[2048,2048]{1,0:T(8,128)(2,1)}) %all-gather.13.cloned.1.call-update) | async-done | bytes 8388624 | tf_op jit(solution)/shard_map/all_gather | solution.py:160
  178.0 39.3 %all-gather.1 = bf16[32,1,256]{2,1,0:T(2,128)(2,1)S(1)} all-gather(bf16[1,1,256]{2,1,0:T(2,128)(2,1)S(1)} %reshape.242), channel_id=1, replica_groups=mesh['seq'=4,'dp'=8] {'seq','dp'}, dimensions={0}, use_global_device_ids=true | all-gather | bytes 16896 | tf_op jit(solution)/shard_map/all_gather | solution.py:171
  217.4 8.1 all-gather
  225.5 23.9 all-gather.11.cloned.1.call-done
  255.4 30.2 all-gather.19.cloned.1.call-done
  290.8 32.4 all-gather.15.cloned.1.call-done
  329.9 23.2 while.40
  353.1 50.6 %all-gather.21.cloned.1.call-done = bf16[2048,2048]{1,0:T(8,128)(2,1)} async-done(((bf16[64,2048]{1,0:T(8,128)(2,1)}), bf16[2048,2048]{1,0:T(8,128)(2,1)}) %all-gather.21.cloned.1.call-update) | async-done | bytes 8388624 | tf_op jit(solution)/shard_map/all_gather | solution.py:164
  408.8 191.3 %all-gather.23.cloned.1.call-done = bf16[2048,8192]{1,0:T(8,128)(2,1)} async-done(((bf16[64,8192]{1,0:T(8,128)(2,1)}), bf16[2048,8192]{1,0:T(8,128)(2,1)}) %all-gather.23.cloned.1.call-update) | async-done | bytes 33554448 | tf_op jit(solution)/shard_map/all_gather | solution.py:170
  600.1 18.0 convolution_add_fusion
  618.1 178.0 %all-gather.25.cloned.1.call-done = bf16[8192,2048]{1,0:T(8,128)(2,1)} async-done(((bf16[256,2048]{1,0:T(8,128)(2,1)}), bf16[8192,2048]{1,0:T(8,128)(2,1)}) %all-gather.25.cloned.1.call-update) | async-done | bytes 33554448 | tf_op jit(solution)/shard_map/all_gather | solution.py:172
  796.1 26.9 convert_reduce_fusion
  823.0 17.2 multiply_reduce_fusion.1
  850.9 63.2 %while.41 = (s32[]{:T(128)}, bf16[8,2,128,128]{2,3,1,0:T(8,128)(2,1)S(1)}, f32[8,2,512,128]{2,3,1,0:T(8,128)}, f32[8,2,512,128]{2,3,1,0:T(8,128)}, bf16[8,2,128,...) while((s32[]{:T(128)}, ...), condition=%wide.region_18.19_spmd.clone, body=%wide.region_16.18_spmd.clone.sunk | while | flops 169936384 | bytes 8137865 | solution.py:279
  921.9 43.2 %reduce-scatter.9.cloned.1.call-done = f32[128,2048]{0,1:T(8,128)} async-done(((f32[512,2048]{0,1:T(8,128)}), f32[128,2048]{0,1:T(8,128)}) %reduce-scatter.9.cloned.1.call-update) | async-done | bytes 1048592 | tf_op jit(solution)/shard_map/reduce_scatter | solution.py:291
  972.7 48.2 %reduce-scatter.11.cloned.1.call-done = f32[128,2048]{0,1:T(8,128)} async-done(((f32[512,2048]{0,1:T(8,128)}), f32[128,2048]{0,1:T(8,128)}) %reduce-scatter.11.cloned.1.call-update) | async-done | bytes 1048592 | tf_op jit(solution)/shard_map/reduce_scatter | solution.py:292
  1032.7 8.3 fusion.167
  1042.2 8.1 fusion.245
  1051.6 8.2 fusion.192
  1061.0 8.2 fusion.186
  1070.2 28.7 fusion.117
  1099.5 24.8 fusion.227
  1125.2 35.3 %while.39 = (s32[]{:T(128)}, bf16[8,2,128,128]{2,3,1,0:T(8,128)(2,1)S(1)}, bf16[8,2,128,128]{3,2,1,0:T(8,128)(2,1)}, bf16[8,2,512,128]{3,2,1,0:T(8,128)(2,1)}, b...) while((s32[]{:T(128)}, ...), condition=%wide.region_5.6_spmd.clone, body=%wide.region_2.5_spmd.clone.sunk | while | flops 102171904 | bytes 2826341 | solution.py:81
  1165.6 28.0 fusion.115
  1205.0 143.7 %reduce-scatter.13.cloned.1.call-done = f32[64,2048]{1,0:T(8,128)} async-done(((f32[2048,2048]{1,0:T(8,128)}), f32[64,2048]{1,0:T(8,128)}) %reduce-scatter.13.cloned.1.call-update) | async-done | bytes 524304 | tf_op jit(solution)/shard_map/reduce_scatter | solution.py:314
  1348.7 187.4 %reduce-scatter.19.cloned.1.call-done = f32[64,2048]{1,0:T(8,128)} async-done(((f32[2048,2048]{1,0:T(8,128)}), f32[64,2048]{1,0:T(8,128)}) %reduce-scatter.19.cloned.1.call-update) | async-done | bytes 524304 | tf_op jit(solution)/shard_map/reduce_scatter | solution.py:319
  1536.1 187.2 %reduce-scatter.17.cloned.1.call-done = f32[64,2048]{1,0:T(8,128)} async-done(((f32[2048,2048]{1,0:T(8,128)}), f32[64,2048]{1,0:T(8,128)}) %reduce-scatter.17.cloned.1.call-update) | async-done | bytes 524304 | tf_op jit(solution)/shard_map/reduce_scatter | solution.py:316
  1723.3 187.2 %reduce-scatter.15.cloned.1.call-done = f32[64,2048]{1,0:T(8,128)} async-done(((f32[2048,2048]{1,0:T(8,128)}), f32[64,2048]{1,0:T(8,128)}) %reduce-scatter.15.cloned.1.call-update) | async-done | bytes 524304 | tf_op jit(solution)/shard_map/reduce_scatter | solution.py:315
  1910.6 710.0 %reduce-scatter.23.cloned.1.call-done = f32[256,2048]{1,0:T(8,128)} async-done(((f32[8192,2048]{1,0:T(8,128)}), f32[256,2048]{1,0:T(8,128)}) %reduce-scatter.23.cloned.1.call-update) | async-done | bytes 2097168 | tf_op jit(solution)/shard_map/reduce_scatter | solution.py:258
  2620.6 708.8 %reduce-scatter.21.cloned.1.call-done = f32[64,8192]{1,0:T(8,128)} async-done(((f32[2048,8192]{1,0:T(8,128)}), f32[64,8192]{1,0:T(8,128)}) %reduce-scatter.21.cloned.1.call-update) | async-done | bytes 2097168 | tf_op jit(solution)/shard_map/reduce_scatter | solution.py:256
  (296 shorter events, 229.0 us)
Async XLA Ops:
  7.2 84.2 %all-gather.17.cloned.1.call-start = ((), (), s32[]{:S(2)}) async-start(), calls=%async_computation.11 | async-start | bytes 8650752 | tf_op jit(solution)/shard_map/all_gather | solution.py:161
  7.9 162.3 %all-gather.13.cloned.1.call-start = ((), (), s32[]{:S(2)}) async-start(), calls=%async_computation.9 | async-start | bytes 8650752 | tf_op jit(solution)/shard_map/all_gather | solution.py:160
  8.7 240.7 %all-gather.11.cloned.1.call-start = ((), (), s32[]{:S(2)}) async-start(), calls=%async_computation.8 | async-start | bytes 8650752 | tf_op jit(solution)/shard_map/all_gather | solution.py:159
  9.4 276.2 %all-gather.19.cloned.1.call-start = ((), (), s32[]{:S(2)}) async-start(), calls=%async_computation.12 | async-start | bytes 2621440 | tf_op jit(solution)/shard_map/all_gather | solution.py:179
  61.8 108.4 %copy-start = (bf16[1,128,2048]{2,1,0:T(8,128)(2,1)S(1)}, bf16[1,128,2048]{2,1,0:T(8,128)(2,1)}, u32[]{:S(2)}) copy-start(bf16[1,128,2048]{2,1,0:T(8,128)(2,1)} %param.25) | copy-start | bytes 1572868
  97.1 80.9 %copy-start.24 = (bf16[256]{0:T(256)(128)(2,1)S(1)}, bf16[256]{0:T(256)(128)(2,1)}, u32[]{:S(2)}) copy-start(bf16[256]{0:T(256)(128)(2,1)} %param.41) | copy-start | bytes 1540
  97.1 120.2 %copy-start.18 = (s32[1,128]{1,0:T(1,128)S(1)}, s32[1,128]{1,0:T(1,128)}, u32[]{:S(2)}) copy-start(s32[1,128]{1,0:T(1,128)} %param.26) | copy-start | bytes 1540
  97.1 120.2 %copy-start.25 = (s32[1,128]{1,0:T(1,128)S(1)}, s32[1,128]{1,0:T(1,128)}, u32[]{:S(2)}) copy-start(s32[1,128]{1,0:T(1,128)} %param.27) | copy-start | bytes 1540
  97.1 226.1 %all-gather.15.cloned.1.call-start = ((), (), s32[]{:S(2)}) async-start(), calls=%async_computation.10 | async-start | bytes 2621440 | tf_op jit(solution)/shard_map/all_gather | solution.py:179
  175.8 227.9 %all-gather.21.cloned.1.call-start = ((), (), s32[]{:S(2)}) async-start(), calls=%async_computation.13 | async-start | bytes 8650752 | tf_op jit(solution)/shard_map/all_gather | solution.py:164
  176.4 423.8 %all-gather.23.cloned.1.call-start = ((), (), s32[]{:S(2)}) async-start(), calls=%async_computation.14 | async-start | bytes 34603008 | tf_op jit(solution)/shard_map/all_gather | solution.py:170
  177.1 619.0 %all-gather.25.cloned.1.call-start = ((), (), s32[]{:S(2)}) async-start(), calls=%async_computation.15 | async-start | bytes 34603008 | tf_op jit(solution)/shard_map/all_gather | solution.py:172
  177.9 787.2 %reduce-scatter.9.cloned.1.call-start = ((), (), s32[]{:S(2)}) async-start(), calls=%async_computation.16 | async-start | bytes 5242880 | tf_op jit(solution)/shard_map/reduce_scatter | solution.py:291
  178.0 422.1 %copy-start.14 = (f32[2048]{0:T(1024)}, f32[2048]{0:T(1024)S(1)}, u32[]{:S(2)}) copy-start(f32[2048]{0:T(1024)S(1)} %convert_element_type.180) | copy-start | bytes 24580
  178.0 225.7 %copy-start.19 = (f32[2048]{0:T(1024)}, f32[2048]{0:T(1024)S(1)}, u32[]{:S(2)}) copy-start(f32[2048]{0:T(1024)S(1)} %convert_element_type.176) | copy-start | bytes 24580
  217.3 382.8 %copy-start.16 = (f32[32,1,256]{2,1,0:T(1,128)}, f32[32,1,256]{2,1,0:T(1,128)S(1)}, u32[]{:S(2)}) copy-start(f32[32,1,256]{2,1,0:T(1,128)S(1)} %convert_element_type.206) | copy-start | bytes 98308
  225.5 615.1 %copy-start.21 = (f32[128]{0:T(128)}, f32[128]{0:T(128)S(1)}, u32[]{:S(2)}) copy-start(f32[128]{0:T(128)S(1)} %convert_bitcast_fusion.1) | copy-start | bytes 1540
  353.1 50.6 %copy-start.1 = (bf16[8,2,512,128]{3,2,1,0:T(8,128)(2,1)}, bf16[8,2,512,128]{3,2,1,0:T(8,128)(2,1)S(1)}, u32[]{:S(2)}) copy-start(bf16[8,2,512,128]{3,2,1,0:T(8,128)(2,1)S(1)} %get-tuple-element.639) | copy-start | bytes 6291460
  353.1 55.4 %copy-start.6 = (bf16[8,2,128,128]{2,3,1,0:T(8,128)(2,1)}, bf16[8,2,128,128]{2,3,1,0:T(8,128)(2,1)S(1)}, u32[]{:S(2)}) copy-start(bf16[8,2,128,128]{2,3,1,0:T(8,128)(2,1)S(1)} %get-tuple-element.142) | copy-start | bytes 1572868
  600.1 196.0 %copy-start.11 = (bf16[1,128,2048]{2,1,0:T(8,128)(2,1)S(1)}, bf16[1,128,2048]{2,1,0:T(8,128)(2,1)}, u32[]{:S(2)}) copy-start(bf16[1,128,2048]{2,1,0:T(8,128)(2,1)} %param.28) | copy-start | bytes 1572868
  914.1 106.8 %reduce-scatter.11.cloned.1.call-start = ((), (), s32[]{:S(2)}) async-start(), calls=%async_computation.17 | async-start | bytes 5242880 | tf_op jit(solution)/shard_map/reduce_scatter | solution.py:292
  914.7 278.9 %all-reduce.21.cloned.1.call-start = ((), (), s32[]{:S(2)}) async-start(), calls=%async_computation.24 | async-start | bytes 196608
  972.7 56.9 %copy-start.3 = (f32[128,2048]{1,0:T(8,128)S(1)}, f32[128,2048]{1,0:T(8,128)}, u32[]{:S(2)}) copy-start(f32[128,2048]{1,0:T(8,128)} %copy-done.2) | copy-start | bytes 3145732
  1020.9 8.7 copy-start.12
  1032.7 316.0 %reduce-scatter.13.cloned.1.call-start = ((), (), s32[]{:S(2)}) async-start(), calls=%async_computation.18 | async-start | bytes 17301504 | tf_op jit(solution)/shard_map/reduce_scatter | solution.py:314
  1041.0 495.1 %reduce-scatter.19.cloned.1.call-start = ((), (), s32[]{:S(2)}) async-start(), calls=%async_computation.21 | async-start | bytes 17301504 | tf_op jit(solution)/shard_map/reduce_scatter | solution.py:319
  1050.4 673.0 %reduce-scatter.17.cloned.1.call-start = ((), (), s32[]{:S(2)}) async-start(), calls=%async_computation.20 | async-start | bytes 17301504 | tf_op jit(solution)/shard_map/reduce_scatter | solution.py:316
  1059.8 850.8 %reduce-scatter.15.cloned.1.call-start = ((), (), s32[]{:S(2)}) async-start(), calls=%async_computation.19 | async-start | bytes 17301504 | tf_op jit(solution)/shard_map/reduce_scatter | solution.py:315
  1069.2 1551.4 %reduce-scatter.23.cloned.1.call-start = ((), (), s32[]{:S(2)}) async-start(), calls=%async_computation.23 | async-start | bytes 69206016 | tf_op jit(solution)/shard_map/reduce_scatter | solution.py:258
  1098.9 2230.5 %reduce-scatter.21.cloned.1.call-start = ((), (), s32[]{:S(2)}) async-start(), calls=%async_computation.22 | async-start | bytes 69206016 | tf_op jit(solution)/shard_map/reduce_scatter | solution.py:256
  1125.1 35.4 %copy-start.20 = (f32[2048]{0:T(1024)S(1)}, f32[2048]{0:T(1024)}, u32[]{:S(2)}) copy-start(f32[2048]{0:T(1024)} %copy-done.19) | copy-start | bytes 24580
  1125.2 35.4 %copy-start.22 = (f32[128]{0:T(128)S(1)}, f32[128]{0:T(128)}, u32[]{:S(2)}) copy-start(f32[128]{0:T(128)} %copy-done.21) | copy-start | bytes 1540
  (11 other events, 17.2 us)
Sparse Core Ops, SparseCore 0:
  11.0 80.3 all-gather.16
  94.4 75.8 all-gather.12
  173.3 76.0 all-gather.10
  251.6 33.8 all-gather.18
  287.8 35.2 all-gather.14
  326.0 77.6 all-gather.20
  406.7 193.3 all-gather.22
  603.1 192.9 all-gather.24
  914.2 50.8 reduce-scatter.8
  968.2 52.6 reduce-scatter.10
  1032.8 125.2 all-reduce.20
  1161.0 187.7 reduce-scatter.12
  1351.7 184.3 reduce-scatter.18
  1538.9 184.3 reduce-scatter.16
  1726.2 184.3 reduce-scatter.14
  1913.5 707.0 reduce-scatter.22
  2623.5 705.8 reduce-scatter.20
where the time goes:
time: 3350 us; the launch traced here: 3340 us
  waiting for transfers between devices  2830 us (84%)
  matrix products  345 us (10%)
  blocking collectives  90.4 us (3%)
  local copies, waits for them, and re-layouts  39.8 us (1%)
    reduce_scatter x1, waiting for transfers between devices, body(): lax.psum_scatter(down_weight_grad, ('seq', 'dp'), scatter_dimension=0, ti...  710 us
    reduce_scatter x1, waiting for transfers between devices, body(): lax.psum_scatter(up_weight_grad, ('seq', 'dp'), scatter_dimension=0, tile...  709 us
    dot_general x91, matrix products, matmul(): jnp.einsum(form, left_side, right_side, preferred_element_type=jnp.float32)  334 us
    all_gather x1, waiting for transfers between devices, body(): lax.all_gather(second_shards[2], ('seq', 'dp'), axis=0, tiled=True)  191 us
    reduce_scatter x1, waiting for transfers between devices, body(): lax.psum_scatter(output_weight_grad, ('seq', 'dp'), scatter_dimension=0,...  187 us
    reduce_scatter x1, waiting for transfers between devices, body(): lax.psum_scatter(value_weight_grad, ('seq', 'dp'), scatter_dimension=0, t...  187 us
    reduce_scatter x1, waiting for transfers between devices, body(): lax.psum_scatter(key_weight_grad, ('seq', 'dp'), scatter_dimension=0, til...  187 us
    all_gather x1, waiting for transfers between devices, body(): lax.all_gather(second_shards[4], ('seq', 'dp'), axis=0, tiled=True)  178 us
  transfers between devices with their start and end apart: 17, of which 16 were waited for; matrix products, arithmetic and copies ran while one was open for 8% of the time, Pallas kernels for 0%

commit v1 on v0

v1 whole, which is shorter than its diff:
```python
import math

import jax
import jax.numpy as jnp
from jax import lax
from jax.sharding import Mesh
from jax.sharding import PartitionSpec as P

H = 16
DH = 128
EPSILON = 1e-05
NEGATIVE = -1e30
BF = jnp.bfloat16
F32 = jnp.float32


def dot(form, left, right):
    return jnp.einsum(form, left, right, preferred_element_type=F32)


def normalize(v):
    center = v - jnp.mean(v, axis=-1, keepdims=True)
    inv = lax.rsqrt(jnp.mean(center * center, axis=-1, keepdims=True) + EPSILON)
    return center * inv, inv


def norm_back(xhat, inv, e):
    return (
        e - jnp.mean(e, axis=-1, keepdims=True) - xhat * jnp.mean(e * xhat, axis=-1, keepdims=True)
    ) * inv


def make_body(S, Z):
    bits = [1 << b for b in range(S.bit_length() - 1)]
    halves = len(bits) if len(bits) > 1 else 1

    def xor_seq(v, q):
        return lax.ppermute(v, "seq", [(i, i ^ q) for i in range(S)])

    def swap_core(v):
        return lax.ppermute(v, "core", [(0, 1), (1, 0)])

    def rotation(h):
        return bits[h:] + bits[:h] if bits else []

    def plane_gather(v):
        pieces = jnp.split(v, 2, axis=0)
        done = []
        for h, piece in enumerate(pieces):
            held = {0: piece}
            for b in rotation(h):
                order = sorted(held)
                got = xor_seq(jnp.concatenate([held[q] for q in order], axis=0), b)
                got = jnp.split(got, len(order), axis=0)
                for q, g in zip(order, got):
                    held[q ^ b] = g
            done.append([held[q] for q in range(S)])
        own = jnp.concatenate([done[h][q] for h in range(2) for q in range(S)], axis=0)
        other = swap_core(own)
        return jnp.concatenate([own, other], axis=0)

    def plane_scatter(v):
        rows, feat = v.shape
        t = rows // (2 * S)
        mine, theirs = v[: rows // 2], v[rows // 2 :].astype(BF)
        total = mine + swap_core(theirs).astype(F32)
        total = total.reshape(2, S, t // 2, feat)
        out = []
        for h in range(2):
            held = {q: total[h, q] for q in range(S)}
            for b in reversed(rotation(h)):
                order = sorted(q for q in held if q & b)
                sent = jnp.concatenate([held[q].astype(BF) for q in order], axis=0)
                got = jnp.split(xor_seq(sent, b), len(order), axis=0)
                kept = {}
                for q, g in zip(order, got):
                    kept[q ^ b] = held[q ^ b] + g.astype(F32)
                held = kept
            out.append(held[0])
        return jnp.concatenate(out, axis=0)

    def line_gather(v):
        z = lax.axis_index("z")
        up, down = [v], [v]
        for k in range(1, Z):
            up.append(lax.ppermute(up[-1], "z", [(i, i + 1) for i in range(k - 1, Z - 1)]))
            down.append(lax.ppermute(down[-1], "z", [(i, i - 1) for i in range(1, Z - k + 1)]))
        return [v] + [jnp.where(z + m < Z, down[m], up[Z - m]) for m in range(1, Z)]

    def line_scatter(pieces):
        up = down = None
        for k in range(1, Z):
            a = pieces[Z - k] if up is None else (pieces[Z - k].astype(F32) + up.astype(F32)).astype(BF)
            b = pieces[k] if down is None else (pieces[k].astype(F32) + down.astype(F32)).astype(BF)
            up = lax.ppermute(a, "z", [(i, i + 1) for i in range(k)])
            down = lax.ppermute(b, "z", [(i, i - 1) for i in range(Z - k, Z)])
        total = pieces[0].astype(F32)
        if Z > 1:
            total = total + up.astype(F32) + down.astype(F32)
        return total

    def roll(v, axis, back=False):
        z = lax.axis_index("z")
        start = (Z - z) % Z if back else z
        return lax.dynamic_slice_in_dim(jnp.concatenate([v, v], axis=axis), start, Z, axis=axis)

    def to_relative(v):
        rows, feat = v.shape
        v = v.reshape(rows, S, Z, feat // (S * Z)).transpose(0, 2, 1, 3)
        return roll(v, 1).reshape(rows, feat)

    def from_relative(v):
        rows, feat = v.shape
        v = roll(v.reshape(rows, Z, S, feat // (S * Z)), 1, back=True)
        return v.transpose(0, 2, 1, 3).reshape(rows, feat)

    def roll_columns(v, back=False):
        rows, feat = v.shape
        return roll(v.reshape(rows, Z, feat // Z), 1, back).reshape(rows, feat)

    def exchange(v):
        return lax.all_to_all(v, ("seq", "core"), split_axis=0, concat_axis=0, tiled=True)

    def body(
        tokens, segment_ids, pad_mask, cotangent,
        first_gain, first_shift, query_weight, key_weight, value_weight, query_bias, value_bias,
        output_weight, output_bias, second_gain, second_shift, up_weight, up_bias, down_weight, down_bias,
    ):
        s, z, c = lax.axis_index("seq"), lax.axis_index("z"), lax.axis_index("core")
        n = S * Z * 2
        R, D = query_weight.shape
        RF = down_weight.shape[0]
        t = tokens.shape[1]
        L = S * t
        heads_own = H // (2 * S)
        cols = D // (2 * S)
        scale = 1.0 / math.sqrt(DH)

        small = jnp.concatenate(
            [first_gain, first_shift, query_bias, value_bias, output_bias, second_gain, second_shift, down_bias, up_bias]
        )[None]
        small = jnp.concatenate([small, swap_core(small)], axis=0)
        small = jnp.concatenate([small] + [xor_seq(small, q) for q in range(1, S)], axis=0)
        small = jnp.concatenate(
            [small] + [lax.ppermute(small, "z", [(i, (i - m) % Z) for i in range(Z)]) for m in range(1, Z)], axis=0
        )
        slot = jnp.arange(n)
        place = ((s ^ (slot // 2 % S)) * Z + (z + slot // (2 * S)) % Z) * 2 + (c ^ (slot % 2))
        order = (place[None, :] == slot[:, None]).astype(BF)
        small = dot("ab,bf->af", order, small)
        fields = [small[:, i * R : (i + 1) * R].reshape(-1) for i in range(8)]
        g1, b1, qb, vb, ob, g2, b2, db = fields
        ub = small[:, 8 * R :].reshape(S, Z, 2, RF)

        codes = jnp.stack([segment_ids[0], pad_mask[0]])
        codes = jnp.stack([codes] + [xor_seq(codes, q) for q in range(1, S)])
        codes = jnp.stack([codes, swap_core(codes)])
        codes = codes.reshape(2, S, 2, 2, t // 2).transpose(2, 0, 3, 1, 4).reshape(2, 2, L)
        segments, padding = codes[0], codes[1]
        where_q = (s ^ jnp.arange(S)) * t
        position = (
            where_q[None, :, None] + jnp.arange(2)[:, None, None] * (t // 2) + jnp.arange(t // 2)[None, None, :]
        ).reshape(L)
        same = (segments[:, None, :] == segments[:, :, None]) & (padding[:, None, :] == 1)
        later = position[None, :] <= position[:, None]
        itself = position[None, :] == position[:, None]
        visible = (later[None] & (same | itself[None]))[:, None]
        keep = pad_mask[0].astype(F32)[:, None]

        wo_pieces = line_gather(output_weight)
        qkv = jnp.stack([query_weight, key_weight, value_weight], axis=1).reshape(R, 3, S * 2, cols)
        qkv = exchange(qkv.transpose(2, 0, 1, 3)).reshape(S * 2 * R, 3 * cols)
        wqkv = jnp.concatenate(line_gather(qkv), axis=0)
        up = up_weight.reshape(R, S, Z, 2, RF).transpose(1, 3, 0, 2, 4).reshape(S * 2, R, Z * RF)
        up = exchange(up).reshape(S * 2 * R, Z * RF)
        wup = jnp.concatenate(line_gather(up), axis=0)
        wdown = jnp.concatenate(line_gather(down_weight), axis=0)

        half = Z // 2
        wo = roll(jnp.stack(wo_pieces), 0, back=True)
        keep_part = lax.dynamic_slice_in_dim(wo, c * half, half, axis=0)
        send_part = lax.dynamic_slice_in_dim(wo, (1 - c) * half, half, axis=0)
        got_part = swap_core(send_part)
        wo = jnp.where(
            c == 0,
            jnp.stack([keep_part, got_part], axis=1),
            jnp.stack([got_part, keep_part], axis=1),
        ).reshape(cols, D)

        xf = tokens[0].astype(F32)
        dy = cotangent[0]
        dyf = dy.astype(F32)
        xhat1, inv1 = normalize(xf)
        normed = plane_gather(to_relative((xhat1 * g1 + b1).astype(BF)))
        dy_all = plane_gather(dy)
        qkv_bias = jnp.stack([qb.reshape(S * 2, cols), jnp.zeros((S * 2, cols), F32), vb.reshape(S * 2, cols)], axis=1)
        qkv_bias = lax.dynamic_index_in_dim(qkv_bias, s * 2 + c, 0, keepdims=False).reshape(3 * cols)
        qkv_out = (dot("td,de->te", normed, wqkv) + qkv_bias).astype(BF)
        split = qkv_out.reshape(2, L, 3, heads_own, DH).transpose(2, 0, 3, 1, 4)
        q, k, v = split[0], split[1], split[2]
        scores = jnp.where(visible, dot("bhqd,bhkd->bhqk", q, k) * scale, NEGATIVE)
        top = jnp.max(scores, axis=-1, keepdims=True)
        powers = jnp.exp(scores - top)
        sums = jnp.sum(powers, axis=-1, keepdims=True)
        probs = powers / sums
        out = dot("bhqk,bhkd->bqhd", probs.astype(BF), v)
        heads = out.astype(BF).reshape(2 * L, cols)
        branch = plane_scatter(dot("td,de->te", heads, wo))
        middle = xf + (branch + ob) * keep
        xhat2, inv2 = normalize(middle)
        second = plane_gather(to_relative((xhat2 * g2 + b2).astype(BF)))
        up_row = lax.dynamic_index_in_dim(lax.dynamic_index_in_dim(ub, s, 0, False), c, 1, False).reshape(Z * RF)
        hidden = dot("td,df->tf", second, wup) + up_row
        phi = 0.5 * (1.0 + lax.erf(hidden * math.sqrt(0.5)))
        slope = phi + hidden * jnp.exp(-0.5 * hidden * hidden) * (1.0 / math.sqrt(2 * math.pi))
        active = roll_columns((hidden * phi).astype(BF))

        dactive = roll_columns(dot("td,fd->tf", dy_all, wdown), back=True)
        dhidden = (dactive * slope).astype(BF)
        down_pieces = jnp.split(dot("tf,td->fd", active, dy_all).astype(BF), Z, axis=0)
        down_weight_grad = line_scatter(down_pieces)
        dsecond = from_relative(plane_scatter(dot("tf,df->td", dhidden, wup)))
        up_pieces = jnp.split(dot("td,tf->df", second, dhidden).astype(BF), Z, axis=0)
        up_grad = line_scatter(up_pieces)
        result = plane_scatter(dot("tf,fd->td", active, wdown))
        block_output = (middle + result + db).astype(BF)
        e2 = g2 * dsecond
        dmiddle = dyf + norm_back(xhat2, inv2, e2)
        dbranch = (dmiddle * keep).astype(BF)
        dbranch_all = plane_gather(dbranch)
        dheads = dot("te,de->td", dbranch_all, wo).astype(BF)
        wo_grad = dot("td,te->de", heads, dbranch_all).astype(BF).reshape(half, 2, R, D)
        keep_part = lax.dynamic_index_in_dim(wo_grad, c, 1, False)
        got_part = swap_core(lax.dynamic_index_in_dim(wo_grad, 1 - c, 1, False))
        wo_grad = jnp.where(
            c == 0,
            jnp.concatenate([keep_part, got_part], axis=0),
            jnp.concatenate([got_part, keep_part], axis=0),
        )
        wo_grad = roll(wo_grad, 0)
        output_weight_grad = line_scatter([wo_grad[m] for m in range(Z)])
        dh = dheads.reshape(2, L, heads_own, DH).transpose(0, 2, 1, 3)
        dp = dot("bhqd,bhkd->bhqk", dh, v)
        delta = jnp.sum(probs * dp, axis=-1, keepdims=True)
        dscores = (probs * (dp - delta) * scale).astype(BF)
        dq = dot("bhqk,bhkd->bqhd", dscores, k)
        dk = dot("bhqk,bhqd->bkhd", dscores, q)
        dv = dot("bhqk,bhqd->bkhd", probs.astype(BF), dh)
        dqkv = jnp.stack([dq, dk, dv], axis=2).astype(BF).reshape(2 * L, 3 * cols)
        qkv_pieces = jnp.split(dot("td,te->de", normed, dqkv).astype(BF), Z, axis=0)
        qkv_grad = line_scatter(qkv_pieces)
        dnormed = from_relative(plane_scatter(dot("te,de->td", dqkv, wqkv)))
        input_grad = dmiddle + norm_back(xhat1, inv1, g1 * dnormed)

        qkv_grad = exchange(qkv_grad.astype(BF).reshape(S * 2, R, 3 * cols))
        qkv_grad = qkv_grad.reshape(S * 2, R, 3, cols).transpose(2, 1, 0, 3).reshape(3, R, D).astype(F32)
        up_grad = exchange(up_grad.astype(BF).reshape(S * 2, R, Z * RF))
        up_weight_grad = up_grad.reshape(S, 2, R, Z, RF).transpose(2, 0, 3, 1, 4).reshape(R, -1).astype(F32)

        bias = jnp.sum(dqkv.astype(F32), axis=0).reshape(3, cols)
        spread = jnp.zeros((2, S * 2, cols), F32)
        spread = lax.dynamic_update_slice(spread, jnp.stack([bias[0], bias[2]])[:, None], (0, s * 2 + c, 0))
        wide = jnp.zeros((S, Z, 2, RF), F32)
        wide = lax.dynamic_update_slice(
            wide, jnp.sum(dhidden.astype(F32), axis=0).reshape(1, Z, 1, RF), (s, 0, c, 0)
        )
        rows = [
            jnp.sum(dnormed * xhat1, axis=0),
            jnp.sum(dnormed, axis=0),
            spread[0].reshape(-1),
            spread[1].reshape(-1),
            jnp.sum(dbranch.astype(F32), axis=0),
            jnp.sum(dsecond * xhat2, axis=0),
            jnp.sum(dsecond, axis=0),
            jnp.sum(dyf, axis=0),
        ]
        packed = jnp.concatenate([r.reshape(n, R) for r in rows] + [wide.reshape(n, RF)], axis=1)
        packed = lax.psum_scatter(packed, ("seq", "z", "core"), scatter_dimension=0, tiled=True)[0]
        sg = [packed[i * R : (i + 1) * R] for i in range(8)]
        return (
            block_output[None],
            input_grad[None],
            sg[0],
            sg[1],
            qkv_grad[0],
            qkv_grad[1],
            qkv_grad[2],
            sg[2],
            sg[3],
            output_weight_grad,
            sg[4],
            sg[5],
            sg[6],
            up_weight_grad,
            packed[8 * R :],
            down_weight_grad,
            sg[7],
        )

    return body


def solution(mesh):
    S, DP = mesh.shape["seq"], mesh.shape["dp"]
    Z = DP // 2
    parts = Mesh(mesh.devices.reshape(S, Z, 2), ("seq", "z", "core"))
    every = ("seq", "z", "core")
    token = P(("z", "core"), "seq", None)
    code = P(("z", "core"), "seq")
    vector = P(every)
    matrix = P(every, None)
    return jax.shard_map(
        make_body(S, Z),
        mesh=parts,
        in_specs=(
            token, code, code, token,
            vector, vector, matrix, matrix, matrix, vector, vector,
            matrix, vector, vector, vector, matrix, vector, matrix, vector,
        ),
        out_specs=(
            token, token, vector, vector, matrix, matrix, matrix, vector, vector,
            matrix, vector, vector, vector, matrix, vector, matrix, vector,
        ),
        check_vma=False,
    )
```

time: 3350 us -> 941 us (0.28)
  waiting for transfers between devices: 2830 us -> 368 us
  matrix products: 345 us -> 103 us
  starting transfers between devices: 1.14 us -> 177 us
  local copies, waits for them, and re-layouts: 39.8 us -> 153 us
  other arithmetic: 14.4 us -> 112 us
  blocking collectives: 90.4 us -> 0 us
    reduce_scatter x8 -> x0, waiting for transfers between devices: 2220 us -> none  [the longest x1 710 us: body(): lax.psum_scatter(down_weight_grad, ('seq', 'dp'), scatter_dimension=0, ti...]
    all_gather x8 -> x0, waiting for transfers between devices: 609 us -> none  [the longest x1 191 us: body(): lax.all_gather(second_shards[2], ('seq', 'dp'), axis=0, tiled=True)]
    ppermute x0 -> x101, waiting for transfers between devices: none -> 253 us  [the longest x12 112 us: line_gather(): lax.ppermute(down[-1], 'z', [(i, i - 1) for i in range(1, Z - k + 1)])]
    dot_general x91 -> x19, matrix products: 334 us -> 103 us  [dot(): return jnp.einsum(form, left, right, preferred_element_type=F32)]
    ppermute x0 -> x101, starting transfers between devices: none -> 160 us  [the longest x12 49.8 us: line_scatter(): up = lax.ppermute(a, 'z', [(i, i + 1) for i in range(k)])]
    unnamed x18 -> x2, waiting for transfers between devices: 4.67 us -> 111 us
    all_gather x2 -> x0, blocking collectives: 47.4 us -> none  [the longest x1 39.3 us: body(): lax.all_gather(second_shards[3], ('seq', 'dp'), axis=0, tiled=True)]
    unnamed x1 -> x0, blocking collectives: 43 us -> none
  transfers between devices with their start and end apart: 17 -> 106, of which waited for: 16 -> 38; matrix products, arithmetic and copies ran while one was open for 8% -> 30% of each run, Pallas kernels for 0% -> 0%
where the time goes in v1:
time: 941 us; the launch traced here: 928 us
  waiting for transfers between devices  368 us (39%)
  starting transfers between devices  177 us (19%)
  local copies, waits for them, and re-layouts  153 us (16%)
  other arithmetic  112 us (12%)
  matrix products  103 us (11%)
  between operations  16.2 us (2%)
    ppermute x12, waiting for transfers between devices, line_gather(): lax.ppermute(down[-1], 'z', [(i, i - 1) for i in range(1, Z - k + 1)])  112 us
    unnamed x2, waiting for transfers between devices  111 us
    dot_general x19, matrix products, dot(): return jnp.einsum(form, left, right, preferred_element_type=F32)  103 us
    ppermute x38, waiting for transfers between devices, xor_seq(): return lax.ppermute(v, 'seq', [(i, i ^ q) for i in range(S)])  77.5 us
    ppermute x12, starting transfers between devices, line_scatter(): up = lax.ppermute(a, 'z', [(i, i + 1) for i in range(k)])  49.8 us
    ppermute x38, starting transfers between devices, xor_seq(): return lax.ppermute(v, 'seq', [(i, i ^ q) for i in range(S)])  48.1 us
    unnamed x200, local copies, waits for them, and re-layouts  47.8 us
    ppermute x12, waiting for transfers between devices, line_scatter(): up = lax.ppermute(a, 'z', [(i, i + 1) for i in range(k)])  42 us
  transfers between devices with their start and end apart: 106, of which 38 were waited for; matrix products, arithmetic and copies ran while one was open for 30% of the time, Pallas kernels for 0%

profile of v1, /device:TPU:0, one launch (start us, length us, event | category | flops | bytes accessed | tf_op | source)
XLA Modules:
  0.0 928.0 jit_solution(13065513734823968948)
XLA Ops:
  12.4 6.1 concatenate.184
  103.2 8.8 collective-permute-done.27
  125.9 14.3 %collective-permute-done.12 = bf16[512,768]{1,0:T(8,128)(2,1)S(1)} collective-permute-done((bf16[512,768]{1,0:T(8,128)(2,1)S(1)}, bf16[512,768]{1,0:T(8,128)(2,1)S(1)}, u32[]{:S(2)}, u32[]{:S(2)}) %collective-permute-start.12) | collective-permute-done | bytes 786464 | tf_op jit(solution)/shard_map/ppermute | solution.py:87
  147.1 15.5 %collective-permute-done.16 = bf16[512,768]{1,0:T(8,128)(2,1)S(1)} collective-permute-done((bf16[512,768]{1,0:T(8,128)(2,1)S(1)}, bf16[512,768]{1,0:T(8,128)(2,1)S(1)}, u32[]{:S(2)}, u32[]{:S(2)}) %collective-permute-start.16) | collective-permute-done | bytes 786464 | tf_op jit(solution)/shard_map/ppermute | solution.py:87
  167.3 32.7 %collective-permute-done.17 = bf16[512,768]{1,0:T(8,128)(2,1)S(1)} collective-permute-done((bf16[512,768]{1,0:T(8,128)(2,1)S(1)}, bf16[512,768]{1,0:T(8,128)(2,1)S(1)}, u32[]{:S(2)}, u32[]{:S(2)}) %collective-permute-start.17) | collective-permute-done | bytes 786464 | tf_op jit(solution)/shard_map/ppermute | solution.py:87
  201.8 6.8 add_convert_fusion
  242.5 16.2 %collective-permute-done.40 = bf16[512,1024]{1,0:T(8,128)(2,1)S(1)} collective-permute-done((bf16[512,1024]{1,0:T(8,128)(2,1)}, bf16[512,1024]{1,0:T(8,128)(2,1)S(1)}, u32[]{:S(2)}, u32[]{:S(2)}) %collective-permute-start.40) | collective-permute-done | bytes 1048608 | tf_op jit(solution)/shard_map/ppermute | solution.py:86
  264.9 20.3 %collective-permute-done.49 = bf16[256,2048]{1,0:T(8,128)(2,1)S(1)} collective-permute-done((bf16[256,2048]{1,0:T(8,128)(2,1)}, bf16[256,2048]{1,0:T(8,128)(2,1)S(1)}, u32[]{:S(2)}, u32[]{:S(2)}) %collective-permute-start.49) | collective-permute-done | bytes 1048608 | tf_op jit(solution)/shard_map/ppermute | solution.py:87
  297.7 15.6 %collective-permute-done.43 = bf16[512,1024]{1,0:T(8,128)(2,1)} collective-permute-done((bf16[512,1024]{1,0:T(8,128)(2,1)S(1)}, bf16[512,1024]{1,0:T(8,128)(2,1)}, u32[]{:S(2)}, u32[]{:S(2)}) %collective-permute-start.43) | collective-permute-done | bytes 1048608 | tf_op jit(solution)/shard_map/ppermute | solution.py:87
  319.2 9.3 %collective-permute-done.32 = bf16[128,2048]{1,0:T(8,128)(2,1)S(1)} collective-permute-done((bf16[128,2048]{1,0:T(8,128)(2,1)S(1)}, bf16[128,2048]{1,0:T(8,128)(2,1)S(1)}, u32[]{:S(2)}, u32[]{:S(2)}) %collective-permute-start.32) | collective-permute-done | bytes 524320 | tf_op jit(solution)/shard_map/ppermute | solution.py:38
  368.5 7.1 fusion.65
  382.5 10.2 %convert_reduce_fusion = (f32[1024]{0:T(1024)S(1)}, bf16[1024,1024]{0,1:T(8,128)(2,1)}, bf16[1024,1024]{0,1:T(8,128)(2,1)S(1)}) fusion(f32[1024]{0:T(1024)S(1)} %bitcast.428, f32[1024,4,256]{0,2,1:T(8,128)S(1)} %fusion.8, bf16[1024,2048]{1,0:T(8,128)(2,1)} %copy-done.62, bf16[512,1024]{1,0:T(8,128)(2,1)S(1)} %copy-done.39, ...), kind=kOutput, calls=%fused_computation.24 | convolution fusion | flops 4327472128 | bytes 16785408 | tf_op jit(solution)/shard_map/td,df->tf/dot_general | solution.py:18
  393.5 7.0 convolution_convert_fusion
  417.5 6.4 fusion.67
  429.7 5.4 collective-permute-start.96
  437.1 9.2 fusion.66
  454.0 5.4 collective-permute-start.90
  459.4 13.3 %collective-permute-done.96 = bf16[256,2048]{1,0:T(8,128)(2,1)} collective-permute-done((bf16[256,2048]{1,0:T(8,128)(2,1)}, bf16[256,2048]{1,0:T(8,128)(2,1)}, u32[]{:S(2)}, u32[]{:S(2)}) %collective-permute-start.96) | collective-permute-done | bytes 1048608 | tf_op jit(solution)/shard_map/ppermute | solution.py:95
  485.5 10.3 %collective-permute-done.62 = bf16[128,2048]{1,0:T(8,128)(2,1)S(1)} collective-permute-done((bf16[128,2048]{1,0:T(8,128)(2,1)S(1)}, bf16[128,2048]{1,0:T(8,128)(2,1)S(1)}, u32[]{:S(2)}, u32[]{:S(2)}) %collective-permute-start.62) | collective-permute-done | bytes 524320 | tf_op jit(solution)/shard_map/ppermute | solution.py:38
  502.6 5.4 collective-permute-start.97
  531.8 5.8 collective-permute-done.66
  546.9 8.3 collective-permute-done.67
  578.3 17.4 %collective-permute-done.69 = bf16[128,2048]{1,0:T(8,128)(2,1)S(1)} collective-permute-done((bf16[128,2048]{1,0:T(8,128)(2,1)S(1)}, bf16[128,2048]{1,0:T(8,128)(2,1)S(1)}, u32[]{:S(2)}, u32[]{:S(2)}) %collective-permute-start.69) | collective-permute-done | bytes 524320 | tf_op jit(solution)/shard_map/ppermute | solution.py:38
  635.3 9.0 fusion.31
  644.3 9.3 %fusion.34 = bf16[2,512,1,2,128]{1,4,3,0,2:T(8,128)(2,1)} fusion(f32[2,2,512,512]{2,3,1,0:T(8,128)} %fusion.115, bf16[3,2,2,512,128]{4,3,2,1,0:T(8,128)(2,1)} %bitcast.391, f32[2,2,512,512]{2,3,1,0:T(8,128)} %copy-done.74, f32[2,2,512]{2,1,0:T(2,128)S(1)} %get-tuple-element.160), kind=kOutput, calls=%fused_computation.85 | convolution fusion | flops 275778048 | bytes 17842176 | tf_op jit(solution)/shard_map/bhqk,bhqd->bkhd/dot_general | solution.py:18
  664.4 5.3 convert_element_type.549
  669.8 5.9 fusion.69
  675.7 8.8 convolution_convert_fusion.2
  694.6 11.4 %collective-permute-done.76 = bf16[512,768]{1,0:T(8,128)(2,1)S(1)} collective-permute-done((bf16[512,768]{1,0:T(8,128)(2,1)S(1)}, bf16[512,768]{1,0:T(8,128)(2,1)S(1)}, u32[]{:S(2)}, u32[]{:S(2)}) %collective-permute-start.76) | collective-permute-done | bytes 786464 | tf_op jit(solution)/shard_map/ppermute | solution.py:95
  718.1 12.1 %collective-permute-done.77 = bf16[512,768]{1,0:T(8,128)(2,1)} collective-permute-done((bf16[512,768]{1,0:T(8,128)(2,1)}, bf16[512,768]{1,0:T(8,128)(2,1)}, u32[]{:S(2)}, u32[]{:S(2)}) %collective-permute-start.77) | collective-permute-done | bytes 786464 | tf_op jit(solution)/shard_map/ppermute | solution.py:95
  732.4 7.1 collective-permute-start.78
  807.3 110.8 %all-reduce.3.cloned.1.call-done = f32[32,768]{1,0:T(8,128)} async-done(((f32[32,768]{1,0:T(8,128)}), f32[32,768]{1,0:T(8,128)}) %all-reduce.3.cloned.1.call-update) | async-done | bytes 98320
  (629 shorter events, 475.4 us)
Async XLA Ops:
  22.8 68.3 %all-to-all-start = ((bf16[8,64,3,256]{3,1,2,0:T(8,128)(2,1)}), bf16[8,64,3,256]{3,1,2,0:T(8,128)(2,1)}, u32[]{:S(2)}, u32[]{:S(2)}) async-start(bf16[8,64,3,256]{3,1,2,0:T(8,128)(2,1)} %copy.161), calls=%async_computation | async-start | bytes 1572864 | tf_op jit(solution)/shard_map/all_to_all | solution.py:122
  27.1 52.5 %collective-permute-start.23 = (bf16[64,2048]{1,0:T(8,128)(2,1)}, bf16[64,2048]{1,0:T(8,128)(2,1)}, u32[]{:S(2)}, u32[]{:S(2)}) collective-permute-start(bf16[64,2048]{1,0:T(8,128)(2,1)} %param.30), channel_id=1, source_target_pairs={{0,2},{2,4},{4,6},{1,3},{3,5},{5,7},{8,10},{10,12},{12,14},{9,11},... | collective-permute-start | bytes 786440 | tf_op jit(solution)/shard_map/ppermute | solution.py:86
  48.4 35.4 %collective-permute-start.22 = (bf16[64,2048]{1,0:T(8,128)(2,1)}, bf16[64,2048]{1,0:T(8,128)(2,1)}, u32[]{:S(2)}, u32[]{:S(2)}) collective-permute-start(bf16[64,2048]{1,0:T(8,128)(2,1)} %param.30), channel_id=1, source_target_pairs={{2,0},{4,2},{6,4},{3,1},{5,3},{7,5},{10,8},{12,10},{14,12},{11,9},... | collective-permute-start | bytes 786440 | tf_op jit(solution)/shard_map/ppermute | solution.py:87
  62.0 178.4 %collective-permute-start.46 = (bf16[256,2048]{1,0:T(8,128)(2,1)}, bf16[256,2048]{1,0:T(8,128)(2,1)}, u32[]{:S(2)}, u32[]{:S(2)}) collective-permute-start(bf16[256,2048]{1,0:T(8,128)(2,1)} %param.36), channel_id=1, source_target_pairs={{0,2},{2,4},{4,6},{1,3},{3,5},{5,7},{8,10},{10,12},{12,14},{9,11},... | collective-permute-start | bytes 3145736 | tf_op jit(solution)/shard_map/ppermute | solution.py:86
  83.9 41.5 %collective-permute-start.57 = (bf16[128,2048]{1,0:T(8,128)(2,1)}, bf16[128,2048]{1,0:T(8,128)(2,1)}, u32[]{:S(2)}, u32[]{:S(2)}) collective-permute-start(bf16[128,2048]{1,0:T(8,128)(2,1)} %pad_maximum_fusion.19), channel_id=1, source_target_pairs={{0,16},{8,24},{16,0},{24,8},{1,17},{9,25},{17,1},{25,9},{2,18},{10... | collective-permute-start | bytes 1572872 | tf_op jit(solution)/shard_map/ppermute | solution.py:38
  91.1 142.6 %all-to-all-start.1 = ((bf16[8,64,1024]{2,1,0:T(8,128)(2,1)}), bf16[8,64,1024]{2,1,0:T(8,128)(2,1)}, u32[]{:S(2)}, u32[]{:S(2)}) async-start(bf16[8,64,1024]{2,1,0:T(8,128)(2,1)} %reshape.918), calls=%async_computation.1 | async-start | bytes 2097152 | tf_op jit(solution)/shard_map/all_to_all | solution.py:122
  125.1 40.2 %collective-permute-start.11 = (bf16[512,2048]{1,0:T(8,128)(2,1)}, bf16[512,2048]{1,0:T(8,128)(2,1)S(1)}, u32[]{:S(2)}, u32[]{:S(2)}) collective-permute-start(bf16[512,2048]{1,0:T(8,128)(2,1)} %get-tuple-element.116), channel_id=1, source_target_pairs={{0,1},{1,0},{2,3},{3,2},{4,5},{5,4},{6,7},{7,6},{8,9},{9,8},{10,11... | collective-permute-start | bytes 6291464 | tf_op jit(solution)/shard_map/ppermute | solution.py:41
  145.8 90.7 %collective-permute-start.45 = (bf16[256,2048]{1,0:T(8,128)(2,1)}, bf16[256,2048]{1,0:T(8,128)(2,1)}, u32[]{:S(2)}, u32[]{:S(2)}) collective-permute-start(bf16[256,2048]{1,0:T(8,128)(2,1)} %param.36), channel_id=1, source_target_pairs={{2,0},{4,2},{6,4},{3,1},{5,3},{7,5},{10,8},{12,10},{14,12},{11,9},... | collective-permute-start | bytes 3145736 | tf_op jit(solution)/shard_map/ppermute | solution.py:87
  162.6 37.3 %collective-permute-start.17 = (bf16[512,768]{1,0:T(8,128)(2,1)S(1)}, bf16[512,768]{1,0:T(8,128)(2,1)S(1)}, u32[]{:S(2)}, u32[]{:S(2)}) collective-permute-start(bf16[512,768]{1,0:T(8,128)(2,1)S(1)} %collective-permute-done.16), channel_id=1, source_target_pairs={{2,0},{3,1},{10,8},{11,9},{18,16},{19,17},{26,24},{27,25}} | collective-permute-start | bytes 2359304 | tf_op jit(solution)/shard_map/ppermute | solution.py:87
  164.6 35.5 %collective-permute-start.15 = (bf16[512,768]{1,0:T(8,128)(2,1)S(1)}, bf16[512,768]{1,0:T(8,128)(2,1)S(1)}, u32[]{:S(2)}, u32[]{:S(2)}) collective-permute-start(bf16[512,768]{1,0:T(8,128)(2,1)S(1)} %collective-permute-done.14), channel_id=1, source_target_pairs={{4,6},{5,7},{12,14},{13,15},{20,22},{21,23},{28,30},{29,31}} | collective-permute-start | bytes 2359304 | tf_op jit(solution)/shard_map/ppermute | solution.py:86
  165.4 66.0 %collective-permute-start.59 = (bf16[128,2048]{1,0:T(8,128)(2,1)}, bf16[128,2048]{1,0:T(8,128)(2,1)}, u32[]{:S(2)}, u32[]{:S(2)}) collective-permute-start(bf16[128,2048]{1,0:T(8,128)(2,1)} %pad_maximum_fusion.20), channel_id=1, source_target_pairs={{0,8},{8,0},{16,24},{24,16},{1,9},{9,1},{17,25},{25,17},{2,10},{10... | collective-permute-start | bytes 1572872 | tf_op jit(solution)/shard_map/ppermute | solution.py:38
  230.5 56.0 %collective-permute-start.29 = (bf16[512,2048]{1,0:T(8,128)(2,1)}, bf16[512,2048]{1,0:T(8,128)(2,1)}, u32[]{:S(2)}, u32[]{:S(2)}) collective-permute-start(bf16[512,2048]{1,0:T(8,128)(2,1)} %slice.581), channel_id=1, source_target_pairs={{0,1},{1,0},{2,3},{3,2},{4,5},{5,4},{6,7},{7,6},{8,9},{9,8},{10,11... | collective-permute-start | bytes 6291464 | tf_op jit(solution)/shard_map/ppermute | solution.py:41
  236.6 48.7 %collective-permute-start.49 = (bf16[256,2048]{1,0:T(8,128)(2,1)}, bf16[256,2048]{1,0:T(8,128)(2,1)S(1)}, u32[]{:S(2)}, u32[]{:S(2)}) collective-permute-start(bf16[256,2048]{1,0:T(8,128)(2,1)} %collective-permute-done.45), channel_id=1, source_target_pairs={{2,0},{4,2},{3,1},{5,3},{10,8},{12,10},{11,9},{13,11},{18,16},{20,... | collective-permute-start | bytes 3145736 | tf_op jit(solution)/shard_map/ppermute | solution.py:87
  240.5 54.0 %collective-permute-start.60 = (bf16[512,2048]{1,0:T(8,128)(2,1)}, bf16[512,2048]{1,0:T(8,128)(2,1)S(1)}, u32[]{:S(2)}, u32[]{:S(2)}) collective-permute-start(bf16[512,2048]{1,0:T(8,128)(2,1)} %get-tuple-element.100), channel_id=1, source_target_pairs={{0,1},{1,0},{2,3},{3,2},{4,5},{5,4},{6,7},{7,6},{8,9},{9,8},{10,11... | collective-permute-start | bytes 6291464 | tf_op jit(solution)/shard_map/ppermute | solution.py:41
  263.3 52.1 %collective-permute-start.41 = (bf16[512,1024]{1,0:T(8,128)(2,1)S(1)}, bf16[512,1024]{1,0:T(8,128)(2,1)}, u32[]{:S(2)}, u32[]{:S(2)}) collective-permute-start(bf16[512,1024]{1,0:T(8,128)(2,1)S(1)} %collective-permute-done.40), channel_id=1, source_target_pairs={{2,4},{4,6},{3,5},{5,7},{10,12},{12,14},{11,13},{13,15},{18,20},{2... | collective-permute-start | bytes 3145736 | tf_op jit(solution)/shard_map/ppermute | solution.py:86
  286.5 49.1 %collective-permute-start.50 = (bf16[256,2048]{1,0:T(8,128)(2,1)S(1)}, bf16[256,2048]{1,0:T(8,128)(2,1)S(1)}, u32[]{:S(2)}, u32[]{:S(2)}) collective-permute-start(bf16[256,2048]{1,0:T(8,128)(2,1)S(1)} %collective-permute-done.49), channel_id=1, source_target_pairs={{2,0},{3,1},{10,8},{11,9},{18,16},{19,17},{26,24},{27,25}} | collective-permute-start | bytes 3145736 | tf_op jit(solution)/shard_map/ppermute | solution.py:87
  294.5 52.6 %collective-permute-start.48 = (bf16[256,2048]{1,0:T(8,128)(2,1)}, bf16[256,2048]{1,0:T(8,128)(2,1)}, u32[]{:S(2)}, u32[]{:S(2)}) collective-permute-start(bf16[256,2048]{1,0:T(8,128)(2,1)} %collective-permute-done.47), channel_id=1, source_target_pairs={{4,6},{5,7},{12,14},{13,15},{20,22},{21,23},{28,30},{29,31}} | collective-permute-start | bytes 3145736 | tf_op jit(solution)/shard_map/ppermute | solution.py:86
  313.3 63.3 %collective-permute-start.44 = (bf16[512,1024]{1,0:T(8,128)(2,1)}, bf16[512,1024]{1,0:T(8,128)(2,1)}, u32[]{:S(2)}, u32[]{:S(2)}) collective-permute-start(bf16[512,1024]{1,0:T(8,128)(2,1)} %collective-permute-done.43), channel_id=1, source_target_pairs={{2,0},{3,1},{10,8},{11,9},{18,16},{19,17},{26,24},{27,25}} | collective-permute-start | bytes 3145736 | tf_op jit(solution)/shard_map/ppermute | solution.py:87
  328.5 50.6 %collective-permute-start.42 = (bf16[512,1024]{1,0:T(8,128)(2,1)}, bf16[512,1024]{1,0:T(8,128)(2,1)}, u32[]{:S(2)}, u32[]{:S(2)}) collective-permute-start(bf16[512,1024]{1,0:T(8,128)(2,1)} %collective-permute-done.41), channel_id=1, source_target_pairs={{4,6},{5,7},{12,14},{13,15},{20,22},{21,23},{28,30},{29,31}} | collective-permute-start | bytes 3145736 | tf_op jit(solution)/shard_map/ppermute | solution.py:86
  413.4 36.8 %collective-permute-start.89 = (bf16[512,1024]{1,0:T(8,128)(2,1)}, bf16[512,1024]{1,0:T(8,128)(2,1)S(1)}, u32[]{:S(2)}, u32[]{:S(2)}) collective-permute-start(bf16[512,1024]{1,0:T(8,128)(2,1)} %get-tuple-element.46), channel_id=1, source_target_pairs={{0,2},{1,3},{8,10},{9,11},{16,18},{17,19},{24,26},{25,27}} | collective-permute-start | bytes 3145736 | tf_op jit(solution)/shard_map/ppermute | solution.py:95
  415.8 34.4 %collective-permute-start.92 = (bf16[512,1024]{1,0:T(8,128)(2,1)}, bf16[512,1024]{1,0:T(8,128)(2,1)}, u32[]{:S(2)}, u32[]{:S(2)}) collective-permute-start(bf16[512,1024]{1,0:T(8,128)(2,1)} %get-tuple-element.47), channel_id=1, source_target_pairs={{6,4},{7,5},{14,12},{15,13},{22,20},{23,21},{30,28},{31,29}} | collective-permute-start | bytes 3145736 | tf_op jit(solution)/shard_map/ppermute | solution.py:96
  425.6 52.4 %collective-permute-start.61 = (bf16[512,2048]{1,0:T(8,128)(2,1)}, bf16[512,2048]{1,0:T(8,128)(2,1)}, u32[]{:S(2)}, u32[]{:S(2)}) collective-permute-start(bf16[512,2048]{1,0:T(8,128)(2,1)} %slice.579), channel_id=1, source_target_pairs={{0,1},{1,0},{2,3},{3,2},{4,5},{5,4},{6,7},{7,6},{8,9},{9,8},{10,11... | collective-permute-start | bytes 6291464 | tf_op jit(solution)/shard_map/ppermute | solution.py:41
  429.7 43.0 %collective-permute-start.96 = (bf16[256,2048]{1,0:T(8,128)(2,1)}, bf16[256,2048]{1,0:T(8,128)(2,1)}, u32[]{:S(2)}, u32[]{:S(2)}) collective-permute-start(bf16[256,2048]{1,0:T(8,128)(2,1)} %get-tuple-element.38), channel_id=1, source_target_pairs={{0,2},{2,4},{1,3},{3,5},{8,10},{10,12},{9,11},{11,13},{16,18},{18,... | collective-permute-start | bytes 3145736 | tf_op jit(solution)/shard_map/ppermute | solution.py:95
  435.1 39.3 %collective-permute-start.99 = (bf16[256,2048]{1,0:T(8,128)(2,1)}, bf16[256,2048]{1,0:T(8,128)(2,1)}, u32[]{:S(2)}, u32[]{:S(2)}) collective-permute-start(bf16[256,2048]{1,0:T(8,128)(2,1)} %get-tuple-element.39), channel_id=1, source_target_pairs={{4,2},{6,4},{5,3},{7,5},{12,10},{14,12},{13,11},{15,13},{20,18},{2... | collective-permute-start | bytes 3145736 | tf_op jit(solution)/shard_map/ppermute | solution.py:96
  454.0 73.1 %collective-permute-start.90 = (bf16[512,1024]{1,0:T(8,128)(2,1)}, bf16[512,1024]{1,0:T(8,128)(2,1)}, u32[]{:S(2)}, u32[]{:S(2)}) collective-permute-start(bf16[512,1024]{1,0:T(8,128)(2,1)} %get-tuple-element.44), channel_id=1, source_target_pairs={{0,2},{2,4},{1,3},{3,5},{8,10},{10,12},{9,11},{11,13},{16,18},{18,... | collective-permute-start | bytes 3145736 | tf_op jit(solution)/shard_map/ppermute | solution.py:95
  472.7 55.1 %collective-permute-start.93 = (bf16[512,1024]{1,0:T(8,128)(2,1)}, bf16[512,1024]{1,0:T(8,128)(2,1)}, u32[]{:S(2)}, u32[]{:S(2)}) collective-permute-start(bf16[512,1024]{1,0:T(8,128)(2,1)} %get-tuple-element.45), channel_id=1, source_target_pairs={{4,2},{6,4},{5,3},{7,5},{12,10},{14,12},{13,11},{15,13},{20,18},{2... | collective-permute-start | bytes 3145736 | tf_op jit(solution)/shard_map/ppermute | solution.py:96
  498.9 99.1 %collective-permute-start.100 = (bf16[256,2048]{1,0:T(8,128)(2,1)}, bf16[256,2048]{1,0:T(8,128)(2,1)}, u32[]{:S(2)}, u32[]{:S(2)}) collective-permute-start(bf16[256,2048]{1,0:T(8,128)(2,1)} %get-tuple-element.37), channel_id=1, source_target_pairs={{2,0},{4,2},{6,4},{3,1},{5,3},{7,5},{10,8},{12,10},{14,12},{11,9},... | collective-permute-start | bytes 3145736 | tf_op jit(solution)/shard_map/ppermute | solution.py:96
  502.6 95.5 %collective-permute-start.97 = (bf16[256,2048]{1,0:T(8,128)(2,1)}, bf16[256,2048]{1,0:T(8,128)(2,1)}, u32[]{:S(2)}, u32[]{:S(2)}) collective-permute-start(bf16[256,2048]{1,0:T(8,128)(2,1)} %get-tuple-element.36), channel_id=1, source_target_pairs={{0,2},{2,4},{4,6},{1,3},{3,5},{5,7},{8,10},{10,12},{12,14},{9,11},... | collective-permute-start | bytes 3145736 | tf_op jit(solution)/shard_map/ppermute | solution.py:95
  555.2 48.2 %collective-permute-start.55 = (bf16[64,2048]{1,0:T(8,128)(2,1)}, bf16[64,2048]{1,0:T(8,128)(2,1)}, u32[]{:S(2)}, u32[]{:S(2)}) collective-permute-start(bf16[64,2048]{1,0:T(8,128)(2,1)} %get-tuple-element.53), channel_id=1, source_target_pairs={{0,16},{8,24},{16,0},{24,8},{1,17},{9,25},{17,1},{25,9},{2,18},{10... | collective-permute-start | bytes 786440 | tf_op jit(solution)/shard_map/ppermute | solution.py:38
  565.6 41.2 %all-to-all-start.3 = ((bf16[8,64,1024]{2,1,0:T(8,128)(2,1)}), bf16[8,64,1024]{2,1,0:T(8,128)(2,1)}, u32[]{:S(2)}, u32[]{:S(2)}) async-start(bf16[8,64,1024]{2,1,0:T(8,128)(2,1)} %bitcast.399), calls=%async_computation.3 | async-start | bytes 2097152 | tf_op jit(solution)/shard_map/all_to_all | solution.py:122
  690.5 50.3 %collective-permute-start.71 = (bf16[512,2048]{1,0:T(8,128)(2,1)}, bf16[512,2048]{1,0:T(8,128)(2,1)}, u32[]{:S(2)}, u32[]{:S(2)}) collective-permute-start(bf16[512,2048]{1,0:T(8,128)(2,1)} %slice.578), channel_id=1, source_target_pairs={{0,1},{1,0},{2,3},{3,2},{4,5},{5,4},{6,7},{7,6},{8,9},{9,8},{10,11... | collective-permute-start | bytes 6291464 | tf_op jit(solution)/shard_map/ppermute | solution.py:41
  764.2 154.0 %all-reduce.3.cloned.1.call-start = ((), (), s32[]{:S(2)}) async-start(), calls=%async_computation.4 | async-start | bytes 196608
  (152 other events, 2797.3 us)
Sparse Core Ops, SparseCore 0:
  799.0 119.1 all-reduce.2

commit v2 on v1

v2 whole, which is shorter than its diff:
```python
import functools
import math

import jax
import jax.numpy as jnp
from jax import lax
from jax.experimental import pallas as pl
from jax.experimental.pallas import tpu as pltpu
from jax.sharding import Mesh
from jax.sharding import PartitionSpec as P

H = 16
DH = 128
EPSILON = 1e-05
NEGATIVE = -1e30
BF = jnp.bfloat16
F32 = jnp.float32
SCALE = 1.0 / math.sqrt(DH)


def dot(form, left, right):
    return jnp.einsum(form, left, right, preferred_element_type=F32)


def normalize(v):
    center = v - jnp.mean(v, axis=-1, keepdims=True)
    inv = lax.rsqrt(jnp.mean(center * center, axis=-1, keepdims=True) + EPSILON)
    return center * inv, inv


def norm_back(xhat, inv, e):
    return (
        e - jnp.mean(e, axis=-1, keepdims=True) - xhat * jnp.mean(e * xhat, axis=-1, keepdims=True)
    ) * inv


def nt(a, b):
    return lax.dot_general(a, b, (((1,), (1,)), ((), ())), preferred_element_type=F32)


def nn(a, b):
    return lax.dot_general(a, b, (((1,), (0,)), ((), ())), preferred_element_type=F32)


def tn(a, b):
    return lax.dot_general(a, b, (((0,), (0,)), ((), ())), preferred_element_type=F32)


def seen(q_ref, k_ref):
    q_pos, q_doc = q_ref[:, 0:1], q_ref[:, 1:2]
    k_pos, k_doc = k_ref[0:1, :], k_ref[1:2, :]
    return ((k_pos <= q_pos) & (k_doc == q_doc)) | (k_pos == q_pos)


def softmax(q, k, visible):
    scores = jnp.where(visible, nt(q, k) * SCALE, NEGATIVE)
    powers = jnp.exp(scores - jnp.max(scores, axis=1, keepdims=True))
    return powers / jnp.sum(powers, axis=1, keepdims=True)


def attend_kernel(heads, q_info, k_info, qkv_ref, out_ref):
    visible = seen(q_info, k_info)
    for h in range(heads):
        q, k, v = (qkv_ref[:, (part * heads + h) * DH : (part * heads + h + 1) * DH] for part in range(3))
        probs = softmax(q, k, visible).astype(BF)
        out_ref[:, h * DH : (h + 1) * DH] = nn(probs, v).astype(BF)


def attend_back_kernel(heads, q_info, k_info, qkv_ref, grad_ref, out_ref):
    visible = seen(q_info, k_info)
    for h in range(heads):
        q, k, v = (qkv_ref[:, (part * heads + h) * DH : (part * heads + h + 1) * DH] for part in range(3))
        grad = grad_ref[:, h * DH : (h + 1) * DH]
        probs = softmax(q, k, visible)
        dp = nt(grad, v)
        delta = jnp.sum(probs * dp, axis=1, keepdims=True)
        dscores = (probs * (dp - delta) * SCALE).astype(BF)
        parts = (nn(dscores, k), tn(dscores, q), tn(probs.astype(BF), grad))
        for part, value in enumerate(parts):
            out_ref[:, (part * heads + h) * DH : (part * heads + h + 1) * DH] = value.astype(BF)


def attend_call(kernel, heads, columns, matmuls, *args):
    rows = args[2].shape[0]
    return pl.pallas_call(
        functools.partial(kernel, heads),
        out_shape=jax.ShapeDtypeStruct((rows, columns), BF),
        compiler_params=pltpu.CompilerParams(vmem_limit_bytes=56 * 1024 * 1024),
        cost_estimate=pl.CostEstimate(
            flops=2 * matmuls * heads * rows * rows * DH, bytes_accessed=8 * rows * columns, transcendentals=heads * rows * rows
        ),
    )(*args)


def make_body(S, Z):
    def xor_seq(v, q):
        return lax.ppermute(v, "seq", [(i, i ^ q) for i in range(S)])

    def swap_core(v):
        return lax.ppermute(v, "core", [(0, 1), (1, 0)])

    def plane_gather(v):
        own = jnp.concatenate([v] + [xor_seq(v, q) for q in range(1, S)], axis=0)
        return own, swap_core(own)

    def plane_scatter(make):
        got = swap_core(make(1).astype(BF))
        total = make(0) + got.astype(F32)
        blocks = total.reshape(S, -1, total.shape[1])
        mine = blocks[0]
        for q in range(1, S):
            mine = mine + xor_seq(blocks[q].astype(BF), q).astype(F32)
        return mine

    def everyone(v):
        return lax.all_to_all(v, ("seq", "z", "core"), split_axis=0, concat_axis=0, tiled=True)

    def in_plane(v):
        return lax.all_to_all(v, ("seq", "core"), split_axis=0, concat_axis=0, tiled=True)

    def body(
        tokens, segment_ids, pad_mask, cotangent,
        first_gain, first_shift, query_weight, key_weight, value_weight, query_bias, value_bias,
        output_weight, output_bias, second_gain, second_shift, up_weight, up_bias, down_weight, down_bias,
    ):
        s, z, c = lax.axis_index("seq"), lax.axis_index("z"), lax.axis_index("core")
        n, tp = S * Z * 2, S * 2
        R, D = query_weight.shape
        RF = down_weight.shape[0]
        t = tokens.shape[1]
        L = S * t
        heads_own = H // tp
        cols = D // tp
        half = Z // 2

        def to_weight_order(v):
            return v.reshape(-1, S, Z, 2 * R).transpose(0, 2, 1, 3).reshape(-1, D)

        def from_weight_order(v):
            return v.reshape(-1, Z, S, 2 * R).transpose(0, 2, 1, 3).reshape(-1, D)

        qkv = jnp.stack([query_weight, key_weight, value_weight], axis=1).reshape(R, 3, tp, cols)
        qkv = qkv.transpose(2, 0, 1, 3).reshape(S, 1, 2, R, 3 * cols)
        qkv = jnp.broadcast_to(qkv, (S, Z, 2, R, 3 * cols)).reshape(n, R, 3 * cols)
        wqkv = everyone(qkv).reshape(D, 3 * cols)
        rows_of = lax.all_gather(jnp.concatenate([output_weight, down_weight], axis=0), "z", axis=0)
        wdown = rows_of[:, R:].reshape(Z * RF, D)
        wo = rows_of[:, :R]
        keep_part = lax.dynamic_slice_in_dim(wo, c * half, half, axis=0)
        got_part = swap_core(lax.dynamic_slice_in_dim(wo, (1 - c) * half, half, axis=0))
        wo = jnp.where(
            c == 0,
            jnp.stack([keep_part, got_part], axis=1),
            jnp.stack([got_part, keep_part], axis=1),
        ).reshape(cols, D)
        up = up_weight.reshape(R, S, Z, 2, RF).transpose(1, 3, 0, 2, 4).reshape(tp, R, Z * RF)
        wup = lax.all_gather(in_plane(up).reshape(tp * R, Z * RF), "z", axis=0, tiled=True)

        small = jnp.concatenate(
            [first_gain, first_shift, query_bias, value_bias, output_bias, second_gain, second_shift, down_bias, up_bias]
        )
        small = everyone(jnp.broadcast_to(small[None], (n, small.shape[0]))).astype(F32)
        g1, b1, qb, vb, ob, g2, b2, db = [small[:, i * R : (i + 1) * R].reshape(-1) for i in range(8)]
        ub = small[:, 8 * R :].reshape(S, Z, 2, RF)

        codes = jnp.stack([segment_ids[0], pad_mask[0]])
        codes = jnp.stack([codes] + [xor_seq(codes, q) for q in range(1, S)], axis=1)
        codes = [codes.reshape(2, L), swap_core(codes).reshape(2, L)]
        position = ((s ^ jnp.arange(S, dtype=jnp.int32))[:, None] * t + jnp.arange(t, dtype=jnp.int32)[None]).reshape(L)
        q_info = [jnp.stack([position, code[0]], axis=1) for code in codes]
        k_info = [jnp.stack([position, jnp.where(code[1] == 1, code[0], -1)]) for code in codes]
        keep = pad_mask[0].astype(F32)[:, None]

        xf = tokens[0].astype(F32)
        dy = cotangent[0]
        dyf = dy.astype(F32)
        xhat1, inv1 = normalize(xf)
        normed = plane_gather((xhat1 * g1 + b1).astype(BF))
        dy_all = plane_gather(dy)
        qkv_bias = jnp.stack([qb.reshape(tp, cols), jnp.zeros((tp, cols), F32), vb.reshape(tp, cols)], axis=1)
        qkv_bias = lax.dynamic_index_in_dim(qkv_bias, s * 2 + c, 0, keepdims=False).reshape(3 * cols)
        both = range(2)
        qkv_out = [(dot("td,de->te", normed[e], wqkv) + qkv_bias).astype(BF) for e in both]
        heads = [
            attend_call(attend_kernel, heads_own, cols, 2, q_info[e], k_info[e], qkv_out[e]) for e in both
        ]
        branch = plane_scatter(lambda e: dot("td,de->te", heads[e], wo))
        middle = xf + (branch + ob) * keep
        xhat2, inv2 = normalize(middle)
        second = plane_gather(to_weight_order((xhat2 * g2 + b2).astype(BF)))
        up_row = lax.dynamic_index_in_dim(lax.dynamic_index_in_dim(ub, s, 0, False), c, 1, False).reshape(Z * RF)
        active, dhidden = [], []
        for e in both:
            hidden = dot("td,df->tf", second[e], wup) + up_row
            phi = 0.5 * (1.0 + lax.erf(hidden * math.sqrt(0.5)))
            slope = phi + hidden * jnp.exp(-0.5 * hidden * hidden) * (1.0 / math.sqrt(2 * math.pi))
            active.append((hidden * phi).astype(BF))
            dhidden.append((dot("td,fd->tf", dy_all[e], wdown) * slope).astype(BF))

        dsecond = from_weight_order(plane_scatter(lambda e: dot("tf,df->td", dhidden[e], wup)))
        join = functools.partial(jnp.concatenate, axis=0)
        dy_join, active_join, second_join, dhidden_join = join(dy_all), join(active), join(second), join(dhidden)
        down_grad = dot("tf,td->fd", active_join, dy_join).astype(BF)
        down_weight_grad = lax.psum_scatter(down_grad, "z", scatter_dimension=0, tiled=True).astype(F32)
        up_grad = dot("td,tf->df", second_join, dhidden_join).astype(BF)
        up_grad = lax.psum_scatter(up_grad, "z", scatter_dimension=0, tiled=True)
        up_grad = in_plane(up_grad.reshape(tp, R, Z * RF))
        up_weight_grad = up_grad.reshape(S, 2, R, Z, RF).transpose(2, 0, 3, 1, 4).reshape(R, -1).astype(F32)
        result = plane_scatter(lambda e: dot("tf,fd->td", active[e], wdown))
        block_output = (middle + result + db).astype(BF)
        dmiddle = dyf + norm_back(xhat2, inv2, g2 * dsecond)
        dbranch = (dmiddle * keep).astype(BF)
        dbranch_all = plane_gather(dbranch)
        dheads = [dot("te,de->td", dbranch_all[e], wo).astype(BF) for e in both]
        wo_grad = dot("td,te->de", join(heads), join(dbranch_all)).astype(BF).reshape(half, 2, R, D)
        keep_part = lax.dynamic_index_in_dim(wo_grad, c, 1, False)
        got_part = swap_core(lax.dynamic_index_in_dim(wo_grad, 1 - c, 1, False))
        wo_grad = jnp.where(c == 0, join([keep_part, got_part]), join([got_part, keep_part]))
        output_weight_grad = lax.psum_scatter(wo_grad, "z", scatter_dimension=0, tiled=True)[0].astype(F32)
        dqkv = [
            attend_call(attend_back_kernel, heads_own, 3 * cols, 5, q_info[e], k_info[e], qkv_out[e], dheads[e]) for e in both
        ]
        dqkv_join = join(dqkv)
        qkv_grad = dot("td,te->de", join(normed), dqkv_join).astype(BF).reshape(n, R, 3 * cols)
        qkv_grad = everyone(qkv_grad).reshape(S, Z, 2, R, 3, cols)
        qkv_grad = jnp.sum(qkv_grad.astype(F32), axis=1).transpose(3, 2, 0, 1, 4).reshape(3, R, D)
        dnormed = plane_scatter(lambda e: dot("te,de->td", dqkv[e], wqkv))
        input_grad = dmiddle + norm_back(xhat1, inv1, g1 * dnormed)

        bias = jnp.sum(dqkv_join.astype(F32), axis=0).reshape(3, cols)
        spread = jnp.zeros((2, tp, cols), F32)
        spread = lax.dynamic_update_slice(spread, jnp.stack([bias[0], bias[2]])[:, None], (0, s * 2 + c, 0))
        wide = jnp.zeros((S, Z, 2, RF), F32)
        wide = lax.dynamic_update_slice(
            wide, jnp.sum(dhidden_join.astype(F32), axis=0).reshape(1, Z, 1, RF), (s, 0, c, 0)
        )

        def share(vectors):
            packed = jnp.concatenate([v.reshape(n, -1) for v in vectors], axis=1)
            packed = jnp.sum(everyone(packed), axis=0)
            out, at = [], 0
            for v in vectors:
                out.append(packed[at : at + v.size // n])
                at += v.size // n
            return out

        ob_grad, g2_grad, b2_grad, db_grad, ub_grad, qb_grad, vb_grad = share(
            [
                jnp.sum(dbranch.astype(F32), axis=0),
                jnp.sum(dsecond * xhat2, axis=0),
                jnp.sum(dsecond, axis=0),
                jnp.sum(dyf, axis=0),
                wide,
                spread[0],
                spread[1],
            ]
        )
        g1_grad, b1_grad = share([jnp.sum(dnormed * xhat1, axis=0), jnp.sum(dnormed, axis=0)])
        return (
            block_output[None], input_grad[None], g1_grad, b1_grad,
            qkv_grad[0], qkv_grad[1], qkv_grad[2], qb_grad, vb_grad,
            output_weight_grad, ob_grad, g2_grad, b2_grad,
            up_weight_grad, ub_grad, down_weight_grad, db_grad,
        )

    return body


def solution(mesh):
    S, DP = mesh.shape["seq"], mesh.shape["dp"]
    Z = DP // 2
    parts = Mesh(mesh.devices.reshape(S, Z, 2), ("seq", "z", "core"))
    every = ("seq", "z", "core")
    token = P(("z", "core"), "seq", None)
    code = P(("z", "core"), "seq")
    vector = P(every)
    matrix = P(every, None)
    return jax.shard_map(
        make_body(S, Z),
        mesh=parts,
        in_specs=(
            token, code, code, token,
            vector, vector, matrix, matrix, matrix, vector, vector,
            matrix, vector, vector, vector, matrix, vector, matrix, vector,
        ),
        out_specs=(
            token, token, vector, vector, matrix, matrix, matrix, vector, vector,
            matrix, vector, vector, vector, matrix, vector, matrix, vector,
        ),
        check_vma=False,
    )
```

time: 941 us -> 693 us (0.74)
  starting transfers between devices: 177 us -> 72.4 us
  other arithmetic: 112 us -> 50.6 us
  local copies, waits for them, and re-layouts: 153 us -> 98.8 us
  waiting for transfers between devices: 368 us -> 329 us
  Pallas kernels: 0 us -> 16.7 us
    ppermute x51 -> x0, waiting for transfers between devices: 175 us -> none  [the longest x12 112 us: line_gather(): lax.ppermute(down[-1], 'z', [(i, i - 1) for i in range(1, Z - k + 1)])]
    unnamed x2 -> x5, waiting for transfers between devices: 111 us -> 0.08 us
    ppermute x51 -> x0, starting transfers between devices: 110 us -> none  [the longest x12 49.8 us: line_scatter(): up = lax.ppermute(a, 'z', [(i, i + 1) for i in range(k)])]
    ppermute x38 -> x27, waiting for transfers between devices: 77.5 us -> 167 us  [xor_seq(): return lax.ppermute(v, 'seq', [(i, i ^ q) for i in range(S)])]
    all_gather x0 -> x2, waiting for transfers between devices: none -> 88.7 us  [the longest x1 88.7 us: body(): lax.all_gather(jnp.concatenate([output_weight, down_weight], axis=0), 'z'...]
    all_to_all x4 -> x7, waiting for transfers between devices: 4.25 us -> 71.7 us  [the longest x5 67 us: everyone(): lax.all_to_all(v, ('seq', 'z', 'core'), split_axis=0, concat_axis=0, tile...]
    unnamed x200 -> x125, local copies, waits for them, and re-layouts: 47.8 us -> 22.1 us
    add x15 -> x2, other arithmetic: 22.1 us -> 1.34 us  [the longest x1 1.26 us: plane_scatter(): mine = mine + xor_seq(blocks[q].astype(BF), q).astype(F32)]
  transfers between devices with their start and end apart: 106 -> 50, of which waited for: 38 -> 27; matrix products, arithmetic and copies ran while one was open for 30% -> 31% of each run, Pallas kernels for 0% -> 2%
where the time goes in v2:
time: 693 us; the launch traced here: 684 us
  waiting for transfers between devices  329 us (47%)
  matrix products  102 us (15%)
  local copies, waits for them, and re-layouts  98.8 us (14%)
  starting transfers between devices  72.4 us (10%)
  other arithmetic  50.6 us (7%)
  Pallas kernels  16.7 us (2%)
  between operations  14.9 us (2%)
    ppermute x27, waiting for transfers between devices, xor_seq(): return lax.ppermute(v, 'seq', [(i, i ^ q) for i in range(S)])  167 us
    dot_general x20, matrix products, dot(): return jnp.einsum(form, left, right, preferred_element_type=F32)  102 us
    all_gather x1, waiting for transfers between devices, body(): lax.all_gather(jnp.concatenate([output_weight, down_weight], axis=0), 'z'...  88.7 us
    all_to_all x5, waiting for transfers between devices, everyone(): lax.all_to_all(v, ('seq', 'z', 'core'), split_axis=0, concat_axis=0, tile...  67 us
    ppermute x27, starting transfers between devices, xor_seq(): return lax.ppermute(v, 'seq', [(i, i ^ q) for i in range(S)])  31.6 us
    unnamed x125, local copies, waits for them, and re-layouts  22.1 us
    all_to_all x5, starting transfers between devices, everyone(): lax.all_to_all(v, ('seq', 'z', 'core'), split_axis=0, concat_axis=0, tile...  19.8 us
    pallas_call x4, Pallas kernels, attend_call(): pl.pallas_call(functools.partial(kernel, heads), out_shape=jax.ShapeDtype...  16.7 us
  transfers between devices with their start and end apart: 50, of which 27 were waited for; matrix products, arithmetic and copies ran while one was open for 31% of the time, Pallas kernels for 2%

profile of v2, /device:TPU:0, one launch (start us, length us, event | category | flops | bytes accessed | tf_op | source)
XLA Modules:
  0.0 684.1 jit_solution(9549732943924163341)
XLA Ops:
  12.3 7.3 %all-to-all-start = ((bf16[32,2,384]{2,1,0:T(2,128)(2,1)}), bf16[32,2,384]{2,1,0:T(2,128)(2,1)S(1)}, u32[]{:S(2)}, u32[]{:S(2)}) async-start(bf16[32,2,384]{2,1,0:T(2,128)(2,1)} %reshape.389), calls=%async_computation | async-start | bytes 98304 | tf_op jit(solution)/shard_map/all_to_all | solution.py:116
  38.1 26.7 %collective-permute-done.5 = bf16[128,2048]{1,0:T(8,128)(2,1)S(1)} collective-permute-done((bf16[128,2048]{1,0:T(8,128)(2,1)S(1)}, bf16[128,2048]{1,0:T(8,128)(2,1)S(1)}, u32[]{:S(2)}, u32[]{:S(2)}) %collective-permute-start.5) | collective-permute-done | bytes 524320 | tf_op jit(solution)/shard_map/ppermute | solution.py:97
  64.7 11.1 %collective-permute-done.4 = bf16[128,2048]{1,0:T(8,128)(2,1)S(1)} collective-permute-done((bf16[128,2048]{1,0:T(8,128)(2,1)S(1)}, bf16[128,2048]{1,0:T(8,128)(2,1)S(1)}, u32[]{:S(2)}, u32[]{:S(2)}) %collective-permute-start.4) | collective-permute-done | bytes 524320 | tf_op jit(solution)/shard_map/ppermute | solution.py:97
  89.3 88.7 %all-gather.6.cloned.1.call-done = bf16[1280,2048]{1,0:T(8,128)(2,1)} async-done(((bf16[320,2048]{1,0:T(8,128)(2,1)}), bf16[1280,2048]{1,0:T(8,128)(2,1)}) %all-gather.6.cloned.1.call-update) | async-done | bytes 5242896 | tf_op jit(solution)/shard_map/all_gather | solution.py:146
  183.3 11.3 %all-gather.4.cloned.1.call-start = ((), (), s32[]{:S(2)}) async-start(), calls=%async_computation.10 | async-start | bytes 5242880 | tf_op jit(solution)/shard_map/all_gather | solution.py:157
  194.6 5.2 add_convert_fusion.qkv_ref
  210.8 5.0 add_convert_fusion.1.qkv_ref
  228.7 11.3 %collective-permute-done.10 = bf16[128,2048]{1,0:T(8,128)(2,1)S(1)} collective-permute-done((bf16[128,2048]{1,0:T(8,128)(2,1)}, bf16[128,2048]{1,0:T(8,128)(2,1)S(1)}, u32[]{:S(2)}, u32[]{:S(2)}) %collective-permute-start.10) | collective-permute-done | bytes 524320 | tf_op jit(solution)/shard_map/ppermute | solution.py:97
  240.0 11.8 %collective-permute-done.12 = bf16[128,2048]{1,0:T(8,128)(2,1)S(1)} collective-permute-done((bf16[128,2048]{1,0:T(8,128)(2,1)}, bf16[128,2048]{1,0:T(8,128)(2,1)S(1)}, u32[]{:S(2)}, u32[]{:S(2)}) %collective-permute-start.12) | collective-permute-done | bytes 524320 | tf_op jit(solution)/shard_map/ppermute | solution.py:97
  268.2 9.7 %collective-permute-done.15 = bf16[128,2048]{0,1:T(8,128)(2,1)} collective-permute-done((bf16[128,2048]{0,1:T(8,128)(2,1)}, bf16[128,2048]{0,1:T(8,128)(2,1)}, u32[]{:S(2)}, u32[]{:S(2)}) %collective-permute-start.15) | collective-permute-done | bytes 524320 | tf_op jit(solution)/shard_map/ppermute | solution.py:97
  279.5 9.7 %collective-permute-done.14 = bf16[128,2048]{0,1:T(8,128)(2,1)} collective-permute-done((bf16[128,2048]{0,1:T(8,128)(2,1)}, bf16[128,2048]{0,1:T(8,128)(2,1)}, u32[]{:S(2)}, u32[]{:S(2)}) %collective-permute-start.14) | collective-permute-done | bytes 524320 | tf_op jit(solution)/shard_map/ppermute | solution.py:97
  292.2 8.1 %collective-permute-done.23 = bf16[128,2048]{1,0:T(8,128)(2,1)} collective-permute-done((bf16[128,2048]{1,0:T(8,128)(2,1)S(1)}, bf16[128,2048]{1,0:T(8,128)(2,1)}, u32[]{:S(2)}, u32[]{:S(2)}) %collective-permute-start.23) | collective-permute-done | bytes 524320 | tf_op jit(solution)/shard_map/ppermute | solution.py:97
  300.4 9.2 %collective-permute-done.22 = bf16[128,2048]{1,0:T(8,128)(2,1)} collective-permute-done((bf16[128,2048]{1,0:T(8,128)(2,1)S(1)}, bf16[128,2048]{1,0:T(8,128)(2,1)}, u32[]{:S(2)}, u32[]{:S(2)}) %collective-permute-start.22) | collective-permute-done | bytes 524320 | tf_op jit(solution)/shard_map/ppermute | solution.py:97
  318.1 5.3 fusion.60
  329.1 6.3 multiply_convert_fusion
  352.7 6.4 convolution_convert_fusion.1
  359.3 5.7 fusion.64
  368.8 6.0 fusion.65
  380.6 10.7 %collective-permute-done.28 = bf16[128,2048]{1,0:T(8,128)(2,1)S(1)} collective-permute-done((bf16[128,2048]{1,0:T(8,128)(2,1)S(1)}, bf16[128,2048]{1,0:T(8,128)(2,1)S(1)}, u32[]{:S(2)}, u32[]{:S(2)}) %collective-permute-start.28) | collective-permute-done | bytes 524320 | tf_op jit(solution)/shard_map/ppermute | solution.py:97
  405.0 8.5 %collective-permute-done.20 = bf16[128,2048]{1,0:T(8,128)(2,1)} collective-permute-done((bf16[128,2048]{1,0:T(8,128)(2,1)}, bf16[128,2048]{1,0:T(8,128)(2,1)}, u32[]{:S(2)}, u32[]{:S(2)}) %collective-permute-start.20) | collective-permute-done | bytes 524320 | tf_op jit(solution)/shard_map/ppermute | solution.py:97
  423.6 12.3 %collective-permute-done.31 = bf16[128,2048]{1,0:T(8,128)(2,1)S(1)} collective-permute-done((bf16[128,2048]{1,0:T(8,128)(2,1)S(1)}, bf16[128,2048]{1,0:T(8,128)(2,1)S(1)}, u32[]{:S(2)}, u32[]{:S(2)}) %collective-permute-start.31) | collective-permute-done | bytes 524320 | tf_op jit(solution)/shard_map/ppermute | solution.py:97
  435.9 9.2 %collective-permute-done.30 = bf16[128,2048]{1,0:T(8,128)(2,1)S(1)} collective-permute-done((bf16[128,2048]{1,0:T(8,128)(2,1)S(1)}, bf16[128,2048]{1,0:T(8,128)(2,1)S(1)}, u32[]{:S(2)}, u32[]{:S(2)}) %collective-permute-start.30) | collective-permute-done | bytes 524320 | tf_op jit(solution)/shard_map/ppermute | solution.py:97
  476.1 5.0 convolution_convert_fusion.6
  488.3 8.3 %convolution_convert_fusion = bf16[1024,2048]{1,0:T(8,128)(2,1)} fusion(bf16[1024,2048]{1,0:T(8,128)(2,1)} %constant_dynamic-update-slice_fusion.15, bf16[512,1024]{1,0:T(8,128)(2,1)S(1)} %copy-done.52, bf16[512,1024]{1,0:T(8,128)(2,1)S(1)} %copy-done.50), kind=kOutput, calls=%fused_computation.5 | convolution fusion | flops 4301258752 | bytes 10485760 | tf_op jit(solution)/shard_map/tf,td->fd/dot_general | solution.py:22
  506.0 7.3 %fusion.63 = (bf16[512,2048]{1,0:T(8,128)(2,1)S(1)}, f32[512,2048]{1,0:T(8,128)}) fusion(bf16[512,2048]{1,0:T(8,128)(2,1)} %collective-permute-done.33, bf16[512,768]{1,0:T(8,128)(2,1)} %shard_map.316, bf16[2048,768]{1,0:T(8,128)(2,1)} %bitcast.11), kind=kOutput, calls=%fused_computation.167 | convolution fusion | flops 1613758464 | bytes 12320768 | tf_op jit(solution)/shard_map/te,de->td/dot_general | solution.py:22
  522.6 6.1 collective-permute-done.34
  528.7 12.2 %collective-permute-done.36 = bf16[128,2048]{1,0:T(8,128)(2,1)} collective-permute-done((bf16[128,2048]{1,0:T(8,128)(2,1)S(1)}, bf16[128,2048]{1,0:T(8,128)(2,1)}, u32[]{:S(2)}, u32[]{:S(2)}) %collective-permute-start.36) | collective-permute-done | bytes 524320 | tf_op jit(solution)/shard_map/ppermute | solution.py:97
  549.1 8.0 %all-to-all-done.3 = f32[32,1,128]{2,1,0:T(1,128)S(1)} async-done(((f32[32,1,128]{2,1,0:T(1,128)}), f32[32,1,128]{2,1,0:T(1,128)S(1)}, u32[]{:S(2)}, u32[]{:S(2)}) %all-to-all-start.3) | async-done | bytes 16416 | tf_op jit(solution)/shard_map/all_to_all | solution.py:116
  564.1 7.4 %convolution_convert_fusion.2 = bf16[2048,768]{1,0:T(8,128)(2,1)} fusion(bf16[1024,2048]{1,0:T(8,128)(2,1)} %constant_dynamic-update-slice_fusion, bf16[512,768]{1,0:T(8,128)(2,1)S(1)} %copy-done.28, bf16[512,768]{1,0:T(8,128)(2,1)S(1)} %copy-done.29), kind=kOutput, calls=%fused_computation.7 | convolution fusion | flops 3225944064 | bytes 8912896 | tf_op jit(solution)/shard_map/td,te->de/dot_general | solution.py:22
  597.5 55.9 %all-to-all-done.4 = bf16[32,64,768]{2,1,0:T(8,128)(2,1)} async-done(((bf16[32,64,768]{2,1,0:T(8,128)(2,1)}), bf16[32,64,768]{2,1,0:T(8,128)(2,1)}, u32[]{:S(2)}, u32[]{:S(2)}) %all-to-all-start.4) | async-done | bytes 3145760 | tf_op jit(solution)/shard_map/all_to_all | solution.py:116
  653.4 10.0 %reshape.382 = f32[4,4,2,64,3,256]{5,4,3,2,1,0:T(4,128)} reshape(bf16[32,64,768]{2,1,0:T(8,128)(2,1)} %all-to-all-done.4) | data formatting | bytes 9437184 | tf_op jit(solution)/shard_map/convert_element_type | solution.py:226
  663.4 6.1 reduce_sum.182
  (348 shorter events, 257.2 us)
Async XLA Ops:
  7.3 170.7 %all-gather.6.cloned.1.call-start = ((), (), s32[]{:S(2)}) async-start(), calls=%async_computation.14 | async-start | bytes 6553600 | tf_op jit(solution)/shard_map/all_gather | solution.py:146
  29.0 150.5 %all-to-all-start.1 = ((bf16[32,64,768]{2,1,0:T(8,128)(2,1)}), bf16[32,64,768]{2,1,0:T(8,128)(2,1)}, u32[]{:S(2)}, u32[]{:S(2)}) async-start(bf16[32,64,768]{2,1,0:T(8,128)(2,1)} %bitcast.156), calls=%async_computation.1 | async-start | bytes 6291456 | tf_op jit(solution)/shard_map/all_to_all | solution.py:116
  34.6 30.2 %collective-permute-start.5 = (bf16[128,2048]{1,0:T(8,128)(2,1)S(1)}, bf16[128,2048]{1,0:T(8,128)(2,1)S(1)}, u32[]{:S(2)}, u32[]{:S(2)}) collective-permute-start(bf16[128,2048]{1,0:T(8,128)(2,1)S(1)} %get-tuple-element.29), channel_id=1, source_target_pairs={{0,24},{8,16},{16,8},{24,0},{1,25},{9,17},{17,9},{25,1},{2,26},{10... | collective-permute-start | bytes 1572872 | tf_op jit(solution)/shard_map/ppermute | solution.py:97
  37.1 38.7 %collective-permute-start.4 = (bf16[128,2048]{1,0:T(8,128)(2,1)S(1)}, bf16[128,2048]{1,0:T(8,128)(2,1)S(1)}, u32[]{:S(2)}, u32[]{:S(2)}) collective-permute-start(bf16[128,2048]{1,0:T(8,128)(2,1)S(1)} %get-tuple-element.29), channel_id=1, source_target_pairs={{0,16},{8,24},{16,0},{24,8},{1,17},{9,25},{17,1},{25,9},{2,18},{10... | collective-permute-start | bytes 1572872 | tf_op jit(solution)/shard_map/ppermute | solution.py:97
  37.6 40.6 %collective-permute-start.3 = (bf16[128,2048]{1,0:T(8,128)(2,1)S(1)}, bf16[128,2048]{1,0:T(8,128)(2,1)S(1)}, u32[]{:S(2)}, u32[]{:S(2)}) collective-permute-start(bf16[128,2048]{1,0:T(8,128)(2,1)S(1)} %get-tuple-element.29), channel_id=1, source_target_pairs={{0,8},{8,0},{16,24},{24,16},{1,9},{9,1},{17,25},{25,17},{2,10},{10... | collective-permute-start | bytes 1572872 | tf_op jit(solution)/shard_map/ppermute | solution.py:97
  79.8 114.8 %collective-permute-start.8 = (bf16[512,2048]{1,0:T(8,128)(2,1)}, bf16[512,2048]{1,0:T(8,128)(2,1)}, u32[]{:S(2)}, u32[]{:S(2)}) collective-permute-start(bf16[512,2048]{1,0:T(8,128)(2,1)} %pad_maximum_fusion), channel_id=1, source_target_pairs={{0,1},{1,0},{2,3},{3,2},{4,5},{5,4},{6,7},{7,6},{8,9},{9,8},{10,11... | collective-permute-start | bytes 6291464 | tf_op jit(solution)/shard_map/ppermute | solution.py:100
  179.5 23.9 %collective-permute-start.6 = (bf16[2,64,2048]{2,1,0:T(8,128)(2,1)S(1)}, bf16[2,64,2048]{2,1,0:T(8,128)(2,1)S(1)}, u32[]{:S(2)}, u32[]{:S(2)}) collective-permute-start(bf16[2,64,2048]{2,1,0:T(8,128)(2,1)S(1)} %get-tuple-element.60), channel_id=1, source_target_pairs={{0,1},{1,0},{2,3},{3,2},{4,5},{5,4},{6,7},{7,6},{8,9},{9,8},{10,11... | collective-permute-start | bytes 1572872 | tf_op jit(solution)/shard_map/ppermute | solution.py:100
  179.6 29.3 %all-to-all-start.2 = ((bf16[8,64,1024]{2,1,0:T(8,128)(2,1)}), bf16[8,64,1024]{2,1,0:T(8,128)(2,1)S(1)}, u32[]{:S(2)}, u32[]{:S(2)}) async-start(bf16[8,64,1024]{2,1,0:T(8,128)(2,1)} %reshape.364), calls=%async_computation.2 | async-start | bytes 2097152 | tf_op jit(solution)/shard_map/all_to_all | solution.py:119
  183.3 134.8 %all-gather.4.cloned.1.call-start = ((), (), s32[]{:S(2)}) async-start(), calls=%async_computation.10 | async-start | bytes 5242880 | tf_op jit(solution)/shard_map/all_gather | solution.py:157
  209.9 347.2 %reduce-scatter.6.cloned.1.call-start = ((), (), s32[]{:S(2)}) async-start(), calls=%async_computation.12 | async-start | bytes 5242880 | tf_op jit(solution)/shard_map/reduce_scatter | solution.py:206
  226.6 25.2 %collective-permute-start.12 = (bf16[128,2048]{1,0:T(8,128)(2,1)}, bf16[128,2048]{1,0:T(8,128)(2,1)S(1)}, u32[]{:S(2)}, u32[]{:S(2)}) collective-permute-start(bf16[128,2048]{1,0:T(8,128)(2,1)} %get-tuple-element.54), channel_id=1, source_target_pairs={{0,24},{8,16},{16,8},{24,0},{1,25},{9,17},{17,9},{25,1},{2,26},{10... | collective-permute-start | bytes 1572872 | tf_op jit(solution)/shard_map/ppermute | solution.py:97
  228.1 25.1 %collective-permute-start.11 = (bf16[128,2048]{1,0:T(8,128)(2,1)}, bf16[128,2048]{1,0:T(8,128)(2,1)S(1)}, u32[]{:S(2)}, u32[]{:S(2)}) collective-permute-start(bf16[128,2048]{1,0:T(8,128)(2,1)} %get-tuple-element.55), channel_id=1, source_target_pairs={{0,16},{8,24},{16,0},{24,8},{1,17},{9,25},{17,1},{25,9},{2,18},{10... | collective-permute-start | bytes 1572872 | tf_op jit(solution)/shard_map/ppermute | solution.py:97
  263.2 25.9 %collective-permute-start.14 = (bf16[128,2048]{0,1:T(8,128)(2,1)}, bf16[128,2048]{0,1:T(8,128)(2,1)}, u32[]{:S(2)}, u32[]{:S(2)}) collective-permute-start(bf16[128,2048]{0,1:T(8,128)(2,1)} %bitcast.171), channel_id=1, source_target_pairs={{0,16},{8,24},{16,0},{24,8},{1,17},{9,25},{17,1},{25,9},{2,18},{10... | collective-permute-start | bytes 1572872 | tf_op jit(solution)/shard_map/ppermute | solution.py:97
  264.7 24.5 %collective-permute-start.13 = (bf16[128,2048]{0,1:T(8,128)(2,1)}, bf16[128,2048]{0,1:T(8,128)(2,1)}, u32[]{:S(2)}, u32[]{:S(2)}) collective-permute-start(bf16[128,2048]{0,1:T(8,128)(2,1)} %bitcast.172), channel_id=1, source_target_pairs={{0,8},{8,0},{16,24},{24,16},{1,9},{9,1},{17,25},{25,17},{2,10},{10... | collective-permute-start | bytes 1572872 | tf_op jit(solution)/shard_map/ppermute | solution.py:97
  265.2 35.1 %collective-permute-start.23 = (bf16[128,2048]{1,0:T(8,128)(2,1)S(1)}, bf16[128,2048]{1,0:T(8,128)(2,1)}, u32[]{:S(2)}, u32[]{:S(2)}) collective-permute-start(bf16[128,2048]{1,0:T(8,128)(2,1)S(1)} %bitcast.165), channel_id=1, source_target_pairs={{0,24},{8,16},{16,8},{24,0},{1,25},{9,17},{17,9},{25,1},{2,26},{10... | collective-permute-start | bytes 1572872 | tf_op jit(solution)/shard_map/ppermute | solution.py:97
  266.7 42.8 %collective-permute-start.22 = (bf16[128,2048]{1,0:T(8,128)(2,1)S(1)}, bf16[128,2048]{1,0:T(8,128)(2,1)}, u32[]{:S(2)}, u32[]{:S(2)}) collective-permute-start(bf16[128,2048]{1,0:T(8,128)(2,1)S(1)} %bitcast.166), channel_id=1, source_target_pairs={{0,16},{8,24},{16,0},{24,8},{1,17},{9,25},{17,1},{25,9},{2,18},{10... | collective-permute-start | bytes 1572872 | tf_op jit(solution)/shard_map/ppermute | solution.py:97
  277.8 31.7 %collective-permute-start.21 = (bf16[128,2048]{1,0:T(8,128)(2,1)S(1)}, bf16[128,2048]{1,0:T(8,128)(2,1)}, u32[]{:S(2)}, u32[]{:S(2)}) collective-permute-start(bf16[128,2048]{1,0:T(8,128)(2,1)S(1)} %bitcast.167), channel_id=1, source_target_pairs={{0,8},{8,0},{16,24},{24,16},{1,9},{9,1},{17,25},{25,17},{2,10},{10... | collective-permute-start | bytes 1572872 | tf_op jit(solution)/shard_map/ppermute | solution.py:97
  292.2 36.9 %collective-permute-start.16 = (bf16[512,2048]{0,1:T(8,128)(2,1)}, bf16[512,2048]{0,1:T(8,128)(2,1)}, u32[]{:S(2)}, u32[]{:S(2)}) collective-permute-start(bf16[512,2048]{0,1:T(8,128)(2,1)} %pad_maximum_fusion.1), channel_id=1, source_target_pairs={{0,1},{1,0},{2,3},{3,2},{4,5},{5,4},{6,7},{7,6},{8,9},{9,8},{10,11... | collective-permute-start | bytes 6291464 | tf_op jit(solution)/shard_map/ppermute | solution.py:100
  312.4 23.0 %collective-permute-start.24 = (bf16[512,2048]{1,0:T(8,128)(2,1)}, bf16[512,2048]{1,0:T(8,128)(2,1)}, u32[]{:S(2)}, u32[]{:S(2)}) collective-permute-start(bf16[512,2048]{1,0:T(8,128)(2,1)} %pad_maximum_fusion.2), channel_id=1, source_target_pairs={{0,1},{1,0},{2,3},{3,2},{4,5},{5,4},{6,7},{7,6},{8,9},{9,8},{10,11... | collective-permute-start | bytes 6291464 | tf_op jit(solution)/shard_map/ppermute | solution.py:100
  359.1 223.0 %reduce-scatter.4.cloned.1.call-start = ((), (), s32[]{:S(2)}) async-start(), calls=%async_computation.11 | async-start | bytes 1310720 | tf_op jit(solution)/shard_map/reduce_scatter | solution.py:219
  365.9 25.4 %collective-permute-start.28 = (bf16[128,2048]{1,0:T(8,128)(2,1)S(1)}, bf16[128,2048]{1,0:T(8,128)(2,1)S(1)}, u32[]{:S(2)}, u32[]{:S(2)}) collective-permute-start(bf16[128,2048]{1,0:T(8,128)(2,1)S(1)} %get-tuple-element.48), channel_id=1, source_target_pairs={{0,24},{8,16},{16,8},{24,0},{1,25},{9,17},{17,9},{25,1},{2,26},{10... | collective-permute-start | bytes 1572872 | tf_op jit(solution)/shard_map/ppermute | solution.py:97
  367.3 26.0 %collective-permute-start.27 = (bf16[128,2048]{1,0:T(8,128)(2,1)S(1)}, bf16[128,2048]{1,0:T(8,128)(2,1)S(1)}, u32[]{:S(2)}, u32[]{:S(2)}) collective-permute-start(bf16[128,2048]{1,0:T(8,128)(2,1)S(1)} %get-tuple-element.49), channel_id=1, source_target_pairs={{0,16},{8,24},{16,0},{24,8},{1,17},{9,25},{17,1},{25,9},{2,18},{10... | collective-permute-start | bytes 1572872 | tf_op jit(solution)/shard_map/ppermute | solution.py:97
  376.0 29.0 %collective-permute-start.18 = (bf16[128,2048]{1,0:T(8,128)(2,1)}, bf16[128,2048]{1,0:T(8,128)(2,1)}, u32[]{:S(2)}, u32[]{:S(2)}) collective-permute-start(bf16[128,2048]{1,0:T(8,128)(2,1)} %get-tuple-element.50), channel_id=1, source_target_pairs={{0,8},{8,0},{16,24},{24,16},{1,9},{9,1},{17,25},{25,17},{2,10},{10... | collective-permute-start | bytes 1572872 | tf_op jit(solution)/shard_map/ppermute | solution.py:97
  376.6 36.9 %collective-permute-start.20 = (bf16[128,2048]{1,0:T(8,128)(2,1)}, bf16[128,2048]{1,0:T(8,128)(2,1)}, u32[]{:S(2)}, u32[]{:S(2)}) collective-permute-start(bf16[128,2048]{1,0:T(8,128)(2,1)} %get-tuple-element.51), channel_id=1, source_target_pairs={{0,24},{8,16},{16,8},{24,0},{1,25},{9,17},{17,9},{25,1},{2,26},{10... | collective-permute-start | bytes 1572872 | tf_op jit(solution)/shard_map/ppermute | solution.py:97
  380.0 34.9 %collective-permute-start.19 = (bf16[128,2048]{1,0:T(8,128)(2,1)}, bf16[128,2048]{1,0:T(8,128)(2,1)}, u32[]{:S(2)}, u32[]{:S(2)}) collective-permute-start(bf16[128,2048]{1,0:T(8,128)(2,1)} %get-tuple-element.52), channel_id=1, source_target_pairs={{0,16},{8,24},{16,0},{24,8},{1,17},{9,25},{17,1},{25,9},{2,18},{10... | collective-permute-start | bytes 1572872 | tf_op jit(solution)/shard_map/ppermute | solution.py:97
  421.6 23.5 %collective-permute-start.30 = (bf16[128,2048]{1,0:T(8,128)(2,1)S(1)}, bf16[128,2048]{1,0:T(8,128)(2,1)S(1)}, u32[]{:S(2)}, u32[]{:S(2)}) collective-permute-start(bf16[128,2048]{1,0:T(8,128)(2,1)S(1)} %get-tuple-element.26), channel_id=1, source_target_pairs={{0,16},{8,24},{16,0},{24,8},{1,17},{9,25},{17,1},{25,9},{2,18},{10... | collective-permute-start | bytes 1572872 | tf_op jit(solution)/shard_map/ppermute | solution.py:97
  475.7 119.1 %reduce-scatter.8.cloned.1.call-start = ((), (), s32[]{:S(2)}) async-start(), calls=%async_computation.13 | async-start | bytes 5242880 | tf_op jit(solution)/shard_map/reduce_scatter | solution.py:204
  481.2 24.8 %collective-permute-start.33 = (bf16[512,2048]{1,0:T(8,128)(2,1)}, bf16[512,2048]{1,0:T(8,128)(2,1)}, u32[]{:S(2)}, u32[]{:S(2)}) collective-permute-start(bf16[512,2048]{1,0:T(8,128)(2,1)} %convolution_convert_fusion.6), channel_id=1, source_target_pairs={{0,1},{1,0},{2,3},{3,2},{4,5},{5,4},{6,7},{7,6},{8,9},{9,8},{10,11... | collective-permute-start | bytes 6291464 | tf_op jit(solution)/shard_map/ppermute | solution.py:100
  515.0 25.9 %collective-permute-start.36 = (bf16[128,2048]{1,0:T(8,128)(2,1)S(1)}, bf16[128,2048]{1,0:T(8,128)(2,1)}, u32[]{:S(2)}, u32[]{:S(2)}) collective-permute-start(bf16[128,2048]{1,0:T(8,128)(2,1)S(1)} %get-tuple-element.45), channel_id=1, source_target_pairs={{0,24},{8,16},{16,8},{24,0},{1,25},{9,17},{17,9},{25,1},{2,26},{10... | collective-permute-start | bytes 1572872 | tf_op jit(solution)/shard_map/ppermute | solution.py:97
  516.5 25.9 %collective-permute-start.35 = (bf16[128,2048]{1,0:T(8,128)(2,1)S(1)}, bf16[128,2048]{1,0:T(8,128)(2,1)}, u32[]{:S(2)}, u32[]{:S(2)}) collective-permute-start(bf16[128,2048]{1,0:T(8,128)(2,1)S(1)} %get-tuple-element.46), channel_id=1, source_target_pairs={{0,16},{8,24},{16,0},{24,8},{1,17},{9,25},{17,1},{25,9},{2,18},{10... | collective-permute-start | bytes 1572872 | tf_op jit(solution)/shard_map/ppermute | solution.py:97
  520.0 25.6 %all-to-all-start.5 = ((f32[32,1,640]{2,1,0:T(1,128)}), f32[32,1,640]{2,1,0:T(1,128)S(1)}, u32[]{:S(2)}, u32[]{:S(2)}) async-start(f32[32,1,640]{2,1,0:T(1,128)} %all_to_all.34), calls=%async_computation.5 | async-start | bytes 163840 | tf_op jit(solution)/shard_map/all_to_all | solution.py:116
  577.1 76.3 %all-to-all-start.4 = ((bf16[32,64,768]{2,1,0:T(8,128)(2,1)}), bf16[32,64,768]{2,1,0:T(8,128)(2,1)}, u32[]{:S(2)}, u32[]{:S(2)}) async-start(bf16[32,64,768]{2,1,0:T(8,128)(2,1)} %bitcast.183), calls=%async_computation.4 | async-start | bytes 6291456 | tf_op jit(solution)/shard_map/all_to_all | solution.py:116
  (71 other events, 774.8 us)
Sparse Core Ops, SparseCore 0:
  10.3 167.7 all-gather.5
  210.0 79.1 all-gather.3
  359.2 74.2 reduce-scatter.5
  475.8 24.4 reduce-scatter.3
  502.5 77.0 reduce-scatter.7

commit v3 on v2

v3 whole, which is shorter than its diff:
```python
import functools
import math

import jax
import jax.numpy as jnp
from jax import lax
from jax.experimental import pallas as pl
from jax.experimental.pallas import tpu as pltpu
from jax.sharding import Mesh
from jax.sharding import PartitionSpec as P

H = 16
DH = 128
EPSILON = 1e-05
NEGATIVE = -1e30
BF = jnp.bfloat16
F32 = jnp.float32
SCALE = 1.0 / math.sqrt(DH)


def dot(form, left, right):
    return jnp.einsum(form, left, right, preferred_element_type=F32)


def normalize(v):
    center = v - jnp.mean(v, axis=-1, keepdims=True)
    inv = lax.rsqrt(jnp.mean(center * center, axis=-1, keepdims=True) + EPSILON)
    return center * inv, inv


def norm_back(xhat, inv, e):
    return (
        e - jnp.mean(e, axis=-1, keepdims=True) - xhat * jnp.mean(e * xhat, axis=-1, keepdims=True)
    ) * inv


def nt(a, b):
    return lax.dot_general(a, b, (((1,), (1,)), ((), ())), preferred_element_type=F32)


def nn(a, b):
    return lax.dot_general(a, b, (((1,), (0,)), ((), ())), preferred_element_type=F32)


def tn(a, b):
    return lax.dot_general(a, b, (((0,), (0,)), ((), ())), preferred_element_type=F32)


def seen(q_ref, k_ref):
    q_pos, q_doc = q_ref[:, 0:1], q_ref[:, 1:2]
    k_pos, k_doc = k_ref[0:1, :], k_ref[1:2, :]
    return ((k_pos <= q_pos) & (k_doc == q_doc)) | (k_pos == q_pos)


def softmax(q, k, visible):
    scores = jnp.where(visible, nt(q, k) * SCALE, NEGATIVE)
    powers = jnp.exp(scores - jnp.max(scores, axis=1, keepdims=True))
    return powers / jnp.sum(powers, axis=1, keepdims=True)


def attend_kernel(heads, q_info, k_info, qkv_ref, out_ref):
    visible = seen(q_info, k_info)
    for h in range(heads):
        q, k, v = (qkv_ref[:, (part * heads + h) * DH : (part * heads + h + 1) * DH] for part in range(3))
        probs = softmax(q, k, visible).astype(BF)
        out_ref[:, h * DH : (h + 1) * DH] = nn(probs, v).astype(BF)


def attend_back_kernel(heads, q_info, k_info, qkv_ref, grad_ref, out_ref):
    visible = seen(q_info, k_info)
    for h in range(heads):
        q, k, v = (qkv_ref[:, (part * heads + h) * DH : (part * heads + h + 1) * DH] for part in range(3))
        grad = grad_ref[:, h * DH : (h + 1) * DH]
        probs = softmax(q, k, visible)
        dp = nt(grad, v)
        delta = jnp.sum(probs * dp, axis=1, keepdims=True)
        dscores = (probs * (dp - delta) * SCALE).astype(BF)
        parts = (nn(dscores, k), tn(dscores, q), tn(probs.astype(BF), grad))
        for part, value in enumerate(parts):
            out_ref[:, (part * heads + h) * DH : (part * heads + h + 1) * DH] = value.astype(BF)


def attend_call(kernel, heads, columns, matmuls, *args):
    rows = args[2].shape[0]
    return pl.pallas_call(
        functools.partial(kernel, heads),
        out_shape=jax.ShapeDtypeStruct((rows, columns), BF),
        compiler_params=pltpu.CompilerParams(vmem_limit_bytes=56 * 1024 * 1024),
        cost_estimate=pl.CostEstimate(
            flops=2 * matmuls * heads * rows * rows * DH, bytes_accessed=8 * rows * columns, transcendentals=heads * rows * rows
        ),
    )(*args)


def finish_kernel(in_ref, q_ref, k_ref, v_ref):
    total = jnp.sum(in_ref[:, 0].astype(F32), axis=0)
    cols = q_ref.shape[1]
    q_ref[...] = total[:, :cols]
    k_ref[...] = total[:, cols : 2 * cols]
    v_ref[...] = total[:, 2 * cols :]


def finish_qkv(v):
    Z, places, R, wide = v.shape
    cols = wide // 3
    out = jax.ShapeDtypeStruct((R, places * cols), F32)
    return pl.pallas_call(
        finish_kernel,
        grid=(places,),
        in_specs=[pl.BlockSpec((Z, 1, R, wide), lambda j: (0, j, 0, 0))],
        out_specs=[pl.BlockSpec((R, cols), lambda j: (0, j))] * 3,
        out_shape=[out] * 3,
    )(v)


def after(values, *others):
    return lax.optimization_barrier((values, others))[0]


def make_body(S, Z):
    every = ("seq", "z", "core")
    join = functools.partial(jnp.concatenate, axis=0)

    def flip(v, axis, size, q):
        return lax.ppermute(v, axis, [(i, i ^ q) for i in range(size)])

    def xor_seq(v, q):
        return flip(v, "seq", S, q)

    def swap_core(v):
        return flip(v, "core", 2, 1)

    def rows(v, block, t):
        return v[block * t : (block + 1) * t]

    def plane_gather(v):
        own = join([v] + [xor_seq(v, q) for q in range(1, S)])
        return own, swap_core(own)

    def plane_scatter(own, other):
        total = own + swap_core(other).astype(F32)
        t = total.shape[0] // S
        got = [xor_seq(rows(total, q, t).astype(BF), q) for q in range(1, S)]
        return rows(total, 0, t), got

    def add_up(mine, got):
        for v in got:
            mine = mine + v.astype(F32)
        return mine

    def exchange(v, axes):
        return lax.all_to_all(v, axes, split_axis=0, concat_axis=0, tiled=True)

    def swap_blocks(v, at, axis, size, me):
        out = v
        for q in range(1, size):
            got = flip(lax.dynamic_index_in_dim(v, me ^ q, at, True), axis, size, q)
            out = lax.dynamic_update_slice_in_dim(out, got, me ^ q, at)
        return out

    def spread_scatter(v, axis, size, me):
        got = [flip(lax.dynamic_index_in_dim(v, me ^ q, 0, False), axis, size, q) for q in range(1, size)]
        return add_up(lax.dynamic_index_in_dim(v, me, 0, False).astype(F32), got)

    def body(
        tokens, segment_ids, pad_mask, cotangent,
        first_gain, first_shift, query_weight, key_weight, value_weight, query_bias, value_bias,
        output_weight, output_bias, second_gain, second_shift, up_weight, up_bias, down_weight, down_bias,
    ):
        s, z, c = (lax.axis_index(a) for a in every)
        n, tp = S * Z * 2, S * 2
        R, D = query_weight.shape
        RF = down_weight.shape[0]
        t = tokens.shape[1]
        L = S * t
        heads_own = H // tp
        cols = D // tp
        half = Z // 2
        both = range(2)

        def lane_blocks(v, order):
            return jnp.concatenate([v[:, i * 2 * R : (i + 1) * 2 * R] for i in order], axis=1)

        natural = [i_s * Z + i_z for i_z in range(Z) for i_s in range(S)]
        back = [natural.index(i) for i in range(S * Z)]

        pieces = [w.reshape(R, tp, cols).transpose(1, 0, 2) for w in (query_weight, key_weight, value_weight)]
        up = up_weight.reshape(R, S, Z, 2, RF).transpose(1, 3, 0, 2, 4).reshape(tp, R, Z * RF)
        mixed = exchange(jnp.concatenate(pieces + [up], axis=2), ("seq", "core")).reshape(tp * R, -1)
        wo = lax.all_gather(output_weight, "z", axis=0)
        wqkv = lax.all_gather(after(mixed[:, : 3 * cols], wo), "z", axis=0, tiled=True)
        wqkv, up = after((wqkv, mixed[:, 3 * cols :]))
        wup = lax.all_gather(up, "z", axis=0, tiled=True)
        wdown = lax.all_gather(after(down_weight, wup), "z", axis=0, tiled=True)
        keep_part = lax.dynamic_slice_in_dim(wo, c * half, half, axis=0)
        got_part = swap_core(lax.dynamic_slice_in_dim(wo, (1 - c) * half, half, axis=0))
        wo = jnp.where(
            c == 0,
            jnp.stack([keep_part, got_part], axis=1),
            jnp.stack([got_part, keep_part], axis=1),
        ).reshape(cols, D)

        small = jnp.concatenate(
            [first_gain, first_shift, query_bias, value_bias, output_bias, second_gain, second_shift, down_bias, up_bias]
        )
        small = exchange(jnp.broadcast_to(after(small, mixed)[None], (n, small.shape[0])), every)
        small = small.astype(F32)
        g1, b1, qb, vb, ob, g2, b2, db = [small[:, i * R : (i + 1) * R].reshape(-1) for i in range(8)]
        ub = small[:, 8 * R :].reshape(S, Z, 2, RF)

        codes = jnp.stack([segment_ids[0], pad_mask[0]])
        codes = jnp.stack([codes] + [xor_seq(codes, q) for q in range(1, S)], axis=1)
        codes = [codes.reshape(2, L), swap_core(codes).reshape(2, L)]
        position = ((s ^ jnp.arange(S, dtype=jnp.int32))[:, None] * t + jnp.arange(t, dtype=jnp.int32)[None]).reshape(L)
        q_info = [jnp.stack([position, code[0]], axis=1) for code in codes]
        k_info = [jnp.stack([position, jnp.where(code[1] == 1, code[0], -1)]) for code in codes]
        keep = pad_mask[0].astype(F32)[:, None]

        xf = tokens[0].astype(F32)
        dy = cotangent[0]
        dyf = dy.astype(F32)
        xhat1, inv1 = normalize(xf)
        normed = plane_gather(lane_blocks((xhat1 * g1 + b1).astype(BF), natural))
        qkv_bias = jnp.stack([qb.reshape(tp, cols), jnp.zeros((tp, cols), F32), vb.reshape(tp, cols)], axis=1)
        qkv_bias = lax.dynamic_index_in_dim(qkv_bias, s * 2 + c, 0, keepdims=False).reshape(3 * cols)
        qkv_out, heads = [None, None], [None, None]
        for e in (1, 0):
            qkv_out[e] = (dot("td,de->te", normed[e], wqkv) + qkv_bias).astype(BF)
            heads[e] = attend_call(attend_kernel, heads_own, cols, 2, q_info[e], k_info[e], qkv_out[e])
        branch = add_up(*plane_scatter(dot("td,de->te", heads[0], wo), dot("td,de->te", heads[1], wo).astype(BF)))
        branch = after(branch, wup)
        middle = xf + (branch + ob) * keep
        xhat2, inv2 = normalize(middle)
        second = plane_gather(lane_blocks((xhat2 * g2 + b2).astype(BF), natural))
        dy_all = plane_gather(after(dy, second[0]))
        up_row = lax.dynamic_index_in_dim(lax.dynamic_index_in_dim(ub, s, 0, False), c, 1, False).reshape(Z * RF)
        active, slope = [None, None], [None, None]
        for e in both:
            hidden = dot("td,df->tf", second[e], wup) + up_row
            phi = 0.5 * (1.0 + lax.erf(hidden * math.sqrt(0.5)))
            slope[e] = phi + hidden * jnp.exp(-0.5 * hidden * hidden) * (1.0 / math.sqrt(2 * math.pi))
            active[e] = (hidden * phi).astype(BF)
        down_grad = dot("tf,td->fd", join(active), join(dy_all)).astype(BF)
        down_grad, wdown = after((down_grad, wdown))
        down_weight_grad = lax.psum_scatter(down_grad, "z", scatter_dimension=0, tiled=True)
        dhidden = [None, None]
        for e in (1, 0):
            dhidden[e] = (dot("td,fd->tf", dy_all[e], wdown) * slope[e]).astype(BF)

        mine, got = plane_scatter(
            dot("tf,df->td", dhidden[0], wup), dot("tf,df->td", dhidden[1], wup).astype(BF)
        )
        fill_dhidden, fill_second = after((dhidden, second), got[0])
        dhidden_join = join(fill_dhidden)
        up_grad = dot("td,tf->df", join(fill_second), dhidden_join).astype(BF)
        mine, got = after((mine, got), up_grad)
        up_grad = lax.psum_scatter(after(up_grad, down_weight_grad), "z", scatter_dimension=0, tiled=True)
        dsecond = lane_blocks(add_up(mine, got), back)
        dmiddle = dyf + norm_back(xhat2, inv2, g2 * dsecond)
        dbranch = (dmiddle * keep).astype(BF)
        dbranch_all = after(plane_gather(dbranch), down_weight_grad)
        dqkv = [None, None]
        for e in both:
            dheads = dot("te,de->td", dbranch_all[e], wo).astype(BF)
            dqkv[e] = attend_call(attend_back_kernel, heads_own, 3 * cols, 5, q_info[e], k_info[e], qkv_out[e], dheads)
        dqkv_join = join(dqkv)
        qkv_grad = dot("td,te->de", join(normed), dqkv_join).astype(BF)
        dqkv, late = after((dqkv, (dbranch_all, heads, active)), qkv_grad)
        qkv_grad = exchange(qkv_grad.reshape(n, R, 3 * cols), ("z", "seq", "core")).reshape(Z, tp, R, 3 * cols)
        mine, got = plane_scatter(dot("te,de->td", dqkv[0], wqkv), dot("te,de->td", dqkv[1], wqkv).astype(BF))
        dbranch_late, heads, active = after(late, got[0])
        wo_grad = dot("td,te->de", join(heads), join(dbranch_late)).astype(BF).reshape(half, 2, R, D)
        keep_part = lax.dynamic_index_in_dim(wo_grad, c, 1, False)
        got_part = swap_core(lax.dynamic_index_in_dim(wo_grad, 1 - c, 1, False))
        wo_grad = jnp.where(c == 0, join([keep_part, got_part]), join([got_part, keep_part]))
        output_weight_grad = spread_scatter(wo_grad, "z", Z, z)
        result = [dot("tf,fd->td", active[0], wdown), dot("tf,fd->td", active[1], wdown).astype(BF)]
        mine, got = after((mine, got), result)
        dnormed = lane_blocks(add_up(mine, got), back)
        input_grad = dmiddle + norm_back(xhat1, inv1, g1 * dnormed)
        block_output = (middle + add_up(*plane_scatter(*result)) + db).astype(BF)
        up_grad = after(up_grad, block_output, output_weight_grad).reshape(S, 2, R, Z * RF)
        up_grad = swap_blocks(swap_blocks(up_grad, 1, "core", 2, c), 0, "seq", S, s)
        up_weight_grad = up_grad.reshape(S, 2, R, Z, RF).transpose(2, 0, 3, 1, 4).reshape(R, -1).astype(F32)
        down_weight_grad = down_weight_grad.astype(F32)
        query_grad, key_grad, value_grad = finish_qkv(qkv_grad)

        bias = jnp.sum(dqkv_join.astype(F32), axis=0).reshape(3, cols)
        spread = jnp.zeros((2, tp, cols), F32)
        spread = lax.dynamic_update_slice(spread, jnp.stack([bias[0], bias[2]])[:, None], (0, s * 2 + c, 0))
        wide = jnp.zeros((S, Z, 2, RF), F32)
        wide = lax.dynamic_update_slice(
            wide, jnp.sum(dhidden_join.astype(F32), axis=0).reshape(1, Z, 1, RF), (s, 0, c, 0)
        )
        vectors = [
            jnp.sum(dbranch.astype(F32), axis=0),
            jnp.sum(dsecond * xhat2, axis=0),
            jnp.sum(dsecond, axis=0),
            jnp.sum(dyf, axis=0),
            wide,
            spread[0],
            spread[1],
            jnp.sum(dnormed * xhat1, axis=0),
            jnp.sum(dnormed, axis=0),
        ]
        packed = jnp.concatenate([v.reshape(S, Z, 2, -1) for v in vectors], axis=3)
        packed = lax.dynamic_index_in_dim(packed, c, 2, False) + swap_core(lax.dynamic_index_in_dim(packed, 1 - c, 2, False))
        packed = spread_scatter(packed, "seq", S, s)
        packed = spread_scatter(packed, "z", Z, z)
        ob_grad, g2_grad, b2_grad, db_grad = [packed[i * R : (i + 1) * R] for i in range(4)]
        ub_grad = packed[4 * R : 4 * R + RF]
        qb_grad, vb_grad, g1_grad, b1_grad = [packed[(4 + i) * R + RF : (5 + i) * R + RF] for i in range(4)]
        return (
            block_output[None], input_grad[None], g1_grad, b1_grad,
            query_grad, key_grad, value_grad, qb_grad, vb_grad,
            output_weight_grad, ob_grad, g2_grad, b2_grad,
            up_weight_grad, ub_grad, down_weight_grad, db_grad,
        )

    return body


def solution(mesh):
    S, DP = mesh.shape["seq"], mesh.shape["dp"]
    Z = DP // 2
    parts = Mesh(mesh.devices.reshape(S, Z, 2), ("seq", "z", "core"))
    every = ("seq", "z", "core")
    token = P(("z", "core"), "seq", None)
    code = P(("z", "core"), "seq")
    vector = P(every)
    matrix = P(every, None)
    return jax.shard_map(
        make_body(S, Z),
        mesh=parts,
        in_specs=(
            token, code, code, token,
            vector, vector, matrix, matrix, matrix, vector, vector,
            matrix, vector, vector, vector, matrix, vector, matrix, vector,
        ),
        out_specs=(
            token, token, vector, vector, matrix, matrix, matrix, vector, vector,
            matrix, vector, vector, vector, matrix, vector, matrix, vector,
        ),
        check_vma=False,
    )
```

time: 693 us -> 630 us (0.909)
  local copies, waits for them, and re-layouts: 98.8 us -> 74.5 us
  other arithmetic: 50.6 us -> 30.7 us
  waiting for transfers between devices: 329 us -> 310 us
    ppermute x38 -> x52, waiting for transfers between devices: 168 us -> 232 us  [flip(): return lax.ppermute(v, axis, [(i, i ^ q) for i in range(size)])]
    all_gather x2 -> x4, waiting for transfers between devices: 88.7 us -> 36.7 us  [the longest x1 19.7 us: body(): wup = lax.all_gather(up, 'z', axis=0, tiled=True)]
    all_to_all x7 -> x3, waiting for transfers between devices: 71.7 us -> 27.6 us  [exchange(): return lax.all_to_all(v, axes, split_axis=0, concat_axis=0, tiled=True)]
    ppermute x38 -> x52, starting transfers between devices: 33.2 us -> 61.4 us  [flip(): return lax.ppermute(v, axis, [(i, i ^ q) for i in range(size)])]
    reshape x12 -> x6, local copies, waits for them, and re-layouts: 14.7 us -> 0.47 us  [body(): packed = jnp.concatenate([v.reshape(S, Z, 2, -1) for v in vectors], axis=3)]
    all_to_all x7 -> x3, starting transfers between devices: 27.2 us -> 13.5 us  [exchange(): return lax.all_to_all(v, axes, split_axis=0, concat_axis=0, tiled=True)]
    reduce_scatter x1, waiting for transfers between devices: 0.01 us -> 12.8 us  [body(): lax.psum_scatter(down_grad, 'z', scatter_dimension=0, tiled=True)]
    unnamed x125 -> x210, local copies, waits for them, and re-layouts: 22.1 us -> 34.1 us
  transfers between devices with their start and end apart: 50 -> 61, of which waited for: 27 -> 27; matrix products, arithmetic and copies ran while one was open for 31% -> 23% of each run, Pallas kernels for 2% -> 2%
where the time goes in v3:
time: 630 us; the launch traced here: 625 us
  waiting for transfers between devices  310 us (49%)
  matrix products  96.3 us (15%)
  starting transfers between devices  75.5 us (12%)
  local copies, waits for them, and re-layouts  74.5 us (12%)
  other arithmetic  30.7 us (5%)
  Pallas kernels  22.5 us (4%)
  between operations  15.9 us (3%)
    ppermute x52, waiting for transfers between devices, flip(): return lax.ppermute(v, axis, [(i, i ^ q) for i in range(size)])  232 us
    dot_general x20, matrix products, dot(): return jnp.einsum(form, left, right, preferred_element_type=F32)  96.3 us
    ppermute x52, starting transfers between devices, flip(): return lax.ppermute(v, axis, [(i, i ^ q) for i in range(size)])  61.4 us
    unnamed x210, local copies, waits for them, and re-layouts  34.1 us
    all_to_all x3, waiting for transfers between devices, exchange(): return lax.all_to_all(v, axes, split_axis=0, concat_axis=0, tiled=True)  27.6 us
    all_gather x1, waiting for transfers between devices, body(): wup = lax.all_gather(up, 'z', axis=0, tiled=True)  19.7 us
    pallas_call x4, Pallas kernels, attend_call(): pl.pallas_call(functools.partial(kernel, heads), out_shape=jax.ShapeDtype...  16.7 us
    all_gather x1, waiting for transfers between devices, body(): lax.all_gather(after(mixed[:, :3 * cols], wo), 'z', axis=0, tiled=True)  15.8 us
  transfers between devices with their start and end apart: 61, of which 27 were waited for; matrix products, arithmetic and copies ran while one was open for 23% of the time, Pallas kernels for 2%

profile of v3, /device:TPU:0, one launch (start us, length us, event | category | flops | bytes accessed | tf_op | source)
XLA Modules:
  0.0 625.1 jit_solution(5919794490099087047)
XLA Ops:
  12.2 5.2 all-to-all-start
  18.7 22.5 %all-to-all-done = bf16[8,64,1792]{2,1,0:T(8,128)(2,1)S(1)} async-done(((bf16[8,64,1792]{2,1,0:T(8,128)(2,1)}), bf16[8,64,1792]{2,1,0:T(8,128)(2,1)S(1)}, u32[]{:S(2)}, u32[]{:S(2)}) %all-to-all-start) | async-done | bytes 1835040 | tf_op jit(solution)/shard_map/all_to_all | solution.py:152
  49.5 5.1 all-to-all-done.1
  69.7 11.3 %collective-permute-done.3 = bf16[128,2048]{1,0:T(8,128)(2,1)S(1)} collective-permute-done((bf16[128,2048]{1,0:T(8,128)(2,1)S(1)}, bf16[128,2048]{1,0:T(8,128)(2,1)S(1)}, u32[]{:S(2)}, u32[]{:S(2)}) %collective-permute-start.3) | collective-permute-done | bytes 524320 | tf_op jit(solution)/shard_map/ppermute | solution.py:125
  81.0 10.5 %collective-permute-done.4 = bf16[128,2048]{1,0:T(8,128)(2,1)S(1)} collective-permute-done((bf16[128,2048]{1,0:T(8,128)(2,1)S(1)}, bf16[128,2048]{1,0:T(8,128)(2,1)S(1)}, u32[]{:S(2)}, u32[]{:S(2)}) %collective-permute-start.4) | collective-permute-done | bytes 524320 | tf_op jit(solution)/shard_map/ppermute | solution.py:125
  99.2 15.8 %all-gather.6.cloned.1.call-done = bf16[2048,768]{1,0:T(8,128)(2,1)} async-done(((bf16[512,768]{1,0:T(8,128)(2,1)}), bf16[2048,768]{1,0:T(8,128)(2,1)}) %all-gather.6.cloned.1.call-update) | async-done | bytes 3145744 | tf_op jit(solution)/shard_map/all_gather | solution.py:191
  120.6 5.5 add_convert_fusion.qkv_ref
  151.2 11.2 %collective-permute-done.10 = bf16[128,2048]{1,0:T(8,128)(2,1)S(1)} collective-permute-done((bf16[128,2048]{1,0:T(8,128)(2,1)}, bf16[128,2048]{1,0:T(8,128)(2,1)S(1)}, u32[]{:S(2)}, u32[]{:S(2)}) %collective-permute-start.10) | collective-permute-done | bytes 524320 | tf_op jit(solution)/shard_map/ppermute | solution.py:125
  162.4 12.0 %collective-permute-done.11 = bf16[128,2048]{1,0:T(8,128)(2,1)S(1)} collective-permute-done((bf16[128,2048]{1,0:T(8,128)(2,1)}, bf16[128,2048]{1,0:T(8,128)(2,1)S(1)}, u32[]{:S(2)}, u32[]{:S(2)}) %collective-permute-start.11) | collective-permute-done | bytes 524320 | tf_op jit(solution)/shard_map/ppermute | solution.py:125
  176.9 19.7 %all-gather.8.cloned.1.call-done = bf16[2048,1024]{1,0:T(8,128)(2,1)} async-done(((bf16[512,1024]{1,0:T(8,128)(2,1)}), bf16[2048,1024]{1,0:T(8,128)(2,1)}) %all-gather.8.cloned.1.call-update) | async-done | bytes 4194320 | tf_op jit(solution)/shard_map/all_gather | solution.py:193
  212.5 11.5 %collective-permute-done.13 = bf16[128,2048]{1,0:T(8,128)(2,1)S(1)} collective-permute-done((bf16[128,2048]{1,0:T(8,128)(2,1)}, bf16[128,2048]{1,0:T(8,128)(2,1)S(1)}, u32[]{:S(2)}, u32[]{:S(2)}) %collective-permute-start.13) | collective-permute-done | bytes 524320 | tf_op jit(solution)/shard_map/ppermute | solution.py:125
  224.0 11.3 %collective-permute-done.14 = bf16[128,2048]{1,0:T(8,128)(2,1)S(1)} collective-permute-done((bf16[128,2048]{1,0:T(8,128)(2,1)}, bf16[128,2048]{1,0:T(8,128)(2,1)S(1)}, u32[]{:S(2)}, u32[]{:S(2)}) %collective-permute-start.14) | collective-permute-done | bytes 524320 | tf_op jit(solution)/shard_map/ppermute | solution.py:125
  242.7 10.3 %collective-permute-done.16 = bf16[128,2048]{1,0:T(8,128)(2,1)S(1)} collective-permute-done((bf16[128,2048]{1,0:T(8,128)(2,1)S(1)}, bf16[128,2048]{1,0:T(8,128)(2,1)S(1)}, u32[]{:S(2)}, u32[]{:S(2)}) %collective-permute-start.16) | collective-permute-done | bytes 524320 | tf_op jit(solution)/shard_map/ppermute | solution.py:125
  253.9 9.2 %collective-permute-done.17 = bf16[128,2048]{1,0:T(8,128)(2,1)S(1)} collective-permute-done((bf16[128,2048]{1,0:T(8,128)(2,1)S(1)}, bf16[128,2048]{1,0:T(8,128)(2,1)S(1)}, u32[]{:S(2)}, u32[]{:S(2)}) %collective-permute-start.17) | collective-permute-done | bytes 524320 | tf_op jit(solution)/shard_map/ppermute | solution.py:125
  267.9 5.3 fusion.89
  273.2 7.0 %multiply_convert_fusion.1 = (bf16[512,1024]{1,0:T(8,128)(2,1)S(1)}, bf16[512,1024]{1,0:T(8,128)(2,1)S(1)}, f32[512,1024]{1,0:T(8,128)}) fusion(f32[1024]{0:T(1024)S(1)} %bitcast.193, f32[512,1024]{1,0:T(8,128)S(1)} %fusion.89, bf16[2048,1024]{1,0:T(8,128)(2,1)S(1)} %copy-done.58, bf16[128,2048]{1,0:T(8,128)(2,1)S(1)} %copy-done.33, ...), kind=kOutput, calls=%fused_computation.45 | convolution fusion | flops 2162163712 | bytes 12587008 | tf_op jit(solution)/shard_map/td,df->tf/dot_general | solution.py:22
  282.7 6.7 %convolution_convert_fusion = bf16[1024,2048]{1,0:T(8,128)(2,1)} fusion(bf16[1024,2048]{1,0:T(8,128)(2,1)S(1)} %constant_dynamic-update-slice_fusion.36, bf16[512,1024]{1,0:T(8,128)(2,1)S(1)} %get-tuple-element.87, bf16[512,1024]{1,0:T(8,128)(2,1)S(1)} %get-tuple-element.86), kind=kOutput, calls=%fused_computation.14 | convolution fusion | flops 4301258752 | bytes 10485760 | tf_op jit(solution)/shard_map/tf,td->fd/dot_general | solution.py:22
  289.5 6.5 %fusion.25 = bf16[512,1024]{1,0:T(8,128)(2,1)S(1)} fusion(f32[512,1024]{1,0:T(8,128)} %copy-done.64, bf16[512,2048]{1,0:T(8,128)(2,1)} %collective-permute-done.20, bf16[1024,2048]{1,0:T(8,128)(2,1)} %all-gather.10.cloned.1.call-done, f32[1024]{0:T(1024)S(1)} %bitcast.194), kind=kOutput, calls=%fused_computation.35 | convolution fusion | flops 2153250816 | bytes 9441280 | tf_op jit(solution)/shard_map/td,fd->tf/dot_general | solution.py:22
  315.4 9.0 %collective-permute-done.22 = bf16[128,2048]{1,0:T(8,128)(2,1)S(1)} collective-permute-done((bf16[128,2048]{1,0:T(8,128)(2,1)}, bf16[128,2048]{1,0:T(8,128)(2,1)S(1)}, u32[]{:S(2)}, u32[]{:S(2)}) %collective-permute-start.22) | collective-permute-done | bytes 524320 | tf_op jit(solution)/shard_map/ppermute | solution.py:125
  327.1 8.7 %fusion.8 = bf16[2048,1024]{1,0:T(8,128)(2,1)} fusion(bf16[1024,1024]{1,0:T(8,128)(2,1)S(1)} %constant_dynamic-update-slice_fusion.41, bf16[512,2048]{1,0:T(8,128)(2,1)} %collective-permute-done.19, bf16[512,2048]{1,0:T(8,128)(2,1)} %pad_maximum_fusion.1), kind=kOutput, calls=%fused_computation.13 | convolution fusion | flops 4305453056 | bytes 10485760 | tf_op jit(solution)/shard_map/td,tf->df/dot_general | solution.py:22
  344.8 11.4 %collective-permute-done.25 = bf16[128,2048]{1,0:T(8,128)(2,1)S(1)} collective-permute-done((bf16[128,2048]{1,0:T(8,128)(2,1)S(1)}, bf16[128,2048]{1,0:T(8,128)(2,1)S(1)}, u32[]{:S(2)}, u32[]{:S(2)}) %collective-permute-start.25) | collective-permute-done | bytes 524320 | tf_op jit(solution)/shard_map/ppermute | solution.py:125
  356.2 10.7 %collective-permute-done.26 = bf16[128,2048]{1,0:T(8,128)(2,1)S(1)} collective-permute-done((bf16[128,2048]{1,0:T(8,128)(2,1)S(1)}, bf16[128,2048]{1,0:T(8,128)(2,1)S(1)}, u32[]{:S(2)}, u32[]{:S(2)}) %collective-permute-start.26) | collective-permute-done | bytes 524320 | tf_op jit(solution)/shard_map/ppermute | solution.py:125
  373.1 12.8 %reduce-scatter.3.cloned.1.call-done = bf16[256,2048]{1,0:T(8,128)(2,1)} async-done(((bf16[1024,2048]{1,0:T(8,128)(2,1)}), bf16[256,2048]{1,0:T(8,128)(2,1)}) %reduce-scatter.3.cloned.1.call-update) | async-done | bytes 1048592 | tf_op jit(solution)/shard_map/reduce_scatter | solution.py:245
  395.3 4.9 shard_map.316
  400.2 7.9 %convolution_convert_fusion.1 = bf16[2048,768]{1,0:T(8,128)(2,1)} fusion(bf16[1024,2048]{1,0:T(8,128)(2,1)} %constant_dynamic-update-slice_fusion.59, bf16[512,768]{1,0:T(8,128)(2,1)S(1)} %copy-done.25, bf16[512,768]{1,0:T(8,128)(2,1)} %shard_map.316), kind=kOutput, calls=%fused_computation.15 | convolution fusion | flops 3225944064 | bytes 8912896 | tf_op jit(solution)/shard_map/td,te->de/dot_general | solution.py:22
  415.8 6.4 %fusion.76 = (bf16[512,2048]{1,0:T(8,128)(2,1)S(1)}, f32[512,2048]{1,0:T(8,128)}) fusion(bf16[512,2048]{1,0:T(8,128)(2,1)} %collective-permute-done.29, bf16[512,768]{1,0:T(8,128)(2,1)S(1)} %copy-done.24, bf16[2048,768]{1,0:T(8,128)(2,1)} %all-gather.6.cloned.1.call-done), kind=kOutput, calls=%fused_computation.270 | convolution fusion | flops 1613758464 | bytes 12320768 | tf_op jit(solution)/shard_map/te,de->td/dot_general | solution.py:22
  450.9 21.0 %collective-permute-done.35 = bf16[128,2048]{1,0:T(8,128)(2,1)S(1)} collective-permute-done((bf16[128,2048]{1,0:T(8,128)(2,1)}, bf16[128,2048]{1,0:T(8,128)(2,1)S(1)}, u32[]{:S(2)}, u32[]{:S(2)}) %collective-permute-start.35) | collective-permute-done | bytes 524320 | tf_op jit(solution)/shard_map/ppermute | solution.py:125
  482.9 5.0 collective-permute-start.32
  489.3 53.4 %collective-permute-done.45 = bf16[64,2048]{1,0:T(8,128)(2,1)S(1)} collective-permute-done((bf16[64,2048]{1,0:T(8,128)(2,1)S(1)}, bf16[64,2048]{1,0:T(8,128)(2,1)S(1)}, u32[]{:S(2)}, u32[]{:S(2)}) %collective-permute-start.45) | collective-permute-done | bytes 262176 | tf_op jit(solution)/shard_map/ppermute | solution.py:125
  545.6 29.7 %collective-permute-done.46 = bf16[64,2048]{1,0:T(8,128)(2,1)S(1)} collective-permute-done((bf16[64,2048]{1,0:T(8,128)(2,1)S(1)}, bf16[64,2048]{1,0:T(8,128)(2,1)S(1)}, u32[]{:S(2)}, u32[]{:S(2)}) %collective-permute-start.46) | collective-permute-done | bytes 262176 | tf_op jit(solution)/shard_map/ppermute | solution.py:125
  589.1 5.6 collective-permute-start.41
  602.9 5.7 shard_map.318
  (450 shorter events, 230.2 us)
Async XLA Ops:
  12.2 29.0 %all-to-all-start = ((bf16[8,64,1792]{2,1,0:T(8,128)(2,1)}), bf16[8,64,1792]{2,1,0:T(8,128)(2,1)S(1)}, u32[]{:S(2)}, u32[]{:S(2)}) async-start(bf16[8,64,1792]{2,1,0:T(8,128)(2,1)} %pad_maximum_fusion.3), calls=%async_computation | async-start | bytes 3670016 | tf_op jit(solution)/shard_map/all_to_all | solution.py:152
  17.3 32.1 %all-gather.12.cloned.1.call-start = ((), (), s32[]{:S(2)}) async-start(), calls=%async_computation.10 | async-start | bytes 1310720 | tf_op jit(solution)/shard_map/all_gather | solution.py:190
  47.3 67.8 %all-gather.6.cloned.1.call-start = ((), (), s32[]{:S(2)}) async-start(), calls=%async_computation.5 | async-start | bytes 3932160 | tf_op jit(solution)/shard_map/all_gather | solution.py:191
  49.4 147.2 %all-gather.8.cloned.1.call-start = ((), (), s32[]{:S(2)}) async-start(), calls=%async_computation.6 | async-start | bytes 5242880 | tf_op jit(solution)/shard_map/all_gather | solution.py:193
  66.9 24.6 %collective-permute-start.4 = (bf16[128,2048]{1,0:T(8,128)(2,1)S(1)}, bf16[128,2048]{1,0:T(8,128)(2,1)S(1)}, u32[]{:S(2)}, u32[]{:S(2)}) collective-permute-start(bf16[128,2048]{1,0:T(8,128)(2,1)S(1)} %get-tuple-element.150), channel_id=1, source_target_pairs={{0,16},{8,24},{16,0},{24,8},{1,17},{9,25},{17,1},{25,9},{2,18},{10... | collective-permute-start | bytes 1572872 | tf_op jit(solution)/shard_map/ppermute | solution.py:125
  67.5 24.0 %collective-permute-start.5 = (bf16[128,2048]{1,0:T(8,128)(2,1)S(1)}, bf16[128,2048]{1,0:T(8,128)(2,1)S(1)}, u32[]{:S(2)}, u32[]{:S(2)}) collective-permute-start(bf16[128,2048]{1,0:T(8,128)(2,1)S(1)} %get-tuple-element.150), channel_id=1, source_target_pairs={{0,24},{8,16},{16,8},{24,0},{1,25},{9,17},{17,9},{25,1},{2,26},{10... | collective-permute-start | bytes 1572872 | tf_op jit(solution)/shard_map/ppermute | solution.py:125
  93.8 26.8 %collective-permute-start.8 = (bf16[512,2048]{1,0:T(8,128)(2,1)}, bf16[512,2048]{1,0:T(8,128)(2,1)}, u32[]{:S(2)}, u32[]{:S(2)}) collective-permute-start(bf16[512,2048]{1,0:T(8,128)(2,1)} %pad_maximum_fusion), channel_id=1, source_target_pairs={{0,1},{1,0},{2,3},{3,2},{4,5},{5,4},{6,7},{7,6},{8,9},{9,8},{10,11... | collective-permute-start | bytes 6291464 | tf_op jit(solution)/shard_map/ppermute | solution.py:125
  115.1 174.4 %all-gather.10.cloned.1.call-start = ((), (), s32[]{:S(2)}) async-start(), calls=%async_computation.7 | async-start | bytes 5242880 | tf_op jit(solution)/shard_map/all_gather | solution.py:194
  148.9 25.5 %collective-permute-start.11 = (bf16[128,2048]{1,0:T(8,128)(2,1)}, bf16[128,2048]{1,0:T(8,128)(2,1)S(1)}, u32[]{:S(2)}, u32[]{:S(2)}) collective-permute-start(bf16[128,2048]{1,0:T(8,128)(2,1)} %get-tuple-element.137), channel_id=1, source_target_pairs={{0,16},{8,24},{16,0},{24,8},{1,17},{9,25},{17,1},{25,9},{2,18},{10... | collective-permute-start | bytes 1572872 | tf_op jit(solution)/shard_map/ppermute | solution.py:125
  150.4 24.1 %collective-permute-start.12 = (bf16[128,2048]{1,0:T(8,128)(2,1)}, bf16[128,2048]{1,0:T(8,128)(2,1)S(1)}, u32[]{:S(2)}, u32[]{:S(2)}) collective-permute-start(bf16[128,2048]{1,0:T(8,128)(2,1)} %get-tuple-element.136), channel_id=1, source_target_pairs={{0,24},{8,16},{16,8},{24,0},{1,25},{9,17},{17,9},{25,1},{2,26},{10... | collective-permute-start | bytes 1572872 | tf_op jit(solution)/shard_map/ppermute | solution.py:125
  206.2 179.7 %reduce-scatter.3.cloned.1.call-start = ((), (), s32[]{:S(2)}) async-start(), calls=%async_computation.8 | async-start | bytes 5242880 | tf_op jit(solution)/shard_map/reduce_scatter | solution.py:245
  210.5 24.8 %collective-permute-start.14 = (bf16[128,2048]{1,0:T(8,128)(2,1)}, bf16[128,2048]{1,0:T(8,128)(2,1)S(1)}, u32[]{:S(2)}, u32[]{:S(2)}) collective-permute-start(bf16[128,2048]{1,0:T(8,128)(2,1)} %constant_dynamic-update-slice_fusion.16), channel_id=1, source_target_pairs={{0,16},{8,24},{16,0},{24,8},{1,17},{9,25},{17,1},{25,9},{2,18},{10... | collective-permute-start | bytes 1572872 | tf_op jit(solution)/shard_map/ppermute | solution.py:125
  212.0 23.3 %collective-permute-start.15 = (bf16[128,2048]{1,0:T(8,128)(2,1)}, bf16[128,2048]{1,0:T(8,128)(2,1)S(1)}, u32[]{:S(2)}, u32[]{:S(2)}) collective-permute-start(bf16[128,2048]{1,0:T(8,128)(2,1)} %constant_dynamic-update-slice_fusion.16), channel_id=1, source_target_pairs={{0,24},{8,16},{16,8},{24,0},{1,25},{9,17},{17,9},{25,1},{2,26},{10... | collective-permute-start | bytes 1572872 | tf_op jit(solution)/shard_map/ppermute | solution.py:125
  238.3 29.6 %collective-permute-start.19 = (bf16[512,2048]{1,0:T(8,128)(2,1)}, bf16[512,2048]{1,0:T(8,128)(2,1)}, u32[]{:S(2)}, u32[]{:S(2)}) collective-permute-start(bf16[512,2048]{1,0:T(8,128)(2,1)} %pad_maximum_fusion.1), channel_id=1, source_target_pairs={{0,1},{1,0},{2,3},{3,2},{4,5},{5,4},{6,7},{7,6},{8,9},{9,8},{10,11... | collective-permute-start | bytes 6291464 | tf_op jit(solution)/shard_map/ppermute | solution.py:125
  239.3 23.9 %collective-permute-start.17 = (bf16[128,2048]{1,0:T(8,128)(2,1)S(1)}, bf16[128,2048]{1,0:T(8,128)(2,1)S(1)}, u32[]{:S(2)}, u32[]{:S(2)}) collective-permute-start(bf16[128,2048]{1,0:T(8,128)(2,1)S(1)} %bitcast.174), channel_id=1, source_target_pairs={{0,16},{8,24},{16,0},{24,8},{1,17},{9,25},{17,1},{25,9},{2,18},{10... | collective-permute-start | bytes 1572872 | tf_op jit(solution)/shard_map/ppermute | solution.py:125
  240.3 24.5 %collective-permute-start.18 = (bf16[128,2048]{1,0:T(8,128)(2,1)S(1)}, bf16[128,2048]{1,0:T(8,128)(2,1)S(1)}, u32[]{:S(2)}, u32[]{:S(2)}) collective-permute-start(bf16[128,2048]{1,0:T(8,128)(2,1)S(1)} %bitcast.175), channel_id=1, source_target_pairs={{0,24},{8,16},{16,8},{24,0},{1,25},{9,17},{17,9},{25,1},{2,26},{10... | collective-permute-start | bytes 1572872 | tf_op jit(solution)/shard_map/ppermute | solution.py:125
  311.3 266.2 %reduce-scatter.5.cloned.1.call-start = ((), (), s32[]{:S(2)}) async-start(), calls=%async_computation.9 | async-start | bytes 5242880 | tf_op jit(solution)/shard_map/reduce_scatter | solution.py:257
  311.3 25.7 %collective-permute-start.23 = (bf16[128,2048]{1,0:T(8,128)(2,1)}, bf16[128,2048]{1,0:T(8,128)(2,1)}, u32[]{:S(2)}, u32[]{:S(2)}) collective-permute-start(bf16[128,2048]{1,0:T(8,128)(2,1)} %get-tuple-element.133), channel_id=1, source_target_pairs={{0,16},{8,24},{16,0},{24,8},{1,17},{9,25},{17,1},{25,9},{2,18},{10... | collective-permute-start | bytes 1572872 | tf_op jit(solution)/shard_map/ppermute | solution.py:125
  312.8 24.1 %collective-permute-start.24 = (bf16[128,2048]{1,0:T(8,128)(2,1)}, bf16[128,2048]{1,0:T(8,128)(2,1)}, u32[]{:S(2)}, u32[]{:S(2)}) collective-permute-start(bf16[128,2048]{1,0:T(8,128)(2,1)} %get-tuple-element.132), channel_id=1, source_target_pairs={{0,24},{8,16},{16,8},{24,0},{1,25},{9,17},{17,9},{25,1},{2,26},{10... | collective-permute-start | bytes 1572872 | tf_op jit(solution)/shard_map/ppermute | solution.py:125
  342.4 24.5 %collective-permute-start.26 = (bf16[128,2048]{1,0:T(8,128)(2,1)S(1)}, bf16[128,2048]{1,0:T(8,128)(2,1)S(1)}, u32[]{:S(2)}, u32[]{:S(2)}) collective-permute-start(bf16[128,2048]{1,0:T(8,128)(2,1)S(1)} %get-tuple-element.114), channel_id=1, source_target_pairs={{0,16},{8,24},{16,0},{24,8},{1,17},{9,25},{17,1},{25,9},{2,18},{10... | collective-permute-start | bytes 1572872 | tf_op jit(solution)/shard_map/ppermute | solution.py:125
  343.4 23.5 %collective-permute-start.27 = (bf16[128,2048]{1,0:T(8,128)(2,1)S(1)}, bf16[128,2048]{1,0:T(8,128)(2,1)S(1)}, u32[]{:S(2)}, u32[]{:S(2)}) collective-permute-start(bf16[128,2048]{1,0:T(8,128)(2,1)S(1)} %get-tuple-element.114), channel_id=1, source_target_pairs={{0,24},{8,16},{16,8},{24,0},{1,25},{9,17},{17,9},{25,1},{2,26},{10... | collective-permute-start | bytes 1572872 | tf_op jit(solution)/shard_map/ppermute | solution.py:125
  425.2 177.7 %all-to-all-start.2 = ((bf16[32,64,768]{2,1,0:T(8,128)(2,1)}), bf16[32,64,768]{2,1,0:T(8,128)(2,1)}, u32[]{:S(2)}, u32[]{:S(2)}) async-start(bf16[32,64,768]{2,1,0:T(8,128)(2,1)} %bitcast.172), calls=%async_computation.3 | async-start | bytes 6291456 | tf_op jit(solution)/shard_map/all_to_all | solution.py:152
  431.1 40.8 %collective-permute-start.35 = (bf16[128,2048]{1,0:T(8,128)(2,1)}, bf16[128,2048]{1,0:T(8,128)(2,1)S(1)}, u32[]{:S(2)}, u32[]{:S(2)}) collective-permute-start(bf16[128,2048]{1,0:T(8,128)(2,1)} %get-tuple-element.127), channel_id=1, source_target_pairs={{0,16},{8,24},{16,0},{24,8},{1,17},{9,25},{17,1},{25,9},{2,18},{10... | collective-permute-start | bytes 1572872 | tf_op jit(solution)/shard_map/ppermute | solution.py:125
  432.8 39.1 %collective-permute-start.36 = (bf16[128,2048]{1,0:T(8,128)(2,1)S(1)}, bf16[128,2048]{1,0:T(8,128)(2,1)S(1)}, u32[]{:S(2)}, u32[]{:S(2)}) collective-permute-start(bf16[128,2048]{1,0:T(8,128)(2,1)S(1)} %copy-done.27), channel_id=1, source_target_pairs={{0,24},{8,16},{16,8},{24,0},{1,25},{9,17},{17,9},{25,1},{2,26},{10... | collective-permute-start | bytes 1572872 | tf_op jit(solution)/shard_map/ppermute | solution.py:125
  442.3 32.0 %collective-permute-start.44 = (bf16[2,64,2048]{2,1,0:T(8,128)(2,1)}, bf16[2,64,2048]{2,1,0:T(8,128)(2,1)S(1)}, u32[]{:S(2)}, u32[]{:S(2)}) collective-permute-start(bf16[2,64,2048]{2,1,0:T(8,128)(2,1)} %get-tuple-element.145), channel_id=1, source_target_pairs={{0,1},{1,0},{2,3},{3,2},{4,5},{5,4},{6,7},{7,6},{8,9},{9,8},{10,11... | collective-permute-start | bytes 1572872 | tf_op jit(solution)/shard_map/ppermute | solution.py:125
  446.0 33.1 %collective-permute-start.31 = (bf16[512,2048]{1,0:T(8,128)(2,1)}, bf16[512,2048]{1,0:T(8,128)(2,1)}, u32[]{:S(2)}, u32[]{:S(2)}) collective-permute-start(bf16[512,2048]{1,0:T(8,128)(2,1)} %convolution_convert_fusion.2), channel_id=1, source_target_pairs={{0,1},{1,0},{2,3},{3,2},{4,5},{5,4},{6,7},{7,6},{8,9},{9,8},{10,11... | collective-permute-start | bytes 6291464 | tf_op jit(solution)/shard_map/ppermute | solution.py:125
  474.6 68.1 %collective-permute-start.45 = (bf16[64,2048]{1,0:T(8,128)(2,1)S(1)}, bf16[64,2048]{1,0:T(8,128)(2,1)S(1)}, u32[]{:S(2)}, u32[]{:S(2)}) collective-permute-start(bf16[64,2048]{1,0:T(8,128)(2,1)S(1)} %get-tuple-element.141), channel_id=1, source_target_pairs={{0,2},{2,0},{4,6},{6,4},{1,3},{3,1},{5,7},{7,5},{8,10},{10,8},{12,... | collective-permute-start | bytes 786440 | tf_op jit(solution)/shard_map/ppermute | solution.py:125
  475.8 99.6 %collective-permute-start.46 = (bf16[64,2048]{1,0:T(8,128)(2,1)S(1)}, bf16[64,2048]{1,0:T(8,128)(2,1)S(1)}, u32[]{:S(2)}, u32[]{:S(2)}) collective-permute-start(bf16[64,2048]{1,0:T(8,128)(2,1)S(1)} %get-tuple-element.143), channel_id=1, source_target_pairs={{0,4},{2,6},{4,0},{6,2},{1,5},{3,7},{5,1},{7,3},{8,12},{10,14},{12... | collective-permute-start | bytes 786440 | tf_op jit(solution)/shard_map/ppermute | solution.py:125
  478.5 96.9 %collective-permute-start.47 = (bf16[64,2048]{1,0:T(8,128)(2,1)S(1)}, bf16[64,2048]{1,0:T(8,128)(2,1)S(1)}, u32[]{:S(2)}, u32[]{:S(2)}) collective-permute-start(bf16[64,2048]{1,0:T(8,128)(2,1)S(1)} %get-tuple-element.142), channel_id=1, source_target_pairs={{0,6},{2,4},{4,2},{6,0},{1,7},{3,5},{5,3},{7,1},{8,14},{10,12},{12... | collective-permute-start | bytes 786440 | tf_op jit(solution)/shard_map/ppermute | solution.py:125
  482.9 93.4 %collective-permute-start.32 = (bf16[128,2048]{1,0:T(8,128)(2,1)S(1)}, bf16[128,2048]{1,0:T(8,128)(2,1)S(1)}, u32[]{:S(2)}, u32[]{:S(2)}) collective-permute-start(bf16[128,2048]{1,0:T(8,128)(2,1)S(1)} %get-tuple-element.129), channel_id=1, source_target_pairs={{0,8},{8,0},{16,24},{24,16},{1,9},{9,1},{17,25},{25,17},{2,10},{10... | collective-permute-start | bytes 1572872 | tf_op jit(solution)/shard_map/ppermute | solution.py:125
  488.0 88.3 %collective-permute-start.33 = (bf16[128,2048]{1,0:T(8,128)(2,1)S(1)}, bf16[128,2048]{1,0:T(8,128)(2,1)S(1)}, u32[]{:S(2)}, u32[]{:S(2)}) collective-permute-start(bf16[128,2048]{1,0:T(8,128)(2,1)S(1)} %get-tuple-element.131), channel_id=1, source_target_pairs={{0,16},{8,24},{16,0},{24,8},{1,17},{9,25},{17,1},{25,9},{2,18},{10... | collective-permute-start | bytes 1572872 | tf_op jit(solution)/shard_map/ppermute | solution.py:125
  542.7 33.6 %collective-permute-start.34 = (bf16[128,2048]{1,0:T(8,128)(2,1)S(1)}, bf16[128,2048]{1,0:T(8,128)(2,1)S(1)}, u32[]{:S(2)}, u32[]{:S(2)}) collective-permute-start(bf16[128,2048]{1,0:T(8,128)(2,1)S(1)} %get-tuple-element.130), channel_id=1, source_target_pairs={{0,24},{8,16},{16,8},{24,0},{1,25},{9,17},{17,9},{25,1},{2,26},{10... | collective-permute-start | bytes 1572872 | tf_op jit(solution)/shard_map/ppermute | solution.py:125
  (96 other events, 1015.2 us)
Sparse Core Ops, SparseCore 0:
  19.7 29.6 all-gather.11
  51.5 63.4 all-gather.5
  117.2 79.3 all-gather.7
  206.4 79.2 all-gather.9
  311.4 74.4 reduce-scatter.2
  413.9 133.1 reduce-scatter.4

commit v4 on v3

--- a/solution.py
+++ b/solution.py
@@ -93,23 +93,49 @@
 
 
 def finish_kernel(in_ref, q_ref, k_ref, v_ref):
-    total = jnp.sum(in_ref[:, 0].astype(F32), axis=0)
-    cols = q_ref.shape[1]
-    q_ref[...] = total[:, :cols]
-    k_ref[...] = total[:, cols : 2 * cols]
-    v_ref[...] = total[:, 2 * cols :]
+    places, _, wide = in_ref.shape
+    cols = wide // 3
+    for j in range(places):
+        for part, out_ref in enumerate((q_ref, k_ref, v_ref)):
+            out_ref[:, j * cols : (j + 1) * cols] = in_ref[j, :, part * cols : (part + 1) * cols].astype(F32)
 
 
 def finish_qkv(v):
-    Z, places, R, wide = v.shape
-    cols = wide // 3
-    out = jax.ShapeDtypeStruct((R, places * cols), F32)
+    places, R, wide = v.shape
+    out = jax.ShapeDtypeStruct((R, places * wide // 3), F32)
+    return pl.pallas_call(finish_kernel, out_shape=[out] * 3)(v)
+
+
+def spread_kernel(starts, width, in_ref, out_ref):
+    for j, row in enumerate(starts):
+        for i, to in enumerate(row):
+            out_ref[:, to * width : (to + 1) * width] = in_ref[j, :, i * width : (i + 1) * width].astype(F32)
+
+
+def finish_up(v, S, Z):
+    places, R, wide = v.shape
+    width = wide // Z
+    starts = [[((j // 2) * Z + i) * 2 + j % 2 for i in range(Z)] for j in range(places)]
+    if width % 128:
+        return v.reshape(S, 2, R, Z, width).transpose(2, 0, 3, 1, 4).reshape(R, -1).astype(F32)
+    out = jax.ShapeDtypeStruct((R, places * wide), F32)
+    return pl.pallas_call(functools.partial(spread_kernel, starts, width), out_shape=out)(v)
+
+
+def reorder_kernel(order, in_ref, out_ref):
+    width = in_ref.shape[1] // len(order)
+    for to, at in enumerate(order):
+        out_ref[:, to * width : (to + 1) * width] = in_ref[:, at * width : (at + 1) * width]
+
+
+def lane_blocks(v, order):
+    width = v.shape[1] // len(order)
+    if width % 128:
+        return jnp.concatenate([v[:, i * width : (i + 1) * width] for i in order], axis=1)
     return pl.pallas_call(
-        finish_kernel,
-        grid=(places,),
-        in_specs=[pl.BlockSpec((Z, 1, R, wide), lambda j: (0, j, 0, 0))],
-        out_specs=[pl.BlockSpec((R, cols), lambda j: (0, j))] * 3,
-        out_shape=[out] * 3,
+        functools.partial(reorder_kernel, order),
+        out_shape=jax.ShapeDtypeStruct(v.shape, v.dtype),
+        cost_estimate=pl.CostEstimate(flops=0, bytes_accessed=2 * v.size * v.dtype.itemsize, transcendentals=0),
     )(v)
 
 
@@ -150,13 +176,6 @@
 
     def exchange(v, axes):
         return lax.all_to_all(v, axes, split_axis=0, concat_axis=0, tiled=True)
-
-    def swap_blocks(v, at, axis, size, me):
-        out = v
-        for q in range(1, size):
-            got = flip(lax.dynamic_index_in_dim(v, me ^ q, at, True), axis, size, q)
-            out = lax.dynamic_update_slice_in_dim(out, got, me ^ q, at)
-        return out
 
     def spread_scatter(v, axis, size, me):
         got = [flip(lax.dynamic_index_in_dim(v, me ^ q, 0, False), axis, size, q) for q in range(1, size)]
@@ -177,9 +196,6 @@
         cols = D // tp
         half = Z // 2
         both = range(2)
-
-        def lane_blocks(v, order):
-            return jnp.concatenate([v[:, i * 2 * R : (i + 1) * 2 * R] for i in order], axis=1)
 
         natural = [i_s * Z + i_z for i_z in range(Z) for i_s in range(S)]
         back = [natural.index(i) for i in range(S * Z)]
@@ -250,38 +266,45 @@
         mine, got = plane_scatter(
             dot("tf,df->td", dhidden[0], wup), dot("tf,df->td", dhidden[1], wup).astype(BF)
         )
-        fill_dhidden, fill_second = after((dhidden, second), got[0])
+        fill_dhidden, fill_second = after((dhidden, second), got)
         dhidden_join = join(fill_dhidden)
         up_grad = dot("td,tf->df", join(fill_second), dhidden_join).astype(BF)
-        mine, got = after((mine, got), up_grad)
+        up_mm = up_grad
         up_grad = lax.psum_scatter(after(up_grad, down_weight_grad), "z", scatter_dimension=0, tiled=True)
         dsecond = lane_blocks(add_up(mine, got), back)
+        active = after(active, up_mm)
+        result = dot("tf,fd->td", active[0], wdown) + swap_core(dot("tf,fd->td", active[1], wdown).astype(BF)).astype(F32)
+        dsecond = after(dsecond, down_weight_grad, result)
         dmiddle = dyf + norm_back(xhat2, inv2, g2 * dsecond)
         dbranch = (dmiddle * keep).astype(BF)
-        dbranch_all = after(plane_gather(dbranch), down_weight_grad)
+        dbranch_all = plane_gather(dbranch)
+        wo_grad = dot("td,te->de", heads[0], dbranch_all[0]) + dot("td,te->de", heads[1], dbranch_all[1])
+        wo_grad = wo_grad.astype(BF).reshape(half, 2, R, D)
+        keep_part = lax.dynamic_index_in_dim(wo_grad, c, 1, False)
+        got_part = swap_core(lax.dynamic_index_in_dim(wo_grad, 1 - c, 1, False))
+        result = after(result, dbranch_all[0])
+        result = add_up(rows(result, 0, t), [xor_seq(rows(result, q, t).astype(BF), q) for q in range(1, S)])
         dqkv = [None, None]
         for e in both:
             dheads = dot("te,de->td", dbranch_all[e], wo).astype(BF)
             dqkv[e] = attend_call(attend_back_kernel, heads_own, 3 * cols, 5, q_info[e], k_info[e], qkv_out[e], dheads)
-        dqkv_join = join(dqkv)
+        dqkv_join = after(join(dqkv), result)
         qkv_grad = dot("td,te->de", join(normed), dqkv_join).astype(BF)
-        dqkv, late = after((dqkv, (dbranch_all, heads, active)), qkv_grad)
-        qkv_grad = exchange(qkv_grad.reshape(n, R, 3 * cols), ("z", "seq", "core")).reshape(Z, tp, R, 3 * cols)
+        wo_grad = jnp.where(c == 0, join([keep_part, got_part]), join([got_part, keep_part]))
+        mixed = jnp.concatenate([after(qkv_grad, up_grad), wo_grad.reshape(D, -1)], axis=1)
+        dqkv = after(dqkv, mixed)
+        mixed = lax.psum_scatter(after(mixed, up_grad), "z", scatter_dimension=0, tiled=True)
+        mixed_sum = mixed
+        qkv_grad = exchange(mixed[:, : 3 * cols].reshape(tp, R, 3 * cols), ("seq", "core"))
+        output_weight_grad = mixed[:, 3 * cols :].reshape(R, D).astype(F32)
         mine, got = plane_scatter(dot("te,de->td", dqkv[0], wqkv), dot("te,de->td", dqkv[1], wqkv).astype(BF))
-        dbranch_late, heads, active = after(late, got[0])
-        wo_grad = dot("td,te->de", join(heads), join(dbranch_late)).astype(BF).reshape(half, 2, R, D)
-        keep_part = lax.dynamic_index_in_dim(wo_grad, c, 1, False)
-        got_part = swap_core(lax.dynamic_index_in_dim(wo_grad, 1 - c, 1, False))
-        wo_grad = jnp.where(c == 0, join([keep_part, got_part]), join([got_part, keep_part]))
-        output_weight_grad = spread_scatter(wo_grad, "z", Z, z)
-        result = [dot("tf,fd->td", active[0], wdown), dot("tf,fd->td", active[1], wdown).astype(BF)]
-        mine, got = after((mine, got), result)
+        up_grad = exchange(up_grad.reshape(tp, R, Z * RF), ("seq", "core"))
+        mine, got = after((mine, got), up_grad)
         dnormed = lane_blocks(add_up(mine, got), back)
         input_grad = dmiddle + norm_back(xhat1, inv1, g1 * dnormed)
-        block_output = (middle + add_up(*plane_scatter(*result)) + db).astype(BF)
-        up_grad = after(up_grad, block_output, output_weight_grad).reshape(S, 2, R, Z * RF)
-        up_grad = swap_blocks(swap_blocks(up_grad, 1, "core", 2, c), 0, "seq", S, s)
-        up_weight_grad = up_grad.reshape(S, 2, R, Z, RF).transpose(2, 0, 3, 1, 4).reshape(R, -1).astype(F32)
+        block_output = (middle + result + db).astype(BF)
+        up_grad = after(up_grad, mixed_sum)
+        up_weight_grad = finish_up(up_grad.reshape(tp, R, Z * RF), S, Z)
         down_weight_grad = down_weight_grad.astype(F32)
         query_grad, key_grad, value_grad = finish_qkv(qkv_grad)
 

time: 630 us -> 571 us (0.906)
  waiting for transfers between devices: 310 us -> 268 us
  local copies, waits for them, and re-layouts: 74.5 us -> 48.2 us
  starting transfers between devices: 75.5 us -> 59.6 us
  other arithmetic: 30.7 us -> 40.7 us
  Pallas kernels: 22.5 us -> 30.2 us
  matrix products: 96.3 us -> 103 us
    ppermute x52 -> x45, waiting for transfers between devices: 232 us -> 170 us  [flip(): return lax.ppermute(v, axis, [(i, i ^ q) for i in range(size)])]
    ppermute x52 -> x45, starting transfers between devices: 61.4 us -> 41.8 us  [flip(): return lax.ppermute(v, axis, [(i, i ^ q) for i in range(size)])]
    unnamed x210 -> x139, local copies, waits for them, and re-layouts: 34.1 us -> 20.2 us
    all_to_all x3 -> x4, waiting for transfers between devices: 27.6 us -> 40.2 us  [exchange(): return lax.all_to_all(v, axes, split_axis=0, concat_axis=0, tiled=True)]
    pallas_call x1 -> x6, Pallas kernels: 5.73 us -> 13.5 us  [the longest x4 8.54 us: lane_blocks(): pl.pallas_call(functools.partial(reorder_kernel, order), out_shape=jax.Sh...]
    convert_element_type x3 -> x1, local copies, waits for them, and re-layouts: 8.02 us -> 0.88 us  [body(): output_weight_grad = mixed[:, 3 * cols:].reshape(R, D).astype(F32)]
    dot_general x20 -> x21, matrix products: 96.3 us -> 103 us  [dot(): return jnp.einsum(form, left, right, preferred_element_type=F32)]
    all_gather x1, waiting for transfers between devices: 1.1 us -> 7.43 us  [body(): wo = lax.all_gather(output_weight, 'z', axis=0)]
  transfers between devices with their start and end apart: 61 -> 56, of which waited for: 27 -> 33; matrix products, arithmetic and copies ran while one was open for 23% -> 31% of each run, Pallas kernels for 2% -> 5%
where the time goes in v4:
time: 571 us; the launch traced here: 565 us
  waiting for transfers between devices  268 us (47%)
  matrix products  103 us (18%)
  starting transfers between devices  59.6 us (10%)
  local copies, waits for them, and re-layouts  48.2 us (8%)
  other arithmetic  40.7 us (7%)
  Pallas kernels  30.2 us (5%)
  between operations  15.3 us (3%)
    ppermute x45, waiting for transfers between devices, flip(): return lax.ppermute(v, axis, [(i, i ^ q) for i in range(size)])  170 us
    dot_general x21, matrix products, dot(): return jnp.einsum(form, left, right, preferred_element_type=F32)  103 us
    ppermute x45, starting transfers between devices, flip(): return lax.ppermute(v, axis, [(i, i ^ q) for i in range(size)])  41.8 us
    all_to_all x4, waiting for transfers between devices, exchange(): return lax.all_to_all(v, axes, split_axis=0, concat_axis=0, tiled=True)  40.2 us
    all_gather x1, waiting for transfers between devices, body(): wup = lax.all_gather(up, 'z', axis=0, tiled=True)  21.4 us
    unnamed x139, local copies, waits for them, and re-layouts  20.2 us
    pallas_call x4, Pallas kernels, attend_call(): pl.pallas_call(functools.partial(kernel, heads), out_shape=jax.ShapeDtype...  16.7 us
    all_to_all x4, starting transfers between devices, exchange(): return lax.all_to_all(v, axes, split_axis=0, concat_axis=0, tiled=True)  16.5 us
  transfers between devices with their start and end apart: 56, of which 33 were waited for; matrix products, arithmetic and copies ran while one was open for 31% of the time, Pallas kernels for 5%

profile of v4, /device:TPU:0, one launch (start us, length us, event | category | flops | bytes accessed | tf_op | source)
XLA Modules:
  0.0 565.1 jit_solution(4838963103927530678)
XLA Ops:
  18.1 22.9 %all-to-all-done = bf16[8,64,1792]{2,1,0:T(8,128)(2,1)S(1)} async-done(((bf16[8,64,1792]{2,1,0:T(8,128)(2,1)}), bf16[8,64,1792]{2,1,0:T(8,128)(2,1)S(1)}, u32[]{:S(2)}, u32[]{:S(2)}) %all-to-all-start) | async-done | bytes 1835040 | tf_op jit(solution)/shard_map/all_to_all | solution.py:178
  42.0 7.4 %all-gather.12.cloned.1.call-done = bf16[256,2048]{1,0:T(8,128)(2,1)} async-done(((bf16[64,2048]{1,0:T(8,128)(2,1)}), bf16[256,2048]{1,0:T(8,128)(2,1)}) %all-gather.12.cloned.1.call-update) | async-done | bytes 1048592 | tf_op jit(solution)/shard_map/all_gather | solution.py:206
  56.4 7.3 %all-to-all-done.1 = bf16[32,2,384]{2,1,0:T(2,128)(2,1)S(1)} async-done(((bf16[32,2,384]{2,1,0:T(2,128)(2,1)}), bf16[32,2,384]{2,1,0:T(2,128)(2,1)S(1)}, u32[]{:S(2)}, u32[]{:S(2)}) %all-to-all-start.1) | async-done | bytes 49184 | tf_op jit(solution)/shard_map/all_to_all | solution.py:178
  71.2 12.5 %collective-permute-done.5 = bf16[128,2048]{1,0:T(8,128)(2,1)S(1)} collective-permute-done((bf16[128,2048]{1,0:T(8,128)(2,1)}, bf16[128,2048]{1,0:T(8,128)(2,1)S(1)}, u32[]{:S(2)}, u32[]{:S(2)}) %collective-permute-start.5) | collective-permute-done | bytes 524320 | tf_op jit(solution)/shard_map/ppermute | solution.py:151
  83.7 9.7 %collective-permute-done.4 = bf16[128,2048]{1,0:T(8,128)(2,1)S(1)} collective-permute-done((bf16[128,2048]{1,0:T(8,128)(2,1)}, bf16[128,2048]{1,0:T(8,128)(2,1)S(1)}, u32[]{:S(2)}, u32[]{:S(2)}) %collective-permute-start.4) | collective-permute-done | bytes 524320 | tf_op jit(solution)/shard_map/ppermute | solution.py:151
  102.3 12.2 %all-gather.6.cloned.1.call-done = bf16[2048,768]{1,0:T(8,128)(2,1)} async-done(((bf16[512,768]{1,0:T(8,128)(2,1)}), bf16[2048,768]{1,0:T(8,128)(2,1)}) %all-gather.6.cloned.1.call-update) | async-done | bytes 3145744 | tf_op jit(solution)/shard_map/all_gather | solution.py:207
  118.7 5.2 add_convert_fusion.qkv_ref
  149.1 12.2 %collective-permute-done.12 = bf16[128,2048]{1,0:T(8,128)(2,1)S(1)} collective-permute-done((bf16[128,2048]{1,0:T(8,128)(2,1)}, bf16[128,2048]{1,0:T(8,128)(2,1)S(1)}, u32[]{:S(2)}, u32[]{:S(2)}) %collective-permute-start.12) | collective-permute-done | bytes 524320 | tf_op jit(solution)/shard_map/ppermute | solution.py:151
  161.3 10.6 %collective-permute-done.11 = bf16[128,2048]{1,0:T(8,128)(2,1)S(1)} collective-permute-done((bf16[128,2048]{1,0:T(8,128)(2,1)}, bf16[128,2048]{1,0:T(8,128)(2,1)S(1)}, u32[]{:S(2)}, u32[]{:S(2)}) %collective-permute-start.11) | collective-permute-done | bytes 524320 | tf_op jit(solution)/shard_map/ppermute | solution.py:151
  174.7 21.4 %all-gather.8.cloned.1.call-done = bf16[2048,1024]{1,0:T(8,128)(2,1)} async-done(((bf16[512,1024]{1,0:T(8,128)(2,1)}), bf16[2048,1024]{1,0:T(8,128)(2,1)}) %all-gather.8.cloned.1.call-update) | async-done | bytes 4194320 | tf_op jit(solution)/shard_map/all_gather | solution.py:209
  204.7 12.5 %collective-permute-done.15 = bf16[128,2048]{1,0:T(8,128)(2,1)S(1)} collective-permute-done((bf16[128,2048]{1,0:T(8,128)(2,1)}, bf16[128,2048]{1,0:T(8,128)(2,1)S(1)}, u32[]{:S(2)}, u32[]{:S(2)}) %collective-permute-start.15) | collective-permute-done | bytes 524320 | tf_op jit(solution)/shard_map/ppermute | solution.py:151
  217.2 10.1 %collective-permute-done.14 = bf16[128,2048]{1,0:T(8,128)(2,1)S(1)} collective-permute-done((bf16[128,2048]{1,0:T(8,128)(2,1)}, bf16[128,2048]{1,0:T(8,128)(2,1)S(1)}, u32[]{:S(2)}, u32[]{:S(2)}) %collective-permute-start.14) | collective-permute-done | bytes 524320 | tf_op jit(solution)/shard_map/ppermute | solution.py:151
  234.8 10.3 %collective-permute-done.17 = bf16[128,2048]{1,0:T(8,128)(2,1)S(1)} collective-permute-done((bf16[128,2048]{1,0:T(8,128)(2,1)S(1)}, bf16[128,2048]{1,0:T(8,128)(2,1)S(1)}, u32[]{:S(2)}, u32[]{:S(2)}) %collective-permute-start.17) | collective-permute-done | bytes 524320 | tf_op jit(solution)/shard_map/ppermute | solution.py:151
  246.1 10.7 %collective-permute-done.18 = bf16[128,2048]{1,0:T(8,128)(2,1)S(1)} collective-permute-done((bf16[128,2048]{1,0:T(8,128)(2,1)S(1)}, bf16[128,2048]{1,0:T(8,128)(2,1)S(1)}, u32[]{:S(2)}, u32[]{:S(2)}) %collective-permute-start.18) | collective-permute-done | bytes 524320 | tf_op jit(solution)/shard_map/ppermute | solution.py:151
  260.8 5.3 fusion.59
  266.1 6.5 %multiply_convert_fusion = (bf16[512,1024]{1,0:T(8,128)(2,1)S(1)}, bf16[512,1024]{1,0:T(8,128)(2,1)S(1)}, f32[512,1024]{1,0:T(8,128)}) fusion(f32[1024]{0:T(1024)S(1)} %bitcast.180, f32[512,1024]{1,0:T(8,128)S(1)} %fusion.59, bf16[512,2048]{1,0:T(8,128)(2,1)} %collective-permute-done.16, bf16[2048,1024]{1,0:T(8,128)(2,1)S(1)} %copy-done.54), kind=kOutput, calls=%fused_computation.39 | convolution fusion | flops 2153775104 | bytes 12587008 | tf_op jit(solution)/shard_map/td,df->tf/dot_general | solution.py:22
  275.1 6.4 %convolution_convert_fusion = bf16[1024,2048]{1,0:T(8,128)(2,1)} fusion(bf16[1024,2048]{1,0:T(8,128)(2,1)S(1)} %constant_dynamic-update-slice_fusion.4, bf16[512,1024]{1,0:T(8,128)(2,1)S(1)} %get-tuple-element.61, bf16[512,1024]{1,0:T(8,128)(2,1)S(1)} %get-tuple-element.60), kind=kOutput, calls=%fused_computation.10 | convolution fusion | flops 4301258752 | bytes 10485760 | tf_op jit(solution)/shard_map/tf,td->fd/dot_general | solution.py:22
  282.0 6.6 %fusion.19 = bf16[512,1024]{1,0:T(8,128)(2,1)S(1)} fusion(f32[512,1024]{1,0:T(8,128)} %get-tuple-element.166, bf16[512,2048]{1,0:T(8,128)(2,1)} %collective-permute-done.20, bf16[1024,2048]{1,0:T(8,128)(2,1)} %all-gather.10.cloned.1.call-done, f32[1024]{0:T(1024)S(1)} %bitcast.181), kind=kOutput, calls=%fused_computation.32 | convolution fusion | flops 2153250816 | bytes 9441280 | tf_op jit(solution)/shard_map/td,fd->tf/dot_general | solution.py:22
  304.5 11.3 %collective-permute-done.22 = bf16[128,2048]{1,0:T(8,128)(2,1)S(1)} collective-permute-done((bf16[128,2048]{1,0:T(8,128)(2,1)S(1)}, bf16[128,2048]{1,0:T(8,128)(2,1)S(1)}, u32[]{:S(2)}, u32[]{:S(2)}) %collective-permute-start.22) | collective-permute-done | bytes 524320 | tf_op jit(solution)/shard_map/ppermute | solution.py:151
  315.7 10.8 %collective-permute-done.23 = bf16[128,2048]{1,0:T(8,128)(2,1)S(1)} collective-permute-done((bf16[128,2048]{1,0:T(8,128)(2,1)S(1)}, bf16[128,2048]{1,0:T(8,128)(2,1)S(1)}, u32[]{:S(2)}, u32[]{:S(2)}) %collective-permute-start.23) | collective-permute-done | bytes 524320 | tf_op jit(solution)/shard_map/ppermute | solution.py:151
  328.8 8.5 %fusion.4 = bf16[2048,1024]{1,0:T(8,128)(2,1)} fusion(bf16[1024,1024]{1,0:T(8,128)(2,1)S(1)} %constant_dynamic-update-slice_fusion.9, bf16[512,2048]{1,0:T(8,128)(2,1)} %collective-permute-done.16, bf16[512,2048]{1,0:T(8,128)(2,1)} %pad_maximum_fusion.1), kind=kOutput, calls=%fused_computation.9 | convolution fusion | flops 4305453056 | bytes 10485760 | tf_op jit(solution)/shard_map/td,tf->df/dot_general | solution.py:22
  337.3 6.2 %convolution_convert_fusion.2 = bf16[512,2048]{1,0:T(8,128)(2,1)} fusion(bf16[512,1024]{1,0:T(8,128)(2,1)} %copy-done.60, bf16[1024,2048]{1,0:T(8,128)(2,1)} %all-gather.10.cloned.1.call-done), kind=kOutput, calls=%fused_computation.15 | convolution fusion | flops 2148532224 | bytes 7340032 | tf_op jit(solution)/shard_map/tf,fd->td/dot_general | solution.py:22
  343.5 12.8 %reduce-scatter.4.cloned.1.call-done = bf16[256,2048]{1,0:T(8,128)(2,1)} async-done(((bf16[1024,2048]{1,0:T(8,128)(2,1)}), bf16[256,2048]{1,0:T(8,128)(2,1)}) %reduce-scatter.4.cloned.1.call-update) | async-done | bytes 1048592 | tf_op jit(solution)/shard_map/reduce_scatter | solution.py:261
  361.8 7.7 %convert_add_fusion.1 = f32[512,2048]{1,0:T(8,128)} fusion(bf16[512,2048]{1,0:T(8,128)(2,1)} %collective-permute-done.25, bf16[512,1024]{1,0:T(8,128)(2,1)} %copy-done.57, bf16[1024,2048]{1,0:T(8,128)(2,1)} %all-gather.10.cloned.1.call-done), kind=kOutput, calls=%fused_computation.6 | convolution fusion | flops 2149580800 | bytes 11534336 | tf_op jit(solution)/shard_map/tf,fd->td/dot_general | solution.py:22
  378.7 9.7 %collective-permute-done.28 = bf16[128,2048]{1,0:T(8,128)(2,1)} collective-permute-done((bf16[128,2048]{1,0:T(8,128)(2,1)}, bf16[128,2048]{1,0:T(8,128)(2,1)}, u32[]{:S(2)}, u32[]{:S(2)}) %collective-permute-start.28) | collective-permute-done | bytes 524320 | tf_op jit(solution)/shard_map/ppermute | solution.py:151
  388.4 10.0 %collective-permute-done.27 = bf16[128,2048]{1,0:T(8,128)(2,1)} collective-permute-done((bf16[128,2048]{1,0:T(8,128)(2,1)}, bf16[128,2048]{1,0:T(8,128)(2,1)}, u32[]{:S(2)}, u32[]{:S(2)}) %collective-permute-start.27) | collective-permute-done | bytes 524320 | tf_op jit(solution)/shard_map/ppermute | solution.py:151
  419.4 10.8 %collective-permute-done.30 = bf16[128,2048]{1,0:T(8,128)(2,1)S(1)} collective-permute-done((bf16[128,2048]{1,0:T(8,128)(2,1)S(1)}, bf16[128,2048]{1,0:T(8,128)(2,1)S(1)}, u32[]{:S(2)}, u32[]{:S(2)}) %collective-permute-start.30) | collective-permute-done | bytes 524320 | tf_op jit(solution)/shard_map/ppermute | solution.py:151
  445.5 7.4 %convolution_convert_fusion.1 = bf16[2048,768]{1,0:T(8,128)(2,1)} fusion(bf16[1024,2048]{1,0:T(8,128)(2,1)} %constant_dynamic-update-slice_fusion.11, bf16[1024,768]{1,0:T(8,128)(2,1)S(1)} %pad_maximum_fusion.4), kind=kOutput, calls=%fused_computation.11 | convolution fusion | flops 3222798336 | bytes 8912896 | tf_op jit(solution)/shard_map/td,te->de/dot_general | solution.py:22
  473.9 6.5 %fusion.60 = (bf16[512,2048]{1,0:T(8,128)(2,1)S(1)}, f32[512,2048]{1,0:T(8,128)}) fusion(bf16[512,2048]{1,0:T(8,128)(2,1)} %collective-permute-done.34, bf16[512,768]{1,0:T(8,128)(2,1)S(1)} %copy-done.23, bf16[2048,768]{1,0:T(8,128)(2,1)} %all-gather.6.cloned.1.call-done), kind=kOutput, calls=%fused_computation.169 | convolution fusion | flops 1613758464 | bytes 12320768 | tf_op jit(solution)/shard_map/te,de->td/dot_general | solution.py:22
  489.7 10.3 %collective-permute-done.35 = bf16[128,2048]{1,0:T(8,128)(2,1)S(1)} collective-permute-done((bf16[128,2048]{1,0:T(8,128)(2,1)}, bf16[128,2048]{1,0:T(8,128)(2,1)S(1)}, u32[]{:S(2)}, u32[]{:S(2)}) %collective-permute-start.35) | collective-permute-done | bytes 524320 | tf_op jit(solution)/shard_map/ppermute | solution.py:151
  500.2 11.7 %collective-permute-done.37 = bf16[128,2048]{1,0:T(8,128)(2,1)} collective-permute-done((bf16[128,2048]{1,0:T(8,128)(2,1)}, bf16[128,2048]{1,0:T(8,128)(2,1)}, u32[]{:S(2)}, u32[]{:S(2)}) %collective-permute-start.37) | collective-permute-done | bytes 524320 | tf_op jit(solution)/shard_map/ppermute | solution.py:151
  547.9 6.8 %all-to-all-done.3.in_ref = bf16[8,64,768]{2,1,0:T(8,128)(2,1)S(1)} async-done(((bf16[8,64,768]{2,1,0:T(8,128)(2,1)}), bf16[8,64,768]{2,1,0:T(8,128)(2,1)S(1)}, u32[]{:S(2)}, u32[]{:S(2)}) %all-to-all-start.3) | async-done | bytes 786464 | tf_op jit(solution)/shard_map/all_to_all | solution.py:178
  (367 shorter events, 229.6 us)
Async XLA Ops:
  12.0 29.0 %all-to-all-start = ((bf16[8,64,1792]{2,1,0:T(8,128)(2,1)}), bf16[8,64,1792]{2,1,0:T(8,128)(2,1)S(1)}, u32[]{:S(2)}, u32[]{:S(2)}) async-start(bf16[8,64,1792]{2,1,0:T(8,128)(2,1)} %pad_maximum_fusion.3), calls=%async_computation | async-start | bytes 3670016 | tf_op jit(solution)/shard_map/all_to_all | solution.py:178
  17.3 32.1 %all-gather.12.cloned.1.call-start = ((), (), s32[]{:S(2)}) async-start(), calls=%async_computation.13 | async-start | bytes 1310720 | tf_op jit(solution)/shard_map/all_gather | solution.py:206
  18.0 96.5 %all-gather.6.cloned.1.call-start = ((), (), s32[]{:S(2)}) async-start(), calls=%async_computation.7 | async-start | bytes 3932160 | tf_op jit(solution)/shard_map/all_gather | solution.py:207
  56.3 139.9 %all-gather.8.cloned.1.call-start = ((), (), s32[]{:S(2)}) async-start(), calls=%async_computation.8 | async-start | bytes 5242880 | tf_op jit(solution)/shard_map/all_gather | solution.py:209
  68.4 25.0 %collective-permute-start.4 = (bf16[128,2048]{1,0:T(8,128)(2,1)}, bf16[128,2048]{1,0:T(8,128)(2,1)S(1)}, u32[]{:S(2)}, u32[]{:S(2)}) collective-permute-start(bf16[128,2048]{1,0:T(8,128)(2,1)} %shard_map.314), channel_id=1, source_target_pairs={{0,16},{8,24},{16,0},{24,8},{1,17},{9,25},{17,1},{25,9},{2,18},{10... | collective-permute-start | bytes 1572872 | tf_op jit(solution)/shard_map/ppermute | solution.py:151
  69.8 23.6 %collective-permute-start.3 = (bf16[128,2048]{1,0:T(8,128)(2,1)}, bf16[128,2048]{1,0:T(8,128)(2,1)S(1)}, u32[]{:S(2)}, u32[]{:S(2)}) collective-permute-start(bf16[128,2048]{1,0:T(8,128)(2,1)} %shard_map.314), channel_id=1, source_target_pairs={{0,8},{8,0},{16,24},{24,16},{1,9},{9,1},{17,25},{25,17},{2,10},{10... | collective-permute-start | bytes 1572872 | tf_op jit(solution)/shard_map/ppermute | solution.py:151
  96.4 22.3 %collective-permute-start.8 = (bf16[512,2048]{1,0:T(8,128)(2,1)}, bf16[512,2048]{1,0:T(8,128)(2,1)}, u32[]{:S(2)}, u32[]{:S(2)}) collective-permute-start(bf16[512,2048]{1,0:T(8,128)(2,1)} %pad_maximum_fusion), channel_id=1, source_target_pairs={{0,1},{1,0},{2,3},{3,2},{4,5},{5,4},{6,7},{7,6},{8,9},{9,8},{10,11... | collective-permute-start | bytes 6291464 | tf_op jit(solution)/shard_map/ppermute | solution.py:151
  97.0 17.8 %collective-permute-start.2 = (s32[2,128]{1,0:T(2,128)}, s32[2,128]{1,0:T(2,128)}, u32[]{:S(2)}, u32[]{:S(2)}) collective-permute-start(s32[2,128]{1,0:T(2,128)} %get-tuple-element.165), channel_id=1, source_target_pairs={{0,24},{8,16},{16,8},{24,0},{1,25},{9,17},{17,9},{25,1},{2,26},{10... | collective-permute-start | bytes 3080 | tf_op jit(solution)/shard_map/ppermute | solution.py:151
  98.4 16.5 %collective-permute-start.1 = (s32[2,128]{1,0:T(2,128)}, s32[2,128]{1,0:T(2,128)}, u32[]{:S(2)}, u32[]{:S(2)}) collective-permute-start(s32[2,128]{1,0:T(2,128)} %get-tuple-element.165), channel_id=1, source_target_pairs={{0,16},{8,24},{16,0},{24,8},{1,17},{9,25},{17,1},{25,9},{2,18},{10... | collective-permute-start | bytes 3080 | tf_op jit(solution)/shard_map/ppermute | solution.py:151
  114.6 166.9 %all-gather.10.cloned.1.call-start = ((), (), s32[]{:S(2)}) async-start(), calls=%async_computation.9 | async-start | bytes 5242880 | tf_op jit(solution)/shard_map/all_gather | solution.py:210
  147.8 24.1 %collective-permute-start.11 = (bf16[128,2048]{1,0:T(8,128)(2,1)}, bf16[128,2048]{1,0:T(8,128)(2,1)S(1)}, u32[]{:S(2)}, u32[]{:S(2)}) collective-permute-start(bf16[128,2048]{1,0:T(8,128)(2,1)} %get-tuple-element.115), channel_id=1, source_target_pairs={{0,16},{8,24},{16,0},{24,8},{1,17},{9,25},{17,1},{25,9},{2,18},{10... | collective-permute-start | bytes 1572872 | tf_op jit(solution)/shard_map/ppermute | solution.py:151
  148.4 23.7 %collective-permute-start.10 = (bf16[128,2048]{1,0:T(8,128)(2,1)}, bf16[128,2048]{1,0:T(8,128)(2,1)}, u32[]{:S(2)}, u32[]{:S(2)}) collective-permute-start(bf16[128,2048]{1,0:T(8,128)(2,1)} %get-tuple-element.113), channel_id=1, source_target_pairs={{0,8},{8,0},{16,24},{24,16},{1,9},{9,1},{17,25},{25,17},{2,10},{10... | collective-permute-start | bytes 1572872 | tf_op jit(solution)/shard_map/ppermute | solution.py:151
  196.2 160.1 %reduce-scatter.4.cloned.1.call-start = ((), (), s32[]{:S(2)}) async-start(), calls=%async_computation.10 | async-start | bytes 5242880 | tf_op jit(solution)/shard_map/reduce_scatter | solution.py:261
  203.7 23.6 %collective-permute-start.14 = (bf16[128,2048]{1,0:T(8,128)(2,1)}, bf16[128,2048]{1,0:T(8,128)(2,1)S(1)}, u32[]{:S(2)}, u32[]{:S(2)}) collective-permute-start(bf16[128,2048]{1,0:T(8,128)(2,1)} %shard_map.317), channel_id=1, source_target_pairs={{0,16},{8,24},{16,0},{24,8},{1,17},{9,25},{17,1},{25,9},{2,18},{10... | collective-permute-start | bytes 1572872 | tf_op jit(solution)/shard_map/ppermute | solution.py:151
  204.2 23.1 %collective-permute-start.13 = (bf16[128,2048]{1,0:T(8,128)(2,1)}, bf16[128,2048]{1,0:T(8,128)(2,1)S(1)}, u32[]{:S(2)}, u32[]{:S(2)}) collective-permute-start(bf16[128,2048]{1,0:T(8,128)(2,1)} %shard_map.317), channel_id=1, source_target_pairs={{0,8},{8,0},{16,24},{24,16},{1,9},{9,1},{17,25},{25,17},{2,10},{10... | collective-permute-start | bytes 1572872 | tf_op jit(solution)/shard_map/ppermute | solution.py:151
  231.8 24.9 %collective-permute-start.18 = (bf16[128,2048]{1,0:T(8,128)(2,1)S(1)}, bf16[128,2048]{1,0:T(8,128)(2,1)S(1)}, u32[]{:S(2)}, u32[]{:S(2)}) collective-permute-start(bf16[128,2048]{1,0:T(8,128)(2,1)S(1)} %bitcast.162), channel_id=1, source_target_pairs={{0,16},{8,24},{16,0},{24,8},{1,17},{9,25},{17,1},{25,9},{2,18},{10... | collective-permute-start | bytes 1572872 | tf_op jit(solution)/shard_map/ppermute | solution.py:151
  232.7 33.4 %collective-permute-start.16 = (bf16[512,2048]{1,0:T(8,128)(2,1)}, bf16[512,2048]{1,0:T(8,128)(2,1)}, u32[]{:S(2)}, u32[]{:S(2)}) collective-permute-start(bf16[512,2048]{1,0:T(8,128)(2,1)} %pad_maximum_fusion.1), channel_id=1, source_target_pairs={{0,1},{1,0},{2,3},{3,2},{4,5},{5,4},{6,7},{7,6},{8,9},{9,8},{10,11... | collective-permute-start | bytes 6291464 | tf_op jit(solution)/shard_map/ppermute | solution.py:151
  232.7 25.0 %collective-permute-start.19 = (bf16[128,2048]{1,0:T(8,128)(2,1)S(1)}, bf16[128,2048]{1,0:T(8,128)(2,1)S(1)}, u32[]{:S(2)}, u32[]{:S(2)}) collective-permute-start(bf16[128,2048]{1,0:T(8,128)(2,1)S(1)} %bitcast.163), channel_id=1, source_target_pairs={{0,24},{8,16},{16,8},{24,0},{1,25},{9,17},{17,9},{25,1},{2,26},{10... | collective-permute-start | bytes 1572872 | tf_op jit(solution)/shard_map/ppermute | solution.py:151
  281.5 172.9 %reduce-scatter.6.cloned.1.call-start = ((), (), s32[]{:S(2)}) async-start(), calls=%async_computation.11 | async-start | bytes 5242880 | tf_op jit(solution)/shard_map/reduce_scatter | solution.py:273
  301.3 25.2 %collective-permute-start.23 = (bf16[128,2048]{1,0:T(8,128)(2,1)S(1)}, bf16[128,2048]{1,0:T(8,128)(2,1)S(1)}, u32[]{:S(2)}, u32[]{:S(2)}) collective-permute-start(bf16[128,2048]{1,0:T(8,128)(2,1)S(1)} %get-tuple-element.111), channel_id=1, source_target_pairs={{0,16},{8,24},{16,0},{24,8},{1,17},{9,25},{17,1},{25,9},{2,18},{10... | collective-permute-start | bytes 1572872 | tf_op jit(solution)/shard_map/ppermute | solution.py:151
  302.7 24.5 %collective-permute-start.24 = (bf16[128,2048]{1,0:T(8,128)(2,1)S(1)}, bf16[128,2048]{1,0:T(8,128)(2,1)}, u32[]{:S(2)}, u32[]{:S(2)}) collective-permute-start(bf16[128,2048]{1,0:T(8,128)(2,1)S(1)} %get-tuple-element.110), channel_id=1, source_target_pairs={{0,24},{8,16},{16,8},{24,0},{1,25},{9,17},{17,9},{25,1},{2,26},{10... | collective-permute-start | bytes 1572872 | tf_op jit(solution)/shard_map/ppermute | solution.py:151
  343.5 18.3 %collective-permute-start.25 = (bf16[512,2048]{1,0:T(8,128)(2,1)}, bf16[512,2048]{1,0:T(8,128)(2,1)}, u32[]{:S(2)}, u32[]{:S(2)}) collective-permute-start(bf16[512,2048]{1,0:T(8,128)(2,1)} %convolution_convert_fusion.2), channel_id=1, source_target_pairs={{0,1},{1,0},{2,3},{3,2},{4,5},{5,4},{6,7},{7,6},{8,9},{9,8},{10,11... | collective-permute-start | bytes 6291464 | tf_op jit(solution)/shard_map/ppermute | solution.py:151
  356.3 180.1 %reduce-scatter.8.cloned.1.call-start = ((), (), s32[]{:S(2)}) async-start(), calls=%async_computation.12 | async-start | bytes 5242880 | tf_op jit(solution)/shard_map/reduce_scatter | solution.py:296
  374.7 23.8 %collective-permute-start.27 = (bf16[128,2048]{1,0:T(8,128)(2,1)}, bf16[128,2048]{1,0:T(8,128)(2,1)}, u32[]{:S(2)}, u32[]{:S(2)}) collective-permute-start(bf16[128,2048]{1,0:T(8,128)(2,1)} %get-tuple-element.92), channel_id=1, source_target_pairs={{0,16},{8,24},{16,0},{24,8},{1,17},{9,25},{17,1},{25,9},{2,18},{10... | collective-permute-start | bytes 1572872 | tf_op jit(solution)/shard_map/ppermute | solution.py:151
  375.2 23.3 %collective-permute-start.26 = (bf16[128,2048]{1,0:T(8,128)(2,1)}, bf16[128,2048]{1,0:T(8,128)(2,1)}, u32[]{:S(2)}, u32[]{:S(2)}) collective-permute-start(bf16[128,2048]{1,0:T(8,128)(2,1)} %get-tuple-element.92), channel_id=1, source_target_pairs={{0,8},{8,0},{16,24},{24,16},{1,9},{9,1},{17,25},{25,17},{2,10},{10... | collective-permute-start | bytes 1572872 | tf_op jit(solution)/shard_map/ppermute | solution.py:151
  400.5 32.1 %collective-permute-start.32 = (bf16[512,2048]{1,0:T(8,128)(2,1)S(1)}, bf16[512,2048]{1,0:T(8,128)(2,1)}, u32[]{:S(2)}, u32[]{:S(2)}) collective-permute-start(bf16[512,2048]{1,0:T(8,128)(2,1)S(1)} %pad_maximum_fusion.2), channel_id=1, source_target_pairs={{0,1},{1,0},{2,3},{3,2},{4,5},{5,4},{6,7},{7,6},{8,9},{9,8},{10,11... | collective-permute-start | bytes 6291464 | tf_op jit(solution)/shard_map/ppermute | solution.py:151
  405.2 25.0 %collective-permute-start.30 = (bf16[128,2048]{1,0:T(8,128)(2,1)S(1)}, bf16[128,2048]{1,0:T(8,128)(2,1)S(1)}, u32[]{:S(2)}, u32[]{:S(2)}) collective-permute-start(bf16[128,2048]{1,0:T(8,128)(2,1)S(1)} %get-tuple-element.109), channel_id=1, source_target_pairs={{0,16},{8,24},{16,0},{24,8},{1,17},{9,25},{17,1},{25,9},{2,18},{10... | collective-permute-start | bytes 1572872 | tf_op jit(solution)/shard_map/ppermute | solution.py:151
  406.4 23.8 %collective-permute-start.29 = (bf16[128,2048]{1,0:T(8,128)(2,1)S(1)}, bf16[128,2048]{1,0:T(8,128)(2,1)S(1)}, u32[]{:S(2)}, u32[]{:S(2)}) collective-permute-start(bf16[128,2048]{1,0:T(8,128)(2,1)S(1)} %get-tuple-element.107), channel_id=1, source_target_pairs={{0,8},{8,0},{16,24},{24,16},{1,9},{9,1},{17,25},{25,17},{2,10},{10... | collective-permute-start | bytes 1572872 | tf_op jit(solution)/shard_map/ppermute | solution.py:151
  470.3 19.4 %all-to-all-start.2 = ((bf16[8,64,1024]{2,1,0:T(8,128)(2,1)}), bf16[8,64,1024]{2,1,0:T(8,128)(2,1)S(1)}, u32[]{:S(2)}, u32[]{:S(2)}) async-start(bf16[8,64,1024]{2,1,0:T(8,128)(2,1)} %bitcast.165), calls=%async_computation.4 | async-start | bytes 2097152 | tf_op jit(solution)/shard_map/all_to_all | solution.py:178
  481.6 18.5 %collective-permute-start.35 = (bf16[128,2048]{1,0:T(8,128)(2,1)}, bf16[128,2048]{1,0:T(8,128)(2,1)S(1)}, u32[]{:S(2)}, u32[]{:S(2)}) collective-permute-start(bf16[128,2048]{1,0:T(8,128)(2,1)} %get-tuple-element.106), channel_id=1, source_target_pairs={{0,8},{8,0},{16,24},{24,16},{1,9},{9,1},{17,25},{25,17},{2,10},{10... | collective-permute-start | bytes 1572872 | tf_op jit(solution)/shard_map/ppermute | solution.py:151
  483.4 16.7 %collective-permute-start.36 = (bf16[128,2048]{1,0:T(8,128)(2,1)}, bf16[128,2048]{1,0:T(8,128)(2,1)}, u32[]{:S(2)}, u32[]{:S(2)}) collective-permute-start(bf16[128,2048]{1,0:T(8,128)(2,1)} %get-tuple-element.105), channel_id=1, source_target_pairs={{0,16},{8,24},{16,0},{24,8},{1,17},{9,25},{17,1},{25,9},{2,18},{10... | collective-permute-start | bytes 1572872 | tf_op jit(solution)/shard_map/ppermute | solution.py:151
  484.9 26.9 %collective-permute-start.37 = (bf16[128,2048]{1,0:T(8,128)(2,1)}, bf16[128,2048]{1,0:T(8,128)(2,1)}, u32[]{:S(2)}, u32[]{:S(2)}) collective-permute-start(bf16[128,2048]{1,0:T(8,128)(2,1)} %get-tuple-element.104), channel_id=1, source_target_pairs={{0,24},{8,16},{16,8},{24,0},{1,25},{9,17},{17,9},{25,1},{2,26},{10... | collective-permute-start | bytes 1572872 | tf_op jit(solution)/shard_map/ppermute | solution.py:151
  (85 other events, 1040.4 us)
Sparse Core Ops, SparseCore 0:
  19.7 29.6 all-gather.11
  51.5 62.9 all-gather.5
  116.7 79.3 all-gather.7
  197.6 79.2 all-gather.9
  281.6 74.6 reduce-scatter.3
  358.5 77.2 reduce-scatter.5
  459.6 76.7 reduce-scatter.7

commit v5 on v4

--- a/solution.py
+++ b/solution.py
@@ -202,10 +202,20 @@
 
         pieces = [w.reshape(R, tp, cols).transpose(1, 0, 2) for w in (query_weight, key_weight, value_weight)]
         up = up_weight.reshape(R, S, Z, 2, RF).transpose(1, 3, 0, 2, 4).reshape(tp, R, Z * RF)
-        mixed = exchange(jnp.concatenate(pieces + [up], axis=2), ("seq", "core")).reshape(tp * R, -1)
+        qkv = exchange(jnp.concatenate(pieces, axis=2), ("seq", "core")).reshape(tp * R, 3 * cols)
+        small = jnp.concatenate(
+            [first_gain, first_shift, query_bias, value_bias, output_bias, second_gain, second_shift, down_bias, up_bias]
+        )
+        small = exchange(jnp.broadcast_to(after(small, qkv)[None], (n, small.shape[0])), every)
+        small_there = small
+        small = small.astype(F32)
+        g1, b1, qb, vb, ob, g2, b2, db = [small[:, i * R : (i + 1) * R].reshape(-1) for i in range(8)]
+        ub = small[:, 8 * R :].reshape(S, Z, 2, RF)
+
         wo = lax.all_gather(output_weight, "z", axis=0)
-        wqkv = lax.all_gather(after(mixed[:, : 3 * cols], wo), "z", axis=0, tiled=True)
-        wqkv, up = after((wqkv, mixed[:, 3 * cols :]))
+        wqkv = lax.all_gather(after(qkv, wo), "z", axis=0, tiled=True)
+        up = exchange(after(up, small_there), ("seq", "core")).reshape(tp * R, Z * RF)
+        wqkv, up = after((wqkv, up))
         wup = lax.all_gather(up, "z", axis=0, tiled=True)
         wdown = lax.all_gather(after(down_weight, wup), "z", axis=0, tiled=True)
         keep_part = lax.dynamic_slice_in_dim(wo, c * half, half, axis=0)
@@ -215,14 +225,6 @@
             jnp.stack([keep_part, got_part], axis=1),
             jnp.stack([got_part, keep_part], axis=1),
         ).reshape(cols, D)
-
-        small = jnp.concatenate(
-            [first_gain, first_shift, query_bias, value_bias, output_bias, second_gain, second_shift, down_bias, up_bias]
-        )
-        small = exchange(jnp.broadcast_to(after(small, mixed)[None], (n, small.shape[0])), every)
-        small = small.astype(F32)
-        g1, b1, qb, vb, ob, g2, b2, db = [small[:, i * R : (i + 1) * R].reshape(-1) for i in range(8)]
-        ub = small[:, 8 * R :].reshape(S, Z, 2, RF)
 
         codes = jnp.stack([segment_ids[0], pad_mask[0]])
         codes = jnp.stack([codes] + [xor_seq(codes, q) for q in range(1, S)], axis=1)
@@ -272,28 +274,28 @@
         up_mm = up_grad
         up_grad = lax.psum_scatter(after(up_grad, down_weight_grad), "z", scatter_dimension=0, tiled=True)
         dsecond = lane_blocks(add_up(mine, got), back)
-        active = after(active, up_mm)
-        result = dot("tf,fd->td", active[0], wdown) + swap_core(dot("tf,fd->td", active[1], wdown).astype(BF)).astype(F32)
-        dsecond = after(dsecond, down_weight_grad, result)
+        dsecond = after(dsecond, down_weight_grad, up_mm)
         dmiddle = dyf + norm_back(xhat2, inv2, g2 * dsecond)
         dbranch = (dmiddle * keep).astype(BF)
         dbranch_all = plane_gather(dbranch)
+        active = after(active, dbranch)
+        result = dot("tf,fd->td", active[0], wdown) + swap_core(dot("tf,fd->td", active[1], wdown).astype(BF)).astype(F32)
         wo_grad = dot("td,te->de", heads[0], dbranch_all[0]) + dot("td,te->de", heads[1], dbranch_all[1])
         wo_grad = wo_grad.astype(BF).reshape(half, 2, R, D)
         keep_part = lax.dynamic_index_in_dim(wo_grad, c, 1, False)
         got_part = swap_core(lax.dynamic_index_in_dim(wo_grad, 1 - c, 1, False))
-        result = after(result, dbranch_all[0])
-        result = add_up(rows(result, 0, t), [xor_seq(rows(result, q, t).astype(BF), q) for q in range(1, S)])
+        result, dbranch_all = after((result, dbranch_all))
+        result_got = [xor_seq(rows(result, q, t).astype(BF), q) for q in range(1, S)]
         dqkv = [None, None]
         for e in both:
             dheads = dot("te,de->td", dbranch_all[e], wo).astype(BF)
             dqkv[e] = attend_call(attend_back_kernel, heads_own, 3 * cols, 5, q_info[e], k_info[e], qkv_out[e], dheads)
-        dqkv_join = after(join(dqkv), result)
-        qkv_grad = dot("td,te->de", join(normed), dqkv_join).astype(BF)
+        qkv_grad = (dot("td,te->de", normed[0], dqkv[0]) + dot("td,te->de", normed[1], dqkv[1])).astype(BF)
         wo_grad = jnp.where(c == 0, join([keep_part, got_part]), join([got_part, keep_part]))
-        mixed = jnp.concatenate([after(qkv_grad, up_grad), wo_grad.reshape(D, -1)], axis=1)
+        result = add_up(rows(result, 0, t), after(result_got, qkv_grad))
+        mixed = jnp.concatenate([qkv_grad, wo_grad.reshape(D, -1)], axis=1)
         dqkv = after(dqkv, mixed)
-        mixed = lax.psum_scatter(after(mixed, up_grad), "z", scatter_dimension=0, tiled=True)
+        mixed = lax.psum_scatter(after(mixed, up_grad, result_got), "z", scatter_dimension=0, tiled=True)
         mixed_sum = mixed
         qkv_grad = exchange(mixed[:, : 3 * cols].reshape(tp, R, 3 * cols), ("seq", "core"))
         output_weight_grad = mixed[:, 3 * cols :].reshape(R, D).astype(F32)
@@ -308,7 +310,7 @@
         down_weight_grad = down_weight_grad.astype(F32)
         query_grad, key_grad, value_grad = finish_qkv(qkv_grad)
 
-        bias = jnp.sum(dqkv_join.astype(F32), axis=0).reshape(3, cols)
+        bias = sum(jnp.sum(v.astype(F32), axis=0) for v in dqkv).reshape(3, cols)
         spread = jnp.zeros((2, tp, cols), F32)
         spread = lax.dynamic_update_slice(spread, jnp.stack([bias[0], bias[2]])[:, None], (0, s * 2 + c, 0))
         wide = jnp.zeros((S, Z, 2, RF), F32)

time: 571 us -> 547 us (0.958)
  waiting for transfers between devices: 268 us -> 233 us
  blocking collectives: 0 us -> 17.8 us
  local copies, waits for them, and re-layouts: 48.2 us -> 37.8 us
    all_to_all x4, waiting for transfers between devices: 40.2 us -> 15.3 us  [exchange(): return lax.all_to_all(v, axes, split_axis=0, concat_axis=0, tiled=True)]
    all_to_all x0 -> x1, blocking collectives: none -> 17.8 us  [exchange(): return lax.all_to_all(v, axes, split_axis=0, concat_axis=0, tiled=True)]
    ppermute x45, waiting for transfers between devices: 170 us -> 155 us  [flip(): return lax.ppermute(v, axis, [(i, i ^ q) for i in range(size)])]
    reduce_scatter x1, waiting for transfers between devices: 12.8 us -> 19.5 us  [body(): lax.psum_scatter(down_grad, 'z', scatter_dimension=0, tiled=True)]
    unnamed x139 -> x120, local copies, waits for them, and re-layouts: 20.2 us -> 14.5 us
    dot_general x21 -> x22, matrix products: 103 us -> 103 us  [dot(): return jnp.einsum(form, left, right, preferred_element_type=F32)]
  transfers between devices with their start and end apart: 56 -> 56, of which waited for: 33 -> 25; matrix products, arithmetic and copies ran while one was open for 31% -> 32% of each run, Pallas kernels for 5% -> 5%
where the time goes in v5:
time: 547 us; the launch traced here: 541 us
  waiting for transfers between devices  233 us (43%)
  matrix products  103 us (19%)
  starting transfers between devices  61.3 us (11%)
  other arithmetic  42.1 us (8%)
  local copies, waits for them, and re-layouts  37.8 us (7%)
  Pallas kernels  30.5 us (6%)
  blocking collectives  17.8 us (3%)
  between operations  15.5 us (3%)
    ppermute x45, waiting for transfers between devices, flip(): return lax.ppermute(v, axis, [(i, i ^ q) for i in range(size)])  155 us
    dot_general x22, matrix products, dot(): return jnp.einsum(form, left, right, preferred_element_type=F32)  103 us
    ppermute x45, starting transfers between devices, flip(): return lax.ppermute(v, axis, [(i, i ^ q) for i in range(size)])  44.5 us
    all_gather x1, waiting for transfers between devices, body(): wup = lax.all_gather(up, 'z', axis=0, tiled=True)  21.6 us
    reduce_scatter x1, waiting for transfers between devices, body(): lax.psum_scatter(down_grad, 'z', scatter_dimension=0, tiled=True)  19.5 us
    all_to_all x1, blocking collectives, exchange(): return lax.all_to_all(v, axes, split_axis=0, concat_axis=0, tiled=True)  17.8 us
    pallas_call x4, Pallas kernels, attend_call(): pl.pallas_call(functools.partial(kernel, heads), out_shape=jax.ShapeDtype...  17 us
    all_to_all x4, starting transfers between devices, exchange(): return lax.all_to_all(v, axes, split_axis=0, concat_axis=0, tiled=True)  15.5 us
  transfers between devices with their start and end apart: 56, of which 25 were waited for; matrix products, arithmetic and copies ran while one was open for 32% of the time, Pallas kernels for 5%

profile of v5, /device:TPU:0, one launch (start us, length us, event | category | flops | bytes accessed | tf_op | source)
XLA Modules:
  0.0 541.5 jit_solution(4257697305750851080)
XLA Ops:
  11.3 17.8 %all_to_all.29 = bf16[8,64,768]{2,1,0:T(8,128)(2,1)} all-to-all(bf16[8,64,768]{2,1,0:T(8,128)(2,1)S(1)} %copy.54), channel_id=1, replica_groups=mesh['seq'=4,'z'=4,'core'=2] {'seq','core'}, dimensions={0} | all-to-all | bytes 1572864 | tf_op jit(solution)/shard_map/all_to_all | solution.py:178
  29.1 11.2 %all-gather.12.cloned.1.call-done = bf16[256,2048]{1,0:T(8,128)(2,1)} async-done(((bf16[64,2048]{1,0:T(8,128)(2,1)}), bf16[256,2048]{1,0:T(8,128)(2,1)}) %all-gather.12.cloned.1.call-update) | async-done | bytes 1048592 | tf_op jit(solution)/shard_map/all_gather | solution.py:215
  47.2 7.3 %all-to-all-done.1 = bf16[32,2,384]{2,1,0:T(2,128)(2,1)S(1)} async-done(((bf16[32,2,384]{2,1,0:T(2,128)(2,1)}), bf16[32,2,384]{2,1,0:T(2,128)(2,1)S(1)}, u32[]{:S(2)}, u32[]{:S(2)}) %all-to-all-start.1) | async-done | bytes 49184 | tf_op jit(solution)/shard_map/all_to_all | solution.py:178
  67.8 5.2 collective-permute-done.3
  73.0 11.7 %collective-permute-done.4 = bf16[128,2048]{1,0:T(8,128)(2,1)} collective-permute-done((bf16[128,2048]{1,0:T(8,128)(2,1)}, bf16[128,2048]{1,0:T(8,128)(2,1)}, u32[]{:S(2)}, u32[]{:S(2)}) %collective-permute-start.4) | collective-permute-done | bytes 524320 | tf_op jit(solution)/shard_map/ppermute | solution.py:151
  94.6 10.2 %all-gather.6.cloned.1.call-done = bf16[2048,768]{1,0:T(8,128)(2,1)} async-done(((bf16[512,768]{1,0:T(8,128)(2,1)}), bf16[2048,768]{1,0:T(8,128)(2,1)}) %all-gather.6.cloned.1.call-update) | async-done | bytes 3145744 | tf_op jit(solution)/shard_map/all_gather | solution.py:216
  108.6 5.2 add_convert_fusion.1.qkv_ref
  121.5 5.1 add_convert_fusion.2.qkv_ref
  139.4 11.3 %collective-permute-done.10 = bf16[128,2048]{1,0:T(8,128)(2,1)S(1)} collective-permute-done((bf16[128,2048]{1,0:T(8,128)(2,1)}, bf16[128,2048]{1,0:T(8,128)(2,1)S(1)}, u32[]{:S(2)}, u32[]{:S(2)}) %collective-permute-start.10) | collective-permute-done | bytes 524320 | tf_op jit(solution)/shard_map/ppermute | solution.py:151
  150.7 11.7 %collective-permute-done.11 = bf16[128,2048]{1,0:T(8,128)(2,1)S(1)} collective-permute-done((bf16[128,2048]{1,0:T(8,128)(2,1)}, bf16[128,2048]{1,0:T(8,128)(2,1)S(1)}, u32[]{:S(2)}, u32[]{:S(2)}) %collective-permute-start.11) | collective-permute-done | bytes 524320 | tf_op jit(solution)/shard_map/ppermute | solution.py:151
  164.8 21.6 %all-gather.8.cloned.1.call-done = bf16[2048,1024]{1,0:T(8,128)(2,1)} async-done(((bf16[512,1024]{1,0:T(8,128)(2,1)}), bf16[2048,1024]{1,0:T(8,128)(2,1)}) %all-gather.8.cloned.1.call-update) | async-done | bytes 4194320 | tf_op jit(solution)/shard_map/all_gather | solution.py:219
  195.0 11.5 %collective-permute-done.13 = bf16[128,2048]{1,0:T(8,128)(2,1)S(1)} collective-permute-done((bf16[128,2048]{1,0:T(8,128)(2,1)}, bf16[128,2048]{1,0:T(8,128)(2,1)S(1)}, u32[]{:S(2)}, u32[]{:S(2)}) %collective-permute-start.13) | collective-permute-done | bytes 524320 | tf_op jit(solution)/shard_map/ppermute | solution.py:151
  206.6 11.3 %collective-permute-done.14 = bf16[128,2048]{1,0:T(8,128)(2,1)S(1)} collective-permute-done((bf16[128,2048]{1,0:T(8,128)(2,1)}, bf16[128,2048]{1,0:T(8,128)(2,1)S(1)}, u32[]{:S(2)}, u32[]{:S(2)}) %collective-permute-start.14) | collective-permute-done | bytes 524320 | tf_op jit(solution)/shard_map/ppermute | solution.py:151
  225.4 10.4 %collective-permute-done.17 = bf16[128,2048]{1,0:T(8,128)(2,1)S(1)} collective-permute-done((bf16[128,2048]{1,0:T(8,128)(2,1)S(1)}, bf16[128,2048]{1,0:T(8,128)(2,1)S(1)}, u32[]{:S(2)}, u32[]{:S(2)}) %collective-permute-start.17) | collective-permute-done | bytes 524320 | tf_op jit(solution)/shard_map/ppermute | solution.py:151
  236.7 9.0 %collective-permute-done.18 = bf16[128,2048]{1,0:T(8,128)(2,1)S(1)} collective-permute-done((bf16[128,2048]{1,0:T(8,128)(2,1)S(1)}, bf16[128,2048]{1,0:T(8,128)(2,1)S(1)}, u32[]{:S(2)}, u32[]{:S(2)}) %collective-permute-start.18) | collective-permute-done | bytes 524320 | tf_op jit(solution)/shard_map/ppermute | solution.py:151
  249.6 5.3 fusion.59
  255.0 6.5 %multiply_convert_fusion = (bf16[512,1024]{1,0:T(8,128)(2,1)S(1)}, bf16[512,1024]{1,0:T(8,128)(2,1)S(1)}, f32[512,1024]{1,0:T(8,128)}) fusion(f32[1024]{0:T(1024)S(1)} %bitcast.181, f32[512,1024]{1,0:T(8,128)S(1)} %fusion.59, bf16[512,2048]{1,0:T(8,128)(2,1)} %collective-permute-done.16, bf16[2048,1024]{1,0:T(8,128)(2,1)S(1)} %copy-done.45), kind=kOutput, calls=%fused_computation.39 | convolution fusion | flops 2153775104 | bytes 12587008 | tf_op jit(solution)/shard_map/td,df->tf/dot_general | solution.py:22
  264.0 6.3 %convolution_convert_fusion = bf16[1024,2048]{1,0:T(8,128)(2,1)} fusion(bf16[1024,2048]{1,0:T(8,128)(2,1)S(1)} %constant_dynamic-update-slice_fusion.4, bf16[512,1024]{1,0:T(8,128)(2,1)S(1)} %get-tuple-element.68, bf16[512,1024]{1,0:T(8,128)(2,1)S(1)} %get-tuple-element.67), kind=kOutput, calls=%fused_computation.12 | convolution fusion | flops 4301258752 | bytes 10485760 | tf_op jit(solution)/shard_map/tf,td->fd/dot_general | solution.py:22
  270.8 6.5 %fusion.19 = bf16[512,1024]{1,0:T(8,128)(2,1)S(1)} fusion(f32[512,1024]{1,0:T(8,128)} %get-tuple-element.172, bf16[512,2048]{1,0:T(8,128)(2,1)} %collective-permute-done.20, bf16[1024,2048]{1,0:T(8,128)(2,1)} %all-gather.10.cloned.1.call-done, f32[1024]{0:T(1024)S(1)} %bitcast.182), kind=kOutput, calls=%fused_computation.32 | convolution fusion | flops 2153250816 | bytes 9441280 | tf_op jit(solution)/shard_map/td,fd->tf/dot_general | solution.py:22
  293.0 11.3 %collective-permute-done.22 = bf16[128,2048]{1,0:T(8,128)(2,1)S(1)} collective-permute-done((bf16[128,2048]{1,0:T(8,128)(2,1)S(1)}, bf16[128,2048]{1,0:T(8,128)(2,1)S(1)}, u32[]{:S(2)}, u32[]{:S(2)}) %collective-permute-start.22) | collective-permute-done | bytes 524320 | tf_op jit(solution)/shard_map/ppermute | solution.py:151
  304.2 11.0 %collective-permute-done.23 = bf16[128,2048]{1,0:T(8,128)(2,1)S(1)} collective-permute-done((bf16[128,2048]{1,0:T(8,128)(2,1)S(1)}, bf16[128,2048]{1,0:T(8,128)(2,1)S(1)}, u32[]{:S(2)}, u32[]{:S(2)}) %collective-permute-start.23) | collective-permute-done | bytes 524320 | tf_op jit(solution)/shard_map/ppermute | solution.py:151
  317.5 8.5 %fusion.4 = bf16[2048,1024]{1,0:T(8,128)(2,1)} fusion(bf16[1024,1024]{1,0:T(8,128)(2,1)S(1)} %constant_dynamic-update-slice_fusion.9, bf16[512,2048]{1,0:T(8,128)(2,1)} %collective-permute-done.16, bf16[512,2048]{1,0:T(8,128)(2,1)} %pad_maximum_fusion.2), kind=kOutput, calls=%fused_computation.11 | convolution fusion | flops 4305453056 | bytes 10485760 | tf_op jit(solution)/shard_map/td,tf->df/dot_general | solution.py:22
  326.0 19.5 %reduce-scatter.4.cloned.1.call-done = bf16[256,2048]{1,0:T(8,128)(2,1)} async-done(((bf16[1024,2048]{1,0:T(8,128)(2,1)}), bf16[256,2048]{1,0:T(8,128)(2,1)}) %reduce-scatter.4.cloned.1.call-update) | async-done | bytes 1048592 | tf_op jit(solution)/shard_map/reduce_scatter | solution.py:263
  361.8 7.6 %collective-permute-done.26 = bf16[128,2048]{1,0:T(8,128)(2,1)S(1)} collective-permute-done((bf16[128,2048]{1,0:T(8,128)(2,1)S(1)}, bf16[128,2048]{1,0:T(8,128)(2,1)S(1)}, u32[]{:S(2)}, u32[]{:S(2)}) %collective-permute-start.26) | collective-permute-done | bytes 524320 | tf_op jit(solution)/shard_map/ppermute | solution.py:151
  369.4 11.3 %collective-permute-done.27 = bf16[128,2048]{1,0:T(8,128)(2,1)S(1)} collective-permute-done((bf16[128,2048]{1,0:T(8,128)(2,1)S(1)}, bf16[128,2048]{1,0:T(8,128)(2,1)S(1)}, u32[]{:S(2)}, u32[]{:S(2)}) %collective-permute-start.27) | collective-permute-done | bytes 524320 | tf_op jit(solution)/shard_map/ppermute | solution.py:151
  382.4 5.6 %convert_add_fusion.1 = f32[512,2048]{1,0:T(8,128)S(1)} fusion(bf16[512,2048]{1,0:T(8,128)(2,1)} %collective-permute-done.25, bf16[512,1024]{1,0:T(8,128)(2,1)} %copy-done.49, bf16[1024,2048]{1,0:T(8,128)(2,1)} %all-gather.10.cloned.1.call-done), kind=kOutput, calls=%fused_computation.8 | convolution fusion | flops 2149580800 | bytes 11534336 | tf_op jit(solution)/shard_map/tf,fd->td/dot_general | solution.py:22
  418.1 5.1 add_convert_fusion
  431.8 5.0 convolution_convert_fusion.4
  441.6 7.3 %fusion.60 = (bf16[512,2048]{1,0:T(8,128)(2,1)}, f32[512,2048]{1,0:T(8,128)}) fusion(bf16[512,2048]{1,0:T(8,128)(2,1)} %collective-permute-done.34, bf16[512,768]{1,0:T(8,128)(2,1)} %shard_map.319, bf16[2048,768]{1,0:T(8,128)(2,1)} %all-gather.6.cloned.1.call-done), kind=kOutput, calls=%fused_computation.162 | convolution fusion | flops 1613758464 | bytes 12320768 | tf_op jit(solution)/shard_map/te,de->td/dot_general | solution.py:22
  461.9 17.0 %collective-permute-done.35 = bf16[128,2048]{1,0:T(8,128)(2,1)S(1)} collective-permute-done((bf16[128,2048]{1,0:T(8,128)(2,1)S(1)}, bf16[128,2048]{1,0:T(8,128)(2,1)S(1)}, u32[]{:S(2)}, u32[]{:S(2)}) %collective-permute-start.35) | collective-permute-done | bytes 524320 | tf_op jit(solution)/shard_map/ppermute | solution.py:151
  479.7 11.0 %collective-permute-done.37 = bf16[128,2048]{1,0:T(8,128)(2,1)} collective-permute-done((bf16[128,2048]{1,0:T(8,128)(2,1)S(1)}, bf16[128,2048]{1,0:T(8,128)(2,1)}, u32[]{:S(2)}, u32[]{:S(2)}) %collective-permute-start.37) | collective-permute-done | bytes 524320 | tf_op jit(solution)/shard_map/ppermute | solution.py:151
  523.6 7.6 %all-to-all-done.4.in_ref = bf16[8,64,768]{2,1,0:T(8,128)(2,1)S(1)} async-done(((bf16[8,64,768]{2,1,0:T(8,128)(2,1)}), bf16[8,64,768]{2,1,0:T(8,128)(2,1)S(1)}, u32[]{:S(2)}, u32[]{:S(2)}) %all-to-all-start.4) | async-done | bytes 786464 | tf_op jit(solution)/shard_map/all_to_all | solution.py:178
  (350 shorter events, 213.1 us)
Async XLA Ops:
  7.2 33.1 %all-gather.12.cloned.1.call-start = ((), (), s32[]{:S(2)}) async-start(), calls=%async_computation.14 | async-start | bytes 1310720 | tf_op jit(solution)/shard_map/all_gather | solution.py:215
  7.9 96.9 %all-gather.6.cloned.1.call-start = ((), (), s32[]{:S(2)}) async-start(), calls=%async_computation.8 | async-start | bytes 3932160 | tf_op jit(solution)/shard_map/all_gather | solution.py:216
  58.5 26.2 %collective-permute-start.4 = (bf16[128,2048]{1,0:T(8,128)(2,1)}, bf16[128,2048]{1,0:T(8,128)(2,1)}, u32[]{:S(2)}, u32[]{:S(2)}) collective-permute-start(bf16[128,2048]{1,0:T(8,128)(2,1)} %shard_map.314), channel_id=1, source_target_pairs={{0,16},{8,24},{16,0},{24,8},{1,17},{9,25},{17,1},{25,9},{2,18},{10... | collective-permute-start | bytes 1572872 | tf_op jit(solution)/shard_map/ppermute | solution.py:151
  59.2 25.5 %collective-permute-start.5 = (bf16[128,2048]{1,0:T(8,128)(2,1)}, bf16[128,2048]{1,0:T(8,128)(2,1)}, u32[]{:S(2)}, u32[]{:S(2)}) collective-permute-start(bf16[128,2048]{1,0:T(8,128)(2,1)} %shard_map.314), channel_id=1, source_target_pairs={{0,24},{8,16},{16,8},{24,0},{1,25},{9,17},{17,9},{25,1},{2,26},{10... | collective-permute-start | bytes 1572872 | tf_op jit(solution)/shard_map/ppermute | solution.py:151
  64.1 30.5 %all-to-all-start.2 = ((bf16[8,64,1024]{2,1,0:T(8,128)(2,1)}), bf16[8,64,1024]{2,1,0:T(8,128)(2,1)S(1)}, u32[]{:S(2)}, u32[]{:S(2)}) async-start(bf16[8,64,1024]{2,1,0:T(8,128)(2,1)} %reshape.284), calls=%async_computation.2 | async-start | bytes 2097152 | tf_op jit(solution)/shard_map/all_to_all | solution.py:178
  67.7 118.7 %all-gather.8.cloned.1.call-start = ((), (), s32[]{:S(2)}) async-start(), calls=%async_computation.9 | async-start | bytes 5242880 | tf_op jit(solution)/shard_map/all_gather | solution.py:219
  87.6 20.9 %collective-permute-start.8 = (bf16[512,2048]{1,0:T(8,128)(2,1)}, bf16[512,2048]{1,0:T(8,128)(2,1)}, u32[]{:S(2)}, u32[]{:S(2)}) collective-permute-start(bf16[512,2048]{1,0:T(8,128)(2,1)} %pad_maximum_fusion.1), channel_id=1, source_target_pairs={{0,1},{1,0},{2,3},{3,2},{4,5},{5,4},{6,7},{7,6},{8,9},{9,8},{10,11... | collective-permute-start | bytes 6291464 | tf_op jit(solution)/shard_map/ppermute | solution.py:151
  87.7 17.4 %collective-permute-start = (s32[2,128]{1,0:T(2,128)S(1)}, s32[2,128]{1,0:T(2,128)S(1)}, u32[]{:S(2)}, u32[]{:S(2)}) collective-permute-start(s32[2,128]{1,0:T(2,128)S(1)} %get-tuple-element.171), channel_id=1, source_target_pairs={{0,8},{8,0},{16,24},{24,16},{1,9},{9,1},{17,25},{25,17},{2,10},{10... | collective-permute-start | bytes 3080 | tf_op jit(solution)/shard_map/ppermute | solution.py:151
  104.9 165.4 %all-gather.10.cloned.1.call-start = ((), (), s32[]{:S(2)}) async-start(), calls=%async_computation.10 | async-start | bytes 5242880 | tf_op jit(solution)/shard_map/all_gather | solution.py:220
  137.2 25.2 %collective-permute-start.11 = (bf16[128,2048]{1,0:T(8,128)(2,1)}, bf16[128,2048]{1,0:T(8,128)(2,1)S(1)}, u32[]{:S(2)}, u32[]{:S(2)}) collective-permute-start(bf16[128,2048]{1,0:T(8,128)(2,1)} %get-tuple-element.121), channel_id=1, source_target_pairs={{0,16},{8,24},{16,0},{24,8},{1,17},{9,25},{17,1},{25,9},{2,18},{10... | collective-permute-start | bytes 1572872 | tf_op jit(solution)/shard_map/ppermute | solution.py:151
  138.7 23.7 %collective-permute-start.12 = (bf16[128,2048]{1,0:T(8,128)(2,1)}, bf16[128,2048]{1,0:T(8,128)(2,1)S(1)}, u32[]{:S(2)}, u32[]{:S(2)}) collective-permute-start(bf16[128,2048]{1,0:T(8,128)(2,1)} %get-tuple-element.120), channel_id=1, source_target_pairs={{0,24},{8,16},{16,8},{24,0},{1,25},{9,17},{17,9},{25,1},{2,26},{10... | collective-permute-start | bytes 1572872 | tf_op jit(solution)/shard_map/ppermute | solution.py:151
  186.5 159.0 %reduce-scatter.4.cloned.1.call-start = ((), (), s32[]{:S(2)}) async-start(), calls=%async_computation.11 | async-start | bytes 5242880 | tf_op jit(solution)/shard_map/reduce_scatter | solution.py:263
  193.1 24.8 %collective-permute-start.14 = (bf16[128,2048]{1,0:T(8,128)(2,1)}, bf16[128,2048]{1,0:T(8,128)(2,1)S(1)}, u32[]{:S(2)}, u32[]{:S(2)}) collective-permute-start(bf16[128,2048]{1,0:T(8,128)(2,1)} %shard_map.317), channel_id=1, source_target_pairs={{0,16},{8,24},{16,0},{24,8},{1,17},{9,25},{17,1},{25,9},{2,18},{10... | collective-permute-start | bytes 1572872 | tf_op jit(solution)/shard_map/ppermute | solution.py:151
  194.5 23.3 %collective-permute-start.15 = (bf16[128,2048]{1,0:T(8,128)(2,1)}, bf16[128,2048]{1,0:T(8,128)(2,1)S(1)}, u32[]{:S(2)}, u32[]{:S(2)}) collective-permute-start(bf16[128,2048]{1,0:T(8,128)(2,1)} %shard_map.317), channel_id=1, source_target_pairs={{0,24},{8,16},{16,8},{24,0},{1,25},{9,17},{17,9},{25,1},{2,26},{10... | collective-permute-start | bytes 1572872 | tf_op jit(solution)/shard_map/ppermute | solution.py:151
  221.9 23.8 %collective-permute-start.18 = (bf16[128,2048]{1,0:T(8,128)(2,1)S(1)}, bf16[128,2048]{1,0:T(8,128)(2,1)S(1)}, u32[]{:S(2)}, u32[]{:S(2)}) collective-permute-start(bf16[128,2048]{1,0:T(8,128)(2,1)S(1)} %bitcast.162), channel_id=1, source_target_pairs={{0,16},{8,24},{16,0},{24,8},{1,17},{9,25},{17,1},{25,9},{2,18},{10... | collective-permute-start | bytes 1572872 | tf_op jit(solution)/shard_map/ppermute | solution.py:151
  223.0 23.7 %collective-permute-start.19 = (bf16[128,2048]{1,0:T(8,128)(2,1)S(1)}, bf16[128,2048]{1,0:T(8,128)(2,1)S(1)}, u32[]{:S(2)}, u32[]{:S(2)}) collective-permute-start(bf16[128,2048]{1,0:T(8,128)(2,1)S(1)} %bitcast.163), channel_id=1, source_target_pairs={{0,24},{8,16},{16,8},{24,0},{1,25},{9,17},{17,9},{25,1},{2,26},{10... | collective-permute-start | bytes 1572872 | tf_op jit(solution)/shard_map/ppermute | solution.py:151
  224.4 30.5 %collective-permute-start.16 = (bf16[512,2048]{1,0:T(8,128)(2,1)}, bf16[512,2048]{1,0:T(8,128)(2,1)}, u32[]{:S(2)}, u32[]{:S(2)}) collective-permute-start(bf16[512,2048]{1,0:T(8,128)(2,1)} %pad_maximum_fusion.2), channel_id=1, source_target_pairs={{0,1},{1,0},{2,3},{3,2},{4,5},{5,4},{6,7},{7,6},{8,9},{9,8},{10,11... | collective-permute-start | bytes 6291464 | tf_op jit(solution)/shard_map/ppermute | solution.py:151
  270.3 160.4 %reduce-scatter.6.cloned.1.call-start = ((), (), s32[]{:S(2)}) async-start(), calls=%async_computation.12 | async-start | bytes 5242880 | tf_op jit(solution)/shard_map/reduce_scatter | solution.py:275
  290.1 25.1 %collective-permute-start.23 = (bf16[128,2048]{1,0:T(8,128)(2,1)S(1)}, bf16[128,2048]{1,0:T(8,128)(2,1)S(1)}, u32[]{:S(2)}, u32[]{:S(2)}) collective-permute-start(bf16[128,2048]{1,0:T(8,128)(2,1)S(1)} %get-tuple-element.118), channel_id=1, source_target_pairs={{0,16},{8,24},{16,0},{24,8},{1,17},{9,25},{17,1},{25,9},{2,18},{10... | collective-permute-start | bytes 1572872 | tf_op jit(solution)/shard_map/ppermute | solution.py:151
  290.4 25.6 %collective-permute-start.24 = (bf16[128,2048]{1,0:T(8,128)(2,1)S(1)}, bf16[128,2048]{1,0:T(8,128)(2,1)}, u32[]{:S(2)}, u32[]{:S(2)}) collective-permute-start(bf16[128,2048]{1,0:T(8,128)(2,1)S(1)} %get-tuple-element.117), channel_id=1, source_target_pairs={{0,24},{8,16},{16,8},{24,0},{1,25},{9,17},{17,9},{25,1},{2,26},{10... | collective-permute-start | bytes 1572872 | tf_op jit(solution)/shard_map/ppermute | solution.py:151
  345.5 166.7 %reduce-scatter.8.cloned.1.call-start = ((), (), s32[]{:S(2)}) async-start(), calls=%async_computation.13 | async-start | bytes 5242880 | tf_op jit(solution)/shard_map/reduce_scatter | solution.py:298
  356.0 24.7 %collective-permute-start.27 = (bf16[128,2048]{1,0:T(8,128)(2,1)S(1)}, bf16[128,2048]{1,0:T(8,128)(2,1)S(1)}, u32[]{:S(2)}, u32[]{:S(2)}) collective-permute-start(bf16[128,2048]{1,0:T(8,128)(2,1)S(1)} %get-tuple-element.100), channel_id=1, source_target_pairs={{0,16},{8,24},{16,0},{24,8},{1,17},{9,25},{17,1},{25,9},{2,18},{10... | collective-permute-start | bytes 1572872 | tf_op jit(solution)/shard_map/ppermute | solution.py:151
  357.5 23.2 %collective-permute-start.28 = (bf16[128,2048]{1,0:T(8,128)(2,1)S(1)}, bf16[128,2048]{1,0:T(8,128)(2,1)S(1)}, u32[]{:S(2)}, u32[]{:S(2)}) collective-permute-start(bf16[128,2048]{1,0:T(8,128)(2,1)S(1)} %get-tuple-element.100), channel_id=1, source_target_pairs={{0,24},{8,16},{16,8},{24,0},{1,25},{9,17},{17,9},{25,1},{2,26},{10... | collective-permute-start | bytes 1572872 | tf_op jit(solution)/shard_map/ppermute | solution.py:151
  361.7 20.6 %collective-permute-start.25 = (bf16[512,2048]{1,0:T(8,128)(2,1)}, bf16[512,2048]{1,0:T(8,128)(2,1)}, u32[]{:S(2)}, u32[]{:S(2)}) collective-permute-start(bf16[512,2048]{1,0:T(8,128)(2,1)} %convolution_convert_fusion.1), channel_id=1, source_target_pairs={{0,1},{1,0},{2,3},{3,2},{4,5},{5,4},{6,7},{7,6},{8,9},{9,8},{10,11... | collective-permute-start | bytes 6291464 | tf_op jit(solution)/shard_map/ppermute | solution.py:151
  392.9 30.3 %collective-permute-start.33 = (bf16[2,64,2048]{2,1,0:T(8,128)(2,1)S(1)}, bf16[2,64,2048]{2,1,0:T(8,128)(2,1)S(1)}, u32[]{:S(2)}, u32[]{:S(2)}) collective-permute-start(bf16[2,64,2048]{2,1,0:T(8,128)(2,1)S(1)} %get-tuple-element.123), channel_id=1, source_target_pairs={{0,1},{1,0},{2,3},{3,2},{4,5},{5,4},{6,7},{7,6},{8,9},{9,8},{10,11... | collective-permute-start | bytes 1572872 | tf_op jit(solution)/shard_map/ppermute | solution.py:151
  394.8 35.9 %collective-permute-start.30 = (bf16[128,2048]{1,0:T(8,128)(2,1)}, bf16[128,2048]{1,0:T(8,128)(2,1)}, u32[]{:S(2)}, u32[]{:S(2)}) collective-permute-start(bf16[128,2048]{1,0:T(8,128)(2,1)} %get-tuple-element.115), channel_id=1, source_target_pairs={{0,8},{8,0},{16,24},{24,16},{1,9},{9,1},{17,25},{25,17},{2,10},{10... | collective-permute-start | bytes 1572872 | tf_op jit(solution)/shard_map/ppermute | solution.py:151
  395.9 34.7 %collective-permute-start.31 = (bf16[128,2048]{1,0:T(8,128)(2,1)}, bf16[128,2048]{1,0:T(8,128)(2,1)}, u32[]{:S(2)}, u32[]{:S(2)}) collective-permute-start(bf16[128,2048]{1,0:T(8,128)(2,1)} %get-tuple-element.114), channel_id=1, source_target_pairs={{0,16},{8,24},{16,0},{24,8},{1,17},{9,25},{17,1},{25,9},{2,18},{10... | collective-permute-start | bytes 1572872 | tf_op jit(solution)/shard_map/ppermute | solution.py:151
  396.9 33.7 %collective-permute-start.32 = (bf16[128,2048]{1,0:T(8,128)(2,1)S(1)}, bf16[128,2048]{1,0:T(8,128)(2,1)}, u32[]{:S(2)}, u32[]{:S(2)}) collective-permute-start(bf16[128,2048]{1,0:T(8,128)(2,1)S(1)} %get-tuple-element.113), channel_id=1, source_target_pairs={{0,24},{8,16},{16,8},{24,0},{1,25},{9,17},{17,9},{25,1},{2,26},{10... | collective-permute-start | bytes 1572872 | tf_op jit(solution)/shard_map/ppermute | solution.py:151
  448.9 41.8 %all-to-all-start.3 = ((bf16[8,64,1024]{2,1,0:T(8,128)(2,1)}), bf16[8,64,1024]{2,1,0:T(8,128)(2,1)S(1)}, u32[]{:S(2)}, u32[]{:S(2)}) async-start(bf16[8,64,1024]{2,1,0:T(8,128)(2,1)} %bitcast.165), calls=%async_computation.5 | async-start | bytes 2097152 | tf_op jit(solution)/shard_map/all_to_all | solution.py:178
  454.2 24.7 %collective-permute-start.35 = (bf16[128,2048]{1,0:T(8,128)(2,1)S(1)}, bf16[128,2048]{1,0:T(8,128)(2,1)S(1)}, u32[]{:S(2)}, u32[]{:S(2)}) collective-permute-start(bf16[128,2048]{1,0:T(8,128)(2,1)S(1)} %get-tuple-element.112), channel_id=1, source_target_pairs={{0,8},{8,0},{16,24},{24,16},{1,9},{9,1},{17,25},{25,17},{2,10},{10... | collective-permute-start | bytes 1572872 | tf_op jit(solution)/shard_map/ppermute | solution.py:151
  456.2 22.6 %collective-permute-start.36 = (bf16[128,2048]{1,0:T(8,128)(2,1)S(1)}, bf16[128,2048]{1,0:T(8,128)(2,1)S(1)}, u32[]{:S(2)}, u32[]{:S(2)}) collective-permute-start(bf16[128,2048]{1,0:T(8,128)(2,1)S(1)} %get-tuple-element.111), channel_id=1, source_target_pairs={{0,16},{8,24},{16,0},{24,8},{1,17},{9,25},{17,1},{25,9},{2,18},{10... | collective-permute-start | bytes 1572872 | tf_op jit(solution)/shard_map/ppermute | solution.py:151
  457.7 33.0 %collective-permute-start.37 = (bf16[128,2048]{1,0:T(8,128)(2,1)S(1)}, bf16[128,2048]{1,0:T(8,128)(2,1)}, u32[]{:S(2)}, u32[]{:S(2)}) collective-permute-start(bf16[128,2048]{1,0:T(8,128)(2,1)S(1)} %get-tuple-element.110), channel_id=1, source_target_pairs={{0,24},{8,16},{16,8},{24,0},{1,25},{9,17},{17,9},{25,1},{2,26},{10... | collective-permute-start | bytes 1572872 | tf_op jit(solution)/shard_map/ppermute | solution.py:151
  (79 other events, 868.6 us)
Sparse Core Ops, SparseCore 0:
  9.6 30.6 all-gather.11
  41.8 62.9 all-gather.5
  107.0 79.4 all-gather.7
  187.9 79.2 all-gather.9
  270.4 75.0 reduce-scatter.3
  347.8 77.2 reduce-scatter.5
  430.9 76.4 reduce-scatter.7

commit v6 on v5

--- a/solution.py
+++ b/solution.py
@@ -258,9 +258,11 @@
             phi = 0.5 * (1.0 + lax.erf(hidden * math.sqrt(0.5)))
             slope[e] = phi + hidden * jnp.exp(-0.5 * hidden * hidden) * (1.0 / math.sqrt(2 * math.pi))
             active[e] = (hidden * phi).astype(BF)
-        down_grad = dot("tf,td->fd", join(active), join(dy_all)).astype(BF)
+        early = D - D // 4
+        active_join, dy_join = join(active), join(dy_all)
+        down_grad = dot("tf,td->fd", active_join, dy_join[:, :early]).astype(BF)
         down_grad, wdown = after((down_grad, wdown))
-        down_weight_grad = lax.psum_scatter(down_grad, "z", scatter_dimension=0, tiled=True)
+        down_early = lax.psum_scatter(down_grad, "z", scatter_dimension=0, tiled=True)
         dhidden = [None, None]
         for e in (1, 0):
             dhidden[e] = (dot("td,fd->tf", dy_all[e], wdown) * slope[e]).astype(BF)
@@ -272,9 +274,11 @@
         dhidden_join = join(fill_dhidden)
         up_grad = dot("td,tf->df", join(fill_second), dhidden_join).astype(BF)
         up_mm = up_grad
-        up_grad = lax.psum_scatter(after(up_grad, down_weight_grad), "z", scatter_dimension=0, tiled=True)
+        active_join, dy_join = after((active_join, dy_join), up_mm)
+        down_rest = dot("tf,td->fd", active_join, dy_join[:, early:]).astype(BF)
+        up_grad = lax.psum_scatter(after(up_grad, down_early), "z", scatter_dimension=0, tiled=True)
         dsecond = lane_blocks(add_up(mine, got), back)
-        dsecond = after(dsecond, down_weight_grad, up_mm)
+        dsecond = after(dsecond, down_early, up_mm, down_rest)
         dmiddle = dyf + norm_back(xhat2, inv2, g2 * dsecond)
         dbranch = (dmiddle * keep).astype(BF)
         dbranch_all = plane_gather(dbranch)
@@ -307,7 +311,8 @@
         block_output = (middle + result + db).astype(BF)
         up_grad = after(up_grad, mixed_sum)
         up_weight_grad = finish_up(up_grad.reshape(tp, R, Z * RF), S, Z)
-        down_weight_grad = down_weight_grad.astype(F32)
+        down_rest = lax.psum_scatter(after(down_rest, mixed_sum), "z", scatter_dimension=0, tiled=True)
+        down_weight_grad = jnp.concatenate([down_early, down_rest], axis=1).astype(F32)
         query_grad, key_grad, value_grad = finish_qkv(qkv_grad)
 
         bias = sum(jnp.sum(v.astype(F32), axis=0) for v in dqkv).reshape(3, cols)

time: 547 us -> 540 us (0.987)
  waiting for transfers between devices: 233 us -> 221 us
    reduce_scatter x1, waiting for transfers between devices: 19.5 us -> 0.01 us  [body(): lax.psum_scatter(down_grad, 'z', scatter_dimension=0, tiled=True)]
    reduce_scatter x1, waiting for transfers between devices: 0.01 us -> 8.03 us  [body(): lax.psum_scatter(after(mixed, up_grad, result_got), 'z', scatter_dimensio...]
    dot_general x22 -> x23, matrix products: 103 us -> 106 us  [dot(): return jnp.einsum(form, left, right, preferred_element_type=F32)]
    unnamed x120 -> x136, local copies, waits for them, and re-layouts: 14.5 us -> 16.9 us
  transfers between devices with their start and end apart: 56 -> 57, of which waited for: 25 -> 25; matrix products, arithmetic and copies ran while one was open for 32% -> 33% of each run, Pallas kernels for 5% -> 6%
where the time goes in v6:
time: 540 us; the launch traced here: 535 us
  waiting for transfers between devices  221 us (41%)
  matrix products  106 us (20%)
  starting transfers between devices  61.1 us (11%)
  other arithmetic  43.2 us (8%)
  local copies, waits for them, and re-layouts  39.1 us (7%)
  Pallas kernels  30.2 us (6%)
  blocking collectives  17.8 us (3%)
  between operations  15.6 us (3%)
    ppermute x45, waiting for transfers between devices, flip(): return lax.ppermute(v, axis, [(i, i ^ q) for i in range(size)])  154 us
    dot_general x23, matrix products, dot(): return jnp.einsum(form, left, right, preferred_element_type=F32)  106 us
    ppermute x45, starting transfers between devices, flip(): return lax.ppermute(v, axis, [(i, i ^ q) for i in range(size)])  44.7 us
    all_gather x1, waiting for transfers between devices, body(): wup = lax.all_gather(up, 'z', axis=0, tiled=True)  21.6 us
    all_to_all x1, blocking collectives, exchange(): return lax.all_to_all(v, axes, split_axis=0, concat_axis=0, tiled=True)  17.8 us
    unnamed x136, local copies, waits for them, and re-layouts  16.9 us
    pallas_call x4, Pallas kernels, attend_call(): pl.pallas_call(functools.partial(kernel, heads), out_shape=jax.ShapeDtype...  16.7 us
    all_to_all x4, waiting for transfers between devices, exchange(): return lax.all_to_all(v, axes, split_axis=0, concat_axis=0, tiled=True)  15.2 us
  transfers between devices with their start and end apart: 57, of which 25 were waited for; matrix products, arithmetic and copies ran while one was open for 33% of the time, Pallas kernels for 6%

profile of v6, /device:TPU:0, one launch (start us, length us, event | category | flops | bytes accessed | tf_op | source)
XLA Modules:
  0.0 534.9 jit_solution(8210263166526517016)
XLA Ops:
  11.3 17.8 %all_to_all.29 = bf16[8,64,768]{2,1,0:T(8,128)(2,1)} all-to-all(bf16[8,64,768]{2,1,0:T(8,128)(2,1)S(1)} %copy.54), channel_id=1, replica_groups=mesh['seq'=4,'z'=4,'core'=2] {'seq','core'}, dimensions={0} | all-to-all | bytes 1572864 | tf_op jit(solution)/shard_map/all_to_all | solution.py:178
  29.1 11.2 %all-gather.12.cloned.1.call-done = bf16[256,2048]{1,0:T(8,128)(2,1)} async-done(((bf16[64,2048]{1,0:T(8,128)(2,1)}), bf16[256,2048]{1,0:T(8,128)(2,1)}) %all-gather.12.cloned.1.call-update) | async-done | bytes 1048592 | tf_op jit(solution)/shard_map/all_gather | solution.py:215
  47.2 7.3 %all-to-all-done.1 = bf16[32,2,384]{2,1,0:T(2,128)(2,1)S(1)} async-done(((bf16[32,2,384]{2,1,0:T(2,128)(2,1)}), bf16[32,2,384]{2,1,0:T(2,128)(2,1)S(1)}, u32[]{:S(2)}, u32[]{:S(2)}) %all-to-all-start.1) | async-done | bytes 49184 | tf_op jit(solution)/shard_map/all_to_all | solution.py:178
  67.8 5.2 collective-permute-done.3
  73.0 11.7 %collective-permute-done.4 = bf16[128,2048]{1,0:T(8,128)(2,1)} collective-permute-done((bf16[128,2048]{1,0:T(8,128)(2,1)}, bf16[128,2048]{1,0:T(8,128)(2,1)}, u32[]{:S(2)}, u32[]{:S(2)}) %collective-permute-start.4) | collective-permute-done | bytes 524320 | tf_op jit(solution)/shard_map/ppermute | solution.py:151
  94.6 10.2 %all-gather.6.cloned.1.call-done = bf16[2048,768]{1,0:T(8,128)(2,1)} async-done(((bf16[512,768]{1,0:T(8,128)(2,1)}), bf16[2048,768]{1,0:T(8,128)(2,1)}) %all-gather.6.cloned.1.call-update) | async-done | bytes 3145744 | tf_op jit(solution)/shard_map/all_gather | solution.py:216
  108.5 5.2 add_convert_fusion.1.qkv_ref
  121.6 5.1 add_convert_fusion.2.qkv_ref
  139.5 11.3 %collective-permute-done.10 = bf16[128,2048]{1,0:T(8,128)(2,1)S(1)} collective-permute-done((bf16[128,2048]{1,0:T(8,128)(2,1)}, bf16[128,2048]{1,0:T(8,128)(2,1)S(1)}, u32[]{:S(2)}, u32[]{:S(2)}) %collective-permute-start.10) | collective-permute-done | bytes 524320 | tf_op jit(solution)/shard_map/ppermute | solution.py:151
  150.8 11.6 %collective-permute-done.11 = bf16[128,2048]{1,0:T(8,128)(2,1)S(1)} collective-permute-done((bf16[128,2048]{1,0:T(8,128)(2,1)}, bf16[128,2048]{1,0:T(8,128)(2,1)S(1)}, u32[]{:S(2)}, u32[]{:S(2)}) %collective-permute-start.11) | collective-permute-done | bytes 524320 | tf_op jit(solution)/shard_map/ppermute | solution.py:151
  164.9 21.6 %all-gather.8.cloned.1.call-done = bf16[2048,1024]{1,0:T(8,128)(2,1)} async-done(((bf16[512,1024]{1,0:T(8,128)(2,1)}), bf16[2048,1024]{1,0:T(8,128)(2,1)}) %all-gather.8.cloned.1.call-update) | async-done | bytes 4194320 | tf_op jit(solution)/shard_map/all_gather | solution.py:219
  195.1 11.5 %collective-permute-done.13 = bf16[128,2048]{1,0:T(8,128)(2,1)S(1)} collective-permute-done((bf16[128,2048]{1,0:T(8,128)(2,1)}, bf16[128,2048]{1,0:T(8,128)(2,1)S(1)}, u32[]{:S(2)}, u32[]{:S(2)}) %collective-permute-start.13) | collective-permute-done | bytes 524320 | tf_op jit(solution)/shard_map/ppermute | solution.py:151
  206.6 11.3 %collective-permute-done.14 = bf16[128,2048]{1,0:T(8,128)(2,1)S(1)} collective-permute-done((bf16[128,2048]{1,0:T(8,128)(2,1)}, bf16[128,2048]{1,0:T(8,128)(2,1)S(1)}, u32[]{:S(2)}, u32[]{:S(2)}) %collective-permute-start.14) | collective-permute-done | bytes 524320 | tf_op jit(solution)/shard_map/ppermute | solution.py:151
  225.4 10.4 %collective-permute-done.17 = bf16[128,2048]{1,0:T(8,128)(2,1)S(1)} collective-permute-done((bf16[128,2048]{1,0:T(8,128)(2,1)S(1)}, bf16[128,2048]{1,0:T(8,128)(2,1)S(1)}, u32[]{:S(2)}, u32[]{:S(2)}) %collective-permute-start.17) | collective-permute-done | bytes 524320 | tf_op jit(solution)/shard_map/ppermute | solution.py:151
  236.8 9.0 %collective-permute-done.18 = bf16[128,2048]{1,0:T(8,128)(2,1)S(1)} collective-permute-done((bf16[128,2048]{1,0:T(8,128)(2,1)S(1)}, bf16[128,2048]{1,0:T(8,128)(2,1)S(1)}, u32[]{:S(2)}, u32[]{:S(2)}) %collective-permute-start.18) | collective-permute-done | bytes 524320 | tf_op jit(solution)/shard_map/ppermute | solution.py:151
  249.8 5.3 fusion.57
  255.2 6.5 %multiply_convert_fusion = (bf16[512,1024]{1,0:T(8,128)(2,1)S(1)}, bf16[512,1024]{1,0:T(8,128)(2,1)S(1)}, f32[512,1024]{1,0:T(8,128)}) fusion(f32[1024]{0:T(1024)S(1)} %bitcast.181, f32[512,1024]{1,0:T(8,128)S(1)} %fusion.57, bf16[512,2048]{1,0:T(8,128)(2,1)} %collective-permute-done.16, bf16[2048,1024]{1,0:T(8,128)(2,1)S(1)} %copy-done.56), kind=kOutput, calls=%fused_computation.38 | convolution fusion | flops 2153775104 | bytes 12587008 | tf_op jit(solution)/shard_map/td,df->tf/dot_general | solution.py:22
  266.4 5.1 convolution_convert_fusion
  271.9 6.5 %fusion.20 = bf16[512,1024]{1,0:T(8,128)(2,1)S(1)} fusion(f32[512,1024]{1,0:T(8,128)} %get-tuple-element.178, bf16[512,2048]{1,0:T(8,128)(2,1)} %collective-permute-done.20, bf16[1024,2048]{1,0:T(8,128)(2,1)} %all-gather.10.cloned.1.call-done, f32[1024]{0:T(1024)S(1)} %bitcast.182), kind=kOutput, calls=%fused_computation.33 | convolution fusion | flops 2153250816 | bytes 9441280 | tf_op jit(solution)/shard_map/td,fd->tf/dot_general | solution.py:22
  295.7 9.7 %collective-permute-done.22 = bf16[128,2048]{1,0:T(8,128)(2,1)S(1)} collective-permute-done((bf16[128,2048]{1,0:T(8,128)(2,1)S(1)}, bf16[128,2048]{1,0:T(8,128)(2,1)S(1)}, u32[]{:S(2)}, u32[]{:S(2)}) %collective-permute-start.22) | collective-permute-done | bytes 524320 | tf_op jit(solution)/shard_map/ppermute | solution.py:151
  305.4 11.0 %collective-permute-done.23 = bf16[128,2048]{1,0:T(8,128)(2,1)S(1)} collective-permute-done((bf16[128,2048]{1,0:T(8,128)(2,1)S(1)}, bf16[128,2048]{1,0:T(8,128)(2,1)S(1)}, u32[]{:S(2)}, u32[]{:S(2)}) %collective-permute-start.23) | collective-permute-done | bytes 524320 | tf_op jit(solution)/shard_map/ppermute | solution.py:151
  318.8 8.5 %fusion.4 = bf16[2048,1024]{1,0:T(8,128)(2,1)} fusion(bf16[1024,1024]{1,0:T(8,128)(2,1)S(1)} %constant_dynamic-update-slice_fusion.9, bf16[512,2048]{1,0:T(8,128)(2,1)} %collective-permute-done.16, bf16[512,2048]{1,0:T(8,128)(2,1)} %pad_maximum_fusion.2), kind=kOutput, calls=%fused_computation.11 | convolution fusion | flops 4305453056 | bytes 10485760 | tf_op jit(solution)/shard_map/td,tf->df/dot_general | solution.py:22
  347.7 7.7 %collective-permute-done.26 = bf16[128,2048]{1,0:T(8,128)(2,1)S(1)} collective-permute-done((bf16[128,2048]{1,0:T(8,128)(2,1)S(1)}, bf16[128,2048]{1,0:T(8,128)(2,1)S(1)}, u32[]{:S(2)}, u32[]{:S(2)}) %collective-permute-start.26) | collective-permute-done | bytes 524320 | tf_op jit(solution)/shard_map/ppermute | solution.py:151
  355.4 10.6 %collective-permute-done.27 = bf16[128,2048]{1,0:T(8,128)(2,1)S(1)} collective-permute-done((bf16[128,2048]{1,0:T(8,128)(2,1)S(1)}, bf16[128,2048]{1,0:T(8,128)(2,1)S(1)}, u32[]{:S(2)}, u32[]{:S(2)}) %collective-permute-start.27) | collective-permute-done | bytes 524320 | tf_op jit(solution)/shard_map/ppermute | solution.py:151
  367.7 5.5 %convert_add_fusion.1 = f32[512,2048]{1,0:T(8,128)S(1)} fusion(bf16[512,2048]{1,0:T(8,128)(2,1)} %collective-permute-done.25, bf16[512,1024]{1,0:T(8,128)(2,1)} %copy-done.20, bf16[1024,2048]{1,0:T(8,128)(2,1)} %all-gather.10.cloned.1.call-done), kind=kOutput, calls=%fused_computation.8 | convolution fusion | flops 2149580800 | bytes 11534336 | tf_op jit(solution)/shard_map/tf,fd->td/dot_general | solution.py:22
  403.6 5.1 add_convert_fusion
  417.3 5.0 convolution_convert_fusion.4
  426.8 7.1 %fusion.58 = (bf16[512,2048]{1,0:T(8,128)(2,1)}, f32[512,2048]{1,0:T(8,128)}) fusion(bf16[512,2048]{1,0:T(8,128)(2,1)} %collective-permute-done.34, bf16[512,768]{1,0:T(8,128)(2,1)S(1)} %copy-done.25, bf16[2048,768]{1,0:T(8,128)(2,1)} %all-gather.6.cloned.1.call-done), kind=kOutput, calls=%fused_computation.163 | convolution fusion | flops 1613758464 | bytes 12320768 | tf_op jit(solution)/shard_map/te,de->td/dot_general | solution.py:22
  447.0 16.6 %collective-permute-done.35 = bf16[128,2048]{1,0:T(8,128)(2,1)S(1)} collective-permute-done((bf16[128,2048]{1,0:T(8,128)(2,1)S(1)}, bf16[128,2048]{1,0:T(8,128)(2,1)S(1)}, u32[]{:S(2)}, u32[]{:S(2)}) %collective-permute-start.35) | collective-permute-done | bytes 524320 | tf_op jit(solution)/shard_map/ppermute | solution.py:151
  464.4 11.0 %collective-permute-done.37 = bf16[128,2048]{1,0:T(8,128)(2,1)} collective-permute-done((bf16[128,2048]{1,0:T(8,128)(2,1)S(1)}, bf16[128,2048]{1,0:T(8,128)(2,1)}, u32[]{:S(2)}, u32[]{:S(2)}) %collective-permute-start.37) | collective-permute-done | bytes 524320 | tf_op jit(solution)/shard_map/ppermute | solution.py:151
  483.0 8.0 %reduce-scatter.9.cloned.1.call-done = bf16[512,1024]{0,1:T(8,128)(2,1)} async-done(((bf16[2048,1024]{0,1:T(8,128)(2,1)}), bf16[512,1024]{0,1:T(8,128)(2,1)}) %reduce-scatter.9.cloned.1.call-update) | async-done | bytes 1048592 | tf_op jit(solution)/shard_map/reduce_scatter | solution.py:302
  514.6 7.5 %all-to-all-done.4.in_ref = bf16[8,64,768]{2,1,0:T(8,128)(2,1)S(1)} async-done(((bf16[8,64,768]{2,1,0:T(8,128)(2,1)}), bf16[8,64,768]{2,1,0:T(8,128)(2,1)S(1)}, u32[]{:S(2)}, u32[]{:S(2)}) %all-to-all-start.4) | async-done | bytes 786464 | tf_op jit(solution)/shard_map/all_to_all | solution.py:178
  (371 shorter events, 222.0 us)
Async XLA Ops:
  7.2 33.1 %all-gather.12.cloned.1.call-start = ((), (), s32[]{:S(2)}) async-start(), calls=%async_computation.16 | async-start | bytes 1310720 | tf_op jit(solution)/shard_map/all_gather | solution.py:215
  7.9 96.9 %all-gather.6.cloned.1.call-start = ((), (), s32[]{:S(2)}) async-start(), calls=%async_computation.9 | async-start | bytes 3932160 | tf_op jit(solution)/shard_map/all_gather | solution.py:216
  58.5 26.1 %collective-permute-start.4 = (bf16[128,2048]{1,0:T(8,128)(2,1)}, bf16[128,2048]{1,0:T(8,128)(2,1)}, u32[]{:S(2)}, u32[]{:S(2)}) collective-permute-start(bf16[128,2048]{1,0:T(8,128)(2,1)} %shard_map.314), channel_id=1, source_target_pairs={{0,16},{8,24},{16,0},{24,8},{1,17},{9,25},{17,1},{25,9},{2,18},{10... | collective-permute-start | bytes 1572872 | tf_op jit(solution)/shard_map/ppermute | solution.py:151
  59.2 25.5 %collective-permute-start.5 = (bf16[128,2048]{1,0:T(8,128)(2,1)}, bf16[128,2048]{1,0:T(8,128)(2,1)}, u32[]{:S(2)}, u32[]{:S(2)}) collective-permute-start(bf16[128,2048]{1,0:T(8,128)(2,1)} %shard_map.314), channel_id=1, source_target_pairs={{0,24},{8,16},{16,8},{24,0},{1,25},{9,17},{17,9},{25,1},{2,26},{10... | collective-permute-start | bytes 1572872 | tf_op jit(solution)/shard_map/ppermute | solution.py:151
  64.2 30.4 %all-to-all-start.2 = ((bf16[8,64,1024]{2,1,0:T(8,128)(2,1)}), bf16[8,64,1024]{2,1,0:T(8,128)(2,1)S(1)}, u32[]{:S(2)}, u32[]{:S(2)}) async-start(bf16[8,64,1024]{2,1,0:T(8,128)(2,1)} %reshape.284), calls=%async_computation.2 | async-start | bytes 2097152 | tf_op jit(solution)/shard_map/all_to_all | solution.py:178
  67.8 118.7 %all-gather.8.cloned.1.call-start = ((), (), s32[]{:S(2)}) async-start(), calls=%async_computation.10 | async-start | bytes 5242880 | tf_op jit(solution)/shard_map/all_gather | solution.py:219
  87.6 20.9 %collective-permute-start.8 = (bf16[512,2048]{1,0:T(8,128)(2,1)}, bf16[512,2048]{1,0:T(8,128)(2,1)}, u32[]{:S(2)}, u32[]{:S(2)}) collective-permute-start(bf16[512,2048]{1,0:T(8,128)(2,1)} %pad_maximum_fusion.1), channel_id=1, source_target_pairs={{0,1},{1,0},{2,3},{3,2},{4,5},{5,4},{6,7},{7,6},{8,9},{9,8},{10,11... | collective-permute-start | bytes 6291464 | tf_op jit(solution)/shard_map/ppermute | solution.py:151
  104.9 166.5 %all-gather.10.cloned.1.call-start = ((), (), s32[]{:S(2)}) async-start(), calls=%async_computation.11 | async-start | bytes 5242880 | tf_op jit(solution)/shard_map/all_gather | solution.py:220
  137.2 25.2 %collective-permute-start.11 = (bf16[128,2048]{1,0:T(8,128)(2,1)}, bf16[128,2048]{1,0:T(8,128)(2,1)S(1)}, u32[]{:S(2)}, u32[]{:S(2)}) collective-permute-start(bf16[128,2048]{1,0:T(8,128)(2,1)} %get-tuple-element.127), channel_id=1, source_target_pairs={{0,16},{8,24},{16,0},{24,8},{1,17},{9,25},{17,1},{25,9},{2,18},{10... | collective-permute-start | bytes 1572872 | tf_op jit(solution)/shard_map/ppermute | solution.py:151
  138.7 23.7 %collective-permute-start.12 = (bf16[128,2048]{1,0:T(8,128)(2,1)}, bf16[128,2048]{1,0:T(8,128)(2,1)S(1)}, u32[]{:S(2)}, u32[]{:S(2)}) collective-permute-start(bf16[128,2048]{1,0:T(8,128)(2,1)} %get-tuple-element.126), channel_id=1, source_target_pairs={{0,24},{8,16},{16,8},{24,0},{1,25},{9,17},{17,9},{25,1},{2,26},{10... | collective-permute-start | bytes 1572872 | tf_op jit(solution)/shard_map/ppermute | solution.py:151
  186.5 146.0 %reduce-scatter.5.cloned.1.call-start = ((), (), s32[]{:S(2)}) async-start(), calls=%async_computation.12 | async-start | bytes 3932160 | tf_op jit(solution)/shard_map/reduce_scatter | solution.py:265
  193.1 24.8 %collective-permute-start.14 = (bf16[128,2048]{1,0:T(8,128)(2,1)}, bf16[128,2048]{1,0:T(8,128)(2,1)S(1)}, u32[]{:S(2)}, u32[]{:S(2)}) collective-permute-start(bf16[128,2048]{1,0:T(8,128)(2,1)} %shard_map.317), channel_id=1, source_target_pairs={{0,16},{8,24},{16,0},{24,8},{1,17},{9,25},{17,1},{25,9},{2,18},{10... | collective-permute-start | bytes 1572872 | tf_op jit(solution)/shard_map/ppermute | solution.py:151
  194.6 23.3 %collective-permute-start.15 = (bf16[128,2048]{1,0:T(8,128)(2,1)}, bf16[128,2048]{1,0:T(8,128)(2,1)S(1)}, u32[]{:S(2)}, u32[]{:S(2)}) collective-permute-start(bf16[128,2048]{1,0:T(8,128)(2,1)} %shard_map.317), channel_id=1, source_target_pairs={{0,24},{8,16},{16,8},{24,0},{1,25},{9,17},{17,9},{25,1},{2,26},{10... | collective-permute-start | bytes 1572872 | tf_op jit(solution)/shard_map/ppermute | solution.py:151
  222.0 23.8 %collective-permute-start.18 = (bf16[128,2048]{1,0:T(8,128)(2,1)S(1)}, bf16[128,2048]{1,0:T(8,128)(2,1)S(1)}, u32[]{:S(2)}, u32[]{:S(2)}) collective-permute-start(bf16[128,2048]{1,0:T(8,128)(2,1)S(1)} %bitcast.162), channel_id=1, source_target_pairs={{0,16},{8,24},{16,0},{24,8},{1,17},{9,25},{17,1},{25,9},{2,18},{10... | collective-permute-start | bytes 1572872 | tf_op jit(solution)/shard_map/ppermute | solution.py:151
  223.0 23.7 %collective-permute-start.19 = (bf16[128,2048]{1,0:T(8,128)(2,1)S(1)}, bf16[128,2048]{1,0:T(8,128)(2,1)S(1)}, u32[]{:S(2)}, u32[]{:S(2)}) collective-permute-start(bf16[128,2048]{1,0:T(8,128)(2,1)S(1)} %bitcast.163), channel_id=1, source_target_pairs={{0,24},{8,16},{16,8},{24,0},{1,25},{9,17},{17,9},{25,1},{2,26},{10... | collective-permute-start | bytes 1572872 | tf_op jit(solution)/shard_map/ppermute | solution.py:151
  224.5 30.7 %collective-permute-start.16 = (bf16[512,2048]{1,0:T(8,128)(2,1)}, bf16[512,2048]{1,0:T(8,128)(2,1)}, u32[]{:S(2)}, u32[]{:S(2)}) collective-permute-start(bf16[512,2048]{1,0:T(8,128)(2,1)} %pad_maximum_fusion.2), channel_id=1, source_target_pairs={{0,1},{1,0},{2,3},{3,2},{4,5},{5,4},{6,7},{7,6},{8,9},{9,8},{10,11... | collective-permute-start | bytes 6291464 | tf_op jit(solution)/shard_map/ppermute | solution.py:151
  271.4 144.8 %reduce-scatter.7.cloned.1.call-start = ((), (), s32[]{:S(2)}) async-start(), calls=%async_computation.13 | async-start | bytes 5242880 | tf_op jit(solution)/shard_map/reduce_scatter | solution.py:279
  291.3 25.1 %collective-permute-start.23 = (bf16[128,2048]{1,0:T(8,128)(2,1)S(1)}, bf16[128,2048]{1,0:T(8,128)(2,1)S(1)}, u32[]{:S(2)}, u32[]{:S(2)}) collective-permute-start(bf16[128,2048]{1,0:T(8,128)(2,1)S(1)} %get-tuple-element.124), channel_id=1, source_target_pairs={{0,16},{8,24},{16,0},{24,8},{1,17},{9,25},{17,1},{25,9},{2,18},{10... | collective-permute-start | bytes 1572872 | tf_op jit(solution)/shard_map/ppermute | solution.py:151
  291.5 24.9 %collective-permute-start.24 = (bf16[128,2048]{1,0:T(8,128)(2,1)S(1)}, bf16[128,2048]{1,0:T(8,128)(2,1)S(1)}, u32[]{:S(2)}, u32[]{:S(2)}) collective-permute-start(bf16[128,2048]{1,0:T(8,128)(2,1)S(1)} %get-tuple-element.123), channel_id=1, source_target_pairs={{0,24},{8,16},{16,8},{24,0},{1,25},{9,17},{17,9},{25,1},{2,26},{10... | collective-permute-start | bytes 1572872 | tf_op jit(solution)/shard_map/ppermute | solution.py:151
  332.6 158.4 %reduce-scatter.9.cloned.1.call-start = ((), (), s32[]{:S(2)}) async-start(), calls=%async_computation.14 | async-start | bytes 5242880 | tf_op jit(solution)/shard_map/reduce_scatter | solution.py:302
  341.9 24.1 %collective-permute-start.27 = (bf16[128,2048]{1,0:T(8,128)(2,1)S(1)}, bf16[128,2048]{1,0:T(8,128)(2,1)S(1)}, u32[]{:S(2)}, u32[]{:S(2)}) collective-permute-start(bf16[128,2048]{1,0:T(8,128)(2,1)S(1)} %get-tuple-element.106), channel_id=1, source_target_pairs={{0,16},{8,24},{16,0},{24,8},{1,17},{9,25},{17,1},{25,9},{2,18},{10... | collective-permute-start | bytes 1572872 | tf_op jit(solution)/shard_map/ppermute | solution.py:151
  342.5 23.5 %collective-permute-start.28 = (bf16[128,2048]{1,0:T(8,128)(2,1)S(1)}, bf16[128,2048]{1,0:T(8,128)(2,1)S(1)}, u32[]{:S(2)}, u32[]{:S(2)}) collective-permute-start(bf16[128,2048]{1,0:T(8,128)(2,1)S(1)} %get-tuple-element.106), channel_id=1, source_target_pairs={{0,24},{8,16},{16,8},{24,0},{1,25},{9,17},{17,9},{25,1},{2,26},{10... | collective-permute-start | bytes 1572872 | tf_op jit(solution)/shard_map/ppermute | solution.py:151
  347.7 20.0 %collective-permute-start.25 = (bf16[512,2048]{1,0:T(8,128)(2,1)}, bf16[512,2048]{1,0:T(8,128)(2,1)}, u32[]{:S(2)}, u32[]{:S(2)}) collective-permute-start(bf16[512,2048]{1,0:T(8,128)(2,1)} %convolution_convert_fusion.1), channel_id=1, source_target_pairs={{0,1},{1,0},{2,3},{3,2},{4,5},{5,4},{6,7},{7,6},{8,9},{9,8},{10,11... | collective-permute-start | bytes 6291464 | tf_op jit(solution)/shard_map/ppermute | solution.py:151
  378.1 30.5 %collective-permute-start.33 = (bf16[2,64,2048]{2,1,0:T(8,128)(2,1)S(1)}, bf16[2,64,2048]{2,1,0:T(8,128)(2,1)S(1)}, u32[]{:S(2)}, u32[]{:S(2)}) collective-permute-start(bf16[2,64,2048]{2,1,0:T(8,128)(2,1)S(1)} %get-tuple-element.129), channel_id=1, source_target_pairs={{0,1},{1,0},{2,3},{3,2},{4,5},{5,4},{6,7},{7,6},{8,9},{9,8},{10,11... | collective-permute-start | bytes 1572872 | tf_op jit(solution)/shard_map/ppermute | solution.py:151
  380.2 36.0 %collective-permute-start.30 = (bf16[128,2048]{1,0:T(8,128)(2,1)}, bf16[128,2048]{1,0:T(8,128)(2,1)}, u32[]{:S(2)}, u32[]{:S(2)}) collective-permute-start(bf16[128,2048]{1,0:T(8,128)(2,1)} %get-tuple-element.121), channel_id=1, source_target_pairs={{0,8},{8,0},{16,24},{24,16},{1,9},{9,1},{17,25},{25,17},{2,10},{10... | collective-permute-start | bytes 1572872 | tf_op jit(solution)/shard_map/ppermute | solution.py:151
  380.7 35.5 %collective-permute-start.31 = (bf16[128,2048]{1,0:T(8,128)(2,1)}, bf16[128,2048]{1,0:T(8,128)(2,1)}, u32[]{:S(2)}, u32[]{:S(2)}) collective-permute-start(bf16[128,2048]{1,0:T(8,128)(2,1)} %get-tuple-element.120), channel_id=1, source_target_pairs={{0,16},{8,24},{16,0},{24,8},{1,17},{9,25},{17,1},{25,9},{2,18},{10... | collective-permute-start | bytes 1572872 | tf_op jit(solution)/shard_map/ppermute | solution.py:151
  382.1 34.1 %collective-permute-start.32 = (bf16[128,2048]{1,0:T(8,128)(2,1)}, bf16[128,2048]{1,0:T(8,128)(2,1)}, u32[]{:S(2)}, u32[]{:S(2)}) collective-permute-start(bf16[128,2048]{1,0:T(8,128)(2,1)} %get-tuple-element.119), channel_id=1, source_target_pairs={{0,24},{8,16},{16,8},{24,0},{1,25},{9,17},{17,9},{25,1},{2,26},{10... | collective-permute-start | bytes 1572872 | tf_op jit(solution)/shard_map/ppermute | solution.py:151
  433.9 41.5 %all-to-all-start.3 = ((bf16[8,64,1024]{2,1,0:T(8,128)(2,1)}), bf16[8,64,1024]{2,1,0:T(8,128)(2,1)S(1)}, u32[]{:S(2)}, u32[]{:S(2)}) async-start(bf16[8,64,1024]{2,1,0:T(8,128)(2,1)} %bitcast.165), calls=%async_computation.5 | async-start | bytes 2097152 | tf_op jit(solution)/shard_map/all_to_all | solution.py:178
  437.5 87.8 %reduce-scatter.11.cloned.1.call-start = ((), (), s32[]{:S(2)}) async-start(), calls=%async_computation.15 | async-start | bytes 1310720 | tf_op jit(solution)/shard_map/reduce_scatter | solution.py:314
  439.2 24.4 %collective-permute-start.35 = (bf16[128,2048]{1,0:T(8,128)(2,1)S(1)}, bf16[128,2048]{1,0:T(8,128)(2,1)S(1)}, u32[]{:S(2)}, u32[]{:S(2)}) collective-permute-start(bf16[128,2048]{1,0:T(8,128)(2,1)S(1)} %get-tuple-element.118), channel_id=1, source_target_pairs={{0,8},{8,0},{16,24},{24,16},{1,9},{9,1},{17,25},{25,17},{2,10},{10... | collective-permute-start | bytes 1572872 | tf_op jit(solution)/shard_map/ppermute | solution.py:151
  441.2 22.5 %collective-permute-start.36 = (bf16[128,2048]{1,0:T(8,128)(2,1)S(1)}, bf16[128,2048]{1,0:T(8,128)(2,1)S(1)}, u32[]{:S(2)}, u32[]{:S(2)}) collective-permute-start(bf16[128,2048]{1,0:T(8,128)(2,1)S(1)} %get-tuple-element.117), channel_id=1, source_target_pairs={{0,16},{8,24},{16,0},{24,8},{1,17},{9,25},{17,1},{25,9},{2,18},{10... | collective-permute-start | bytes 1572872 | tf_op jit(solution)/shard_map/ppermute | solution.py:151
  442.7 32.8 %collective-permute-start.37 = (bf16[128,2048]{1,0:T(8,128)(2,1)S(1)}, bf16[128,2048]{1,0:T(8,128)(2,1)}, u32[]{:S(2)}, u32[]{:S(2)}) collective-permute-start(bf16[128,2048]{1,0:T(8,128)(2,1)S(1)} %get-tuple-element.116), channel_id=1, source_target_pairs={{0,24},{8,16},{16,8},{24,0},{1,25},{9,17},{17,9},{25,1},{2,26},{10... | collective-permute-start | bytes 1572872 | tf_op jit(solution)/shard_map/ppermute | solution.py:151
  (88 other events, 1035.9 us)
Sparse Core Ops, SparseCore 0:
  9.6 30.6 all-gather.11
  41.8 62.9 all-gather.5
  107.0 79.4 all-gather.7
  187.9 79.2 all-gather.9
  271.6 58.5 reduce-scatter.4
  332.7 76.3 reduce-scatter.6
  416.4 74.5 reduce-scatter.8
  493.3 27.8 reduce-scatter.10

commit v7 on v6

--- a/solution.py
+++ b/solution.py
@@ -104,6 +104,35 @@
     places, R, wide = v.shape
     out = jax.ShapeDtypeStruct((R, places * wide // 3), F32)
     return pl.pallas_call(finish_kernel, out_shape=[out] * 3)(v)
+
+
+def widen_kernel(in_ref, *refs):
+    refs[-1][...] = in_ref[...].astype(F32)
+
+
+def widen_first(v, columns):
+    R, own = v.shape
+    block = columns - own
+    return pl.pallas_call(
+        widen_kernel,
+        grid=(own // block,),
+        in_specs=[pl.BlockSpec((R, block), lambda j: (0, j))],
+        out_specs=pl.BlockSpec((R, block), lambda j: (0, j)),
+        out_shape=jax.ShapeDtypeStruct((R, columns), F32),
+    )(v)
+
+
+def widen_last(v, into):
+    R, block = v.shape
+    last = into.shape[1] // block - 1
+    return pl.pallas_call(
+        widen_kernel,
+        grid=(1,),
+        in_specs=[pl.BlockSpec((R, block), lambda j: (0, 0)), pl.BlockSpec(memory_space=pl.ANY)],
+        out_specs=pl.BlockSpec((R, block), lambda j: (0, last)),
+        out_shape=jax.ShapeDtypeStruct(into.shape, F32),
+        input_output_aliases={1: 0},
+    )(v, into)
 
 
 def spread_kernel(starts, width, in_ref, out_ref):
@@ -312,7 +341,7 @@
         up_grad = after(up_grad, mixed_sum)
         up_weight_grad = finish_up(up_grad.reshape(tp, R, Z * RF), S, Z)
         down_rest = lax.psum_scatter(after(down_rest, mixed_sum), "z", scatter_dimension=0, tiled=True)
-        down_weight_grad = jnp.concatenate([down_early, down_rest], axis=1).astype(F32)
+        down_weight_grad = widen_last(down_rest, widen_first(down_early, D))
         query_grad, key_grad, value_grad = finish_qkv(qkv_grad)
 
         bias = sum(jnp.sum(v.astype(F32), axis=0) for v in dqkv).reshape(3, cols)
@@ -336,7 +365,7 @@
         packed = jnp.concatenate([v.reshape(S, Z, 2, -1) for v in vectors], axis=3)
         packed = lax.dynamic_index_in_dim(packed, c, 2, False) + swap_core(lax.dynamic_index_in_dim(packed, 1 - c, 2, False))
         packed = spread_scatter(packed, "seq", S, s)
-        packed = spread_scatter(packed, "z", Z, z)
+        packed = spread_scatter(after(packed, qkv_grad, up_weight_grad, output_weight_grad), "z", Z, z)
         ob_grad, g2_grad, b2_grad, db_grad = [packed[i * R : (i + 1) * R] for i in range(4)]
         ub_grad = packed[4 * R : 4 * R + RF]
         qb_grad, vb_grad, g1_grad, b1_grad = [packed[(4 + i) * R + RF : (5 + i) * R + RF] for i in range(4)]

time: 540 us -> 537 us (level)
  waiting for transfers between devices: 221 us -> 212 us
    unnamed x136 -> x132, local copies, waits for them, and re-layouts: 16.9 us -> 16 us
  transfers between devices with their start and end apart: 57 -> 57, of which waited for: 25 -> 22; matrix products, arithmetic and copies ran while one was open for 33% -> 34% of each run, Pallas kernels for 6% -> 6%
where the time goes in v7:
time: 537 us; the launch traced here: 531 us
  waiting for transfers between devices  212 us (39%)
  matrix products  107 us (20%)
  starting transfers between devices  61 us (11%)
  other arithmetic  42.5 us (8%)
  local copies, waits for them, and re-layouts  41.1 us (8%)
  Pallas kernels  35 us (7%)
  blocking collectives  17.8 us (3%)
  between operations  15.5 us (3%)
    ppermute x45, waiting for transfers between devices, flip(): return lax.ppermute(v, axis, [(i, i ^ q) for i in range(size)])  149 us
    dot_general x23, matrix products, dot(): return jnp.einsum(form, left, right, preferred_element_type=F32)  107 us
    ppermute x45, starting transfers between devices, flip(): return lax.ppermute(v, axis, [(i, i ^ q) for i in range(size)])  44.6 us
    all_gather x1, waiting for transfers between devices, body(): wup = lax.all_gather(up, 'z', axis=0, tiled=True)  21.7 us
    all_to_all x1, blocking collectives, exchange(): return lax.all_to_all(v, axes, split_axis=0, concat_axis=0, tiled=True)  17.8 us
    pallas_call x4, Pallas kernels, attend_call(): pl.pallas_call(functools.partial(kernel, heads), out_shape=jax.ShapeDtype...  16.7 us
    unnamed x132, local copies, waits for them, and re-layouts  16 us
    all_to_all x4, starting transfers between devices, exchange(): return lax.all_to_all(v, axes, split_axis=0, concat_axis=0, tiled=True)  14.9 us
  transfers between devices with their start and end apart: 57, of which 22 were waited for; matrix products, arithmetic and copies ran while one was open for 34% of the time, Pallas kernels for 6%

profile of v7, /device:TPU:0, one launch (start us, length us, event | category | flops | bytes accessed | tf_op | source)
XLA Modules:
  0.0 531.1 jit_solution(16100070427016922399)
XLA Ops:
  11.3 17.8 %all_to_all.29 = bf16[8,64,768]{2,1,0:T(8,128)(2,1)} all-to-all(bf16[8,64,768]{2,1,0:T(8,128)(2,1)S(1)} %copy.55), channel_id=1, replica_groups=mesh['seq'=4,'z'=4,'core'=2] {'seq','core'}, dimensions={0} | all-to-all | bytes 1572864 | tf_op jit(solution)/shard_map/all_to_all | solution.py:207
  29.1 11.2 %all-gather.12.cloned.1.call-done = bf16[256,2048]{1,0:T(8,128)(2,1)} async-done(((bf16[64,2048]{1,0:T(8,128)(2,1)}), bf16[256,2048]{1,0:T(8,128)(2,1)}) %all-gather.12.cloned.1.call-update) | async-done | bytes 1048592 | tf_op jit(solution)/shard_map/all_gather | solution.py:244
  47.2 7.3 %all-to-all-done.1 = bf16[32,2,384]{2,1,0:T(2,128)(2,1)S(1)} async-done(((bf16[32,2,384]{2,1,0:T(2,128)(2,1)}), bf16[32,2,384]{2,1,0:T(2,128)(2,1)S(1)}, u32[]{:S(2)}, u32[]{:S(2)}) %all-to-all-start.1) | async-done | bytes 49184 | tf_op jit(solution)/shard_map/all_to_all | solution.py:207
  67.8 5.2 collective-permute-done.3
  73.0 11.7 %collective-permute-done.4 = bf16[128,2048]{1,0:T(8,128)(2,1)} collective-permute-done((bf16[128,2048]{1,0:T(8,128)(2,1)}, bf16[128,2048]{1,0:T(8,128)(2,1)}, u32[]{:S(2)}, u32[]{:S(2)}) %collective-permute-start.4) | collective-permute-done | bytes 524320 | tf_op jit(solution)/shard_map/ppermute | solution.py:180
  87.6 4.9 collective-permute-start
  94.6 10.2 %all-gather.6.cloned.1.call-done = bf16[2048,768]{1,0:T(8,128)(2,1)} async-done(((bf16[512,768]{1,0:T(8,128)(2,1)}), bf16[2048,768]{1,0:T(8,128)(2,1)}) %all-gather.6.cloned.1.call-update) | async-done | bytes 3145744 | tf_op jit(solution)/shard_map/all_gather | solution.py:245
  108.6 5.2 add_convert_fusion.1.qkv_ref
  121.5 5.1 add_convert_fusion.2.qkv_ref
  139.5 11.3 %collective-permute-done.10 = bf16[128,2048]{1,0:T(8,128)(2,1)S(1)} collective-permute-done((bf16[128,2048]{1,0:T(8,128)(2,1)}, bf16[128,2048]{1,0:T(8,128)(2,1)S(1)}, u32[]{:S(2)}, u32[]{:S(2)}) %collective-permute-start.10) | collective-permute-done | bytes 524320 | tf_op jit(solution)/shard_map/ppermute | solution.py:180
  150.7 11.6 %collective-permute-done.11 = bf16[128,2048]{1,0:T(8,128)(2,1)S(1)} collective-permute-done((bf16[128,2048]{1,0:T(8,128)(2,1)}, bf16[128,2048]{1,0:T(8,128)(2,1)S(1)}, u32[]{:S(2)}, u32[]{:S(2)}) %collective-permute-start.11) | collective-permute-done | bytes 524320 | tf_op jit(solution)/shard_map/ppermute | solution.py:180
  164.9 21.7 %all-gather.8.cloned.1.call-done = bf16[2048,1024]{1,0:T(8,128)(2,1)} async-done(((bf16[512,1024]{1,0:T(8,128)(2,1)}), bf16[2048,1024]{1,0:T(8,128)(2,1)}) %all-gather.8.cloned.1.call-update) | async-done | bytes 4194320 | tf_op jit(solution)/shard_map/all_gather | solution.py:248
  195.1 11.5 %collective-permute-done.13 = bf16[128,2048]{1,0:T(8,128)(2,1)S(1)} collective-permute-done((bf16[128,2048]{1,0:T(8,128)(2,1)}, bf16[128,2048]{1,0:T(8,128)(2,1)S(1)}, u32[]{:S(2)}, u32[]{:S(2)}) %collective-permute-start.13) | collective-permute-done | bytes 524320 | tf_op jit(solution)/shard_map/ppermute | solution.py:180
  206.6 11.3 %collective-permute-done.14 = bf16[128,2048]{1,0:T(8,128)(2,1)S(1)} collective-permute-done((bf16[128,2048]{1,0:T(8,128)(2,1)}, bf16[128,2048]{1,0:T(8,128)(2,1)S(1)}, u32[]{:S(2)}, u32[]{:S(2)}) %collective-permute-start.14) | collective-permute-done | bytes 524320 | tf_op jit(solution)/shard_map/ppermute | solution.py:180
  225.4 10.4 %collective-permute-done.17 = bf16[128,2048]{1,0:T(8,128)(2,1)S(1)} collective-permute-done((bf16[128,2048]{1,0:T(8,128)(2,1)S(1)}, bf16[128,2048]{1,0:T(8,128)(2,1)S(1)}, u32[]{:S(2)}, u32[]{:S(2)}) %collective-permute-start.17) | collective-permute-done | bytes 524320 | tf_op jit(solution)/shard_map/ppermute | solution.py:180
  236.8 9.0 %collective-permute-done.18 = bf16[128,2048]{1,0:T(8,128)(2,1)S(1)} collective-permute-done((bf16[128,2048]{1,0:T(8,128)(2,1)S(1)}, bf16[128,2048]{1,0:T(8,128)(2,1)S(1)}, u32[]{:S(2)}, u32[]{:S(2)}) %collective-permute-start.18) | collective-permute-done | bytes 524320 | tf_op jit(solution)/shard_map/ppermute | solution.py:180
  249.8 5.3 fusion.57
  255.2 6.5 %multiply_convert_fusion = (bf16[512,1024]{1,0:T(8,128)(2,1)S(1)}, bf16[512,1024]{1,0:T(8,128)(2,1)S(1)}, f32[512,1024]{1,0:T(8,128)}) fusion(f32[1024]{0:T(1024)S(1)} %bitcast.181, f32[512,1024]{1,0:T(8,128)S(1)} %fusion.57, bf16[512,2048]{1,0:T(8,128)(2,1)} %collective-permute-done.16, bf16[2048,1024]{1,0:T(8,128)(2,1)S(1)} %copy-done.54), kind=kOutput, calls=%fused_computation.38 | convolution fusion | flops 2153775104 | bytes 12587008 | tf_op jit(solution)/shard_map/td,df->tf/dot_general | solution.py:22
  266.4 5.1 convolution_convert_fusion
  272.0 6.5 %fusion.20 = bf16[512,1024]{1,0:T(8,128)(2,1)S(1)} fusion(f32[512,1024]{1,0:T(8,128)} %get-tuple-element.180, bf16[512,2048]{1,0:T(8,128)(2,1)} %collective-permute-done.20, bf16[1024,2048]{1,0:T(8,128)(2,1)} %all-gather.10.cloned.1.call-done, f32[1024]{0:T(1024)S(1)} %bitcast.182), kind=kOutput, calls=%fused_computation.33 | convolution fusion | flops 2153250816 | bytes 9441280 | tf_op jit(solution)/shard_map/td,fd->tf/dot_general | solution.py:22
  295.8 9.7 %collective-permute-done.22 = bf16[128,2048]{1,0:T(8,128)(2,1)S(1)} collective-permute-done((bf16[128,2048]{1,0:T(8,128)(2,1)S(1)}, bf16[128,2048]{1,0:T(8,128)(2,1)S(1)}, u32[]{:S(2)}, u32[]{:S(2)}) %collective-permute-start.22) | collective-permute-done | bytes 524320 | tf_op jit(solution)/shard_map/ppermute | solution.py:180
  305.5 11.0 %collective-permute-done.23 = bf16[128,2048]{1,0:T(8,128)(2,1)S(1)} collective-permute-done((bf16[128,2048]{1,0:T(8,128)(2,1)S(1)}, bf16[128,2048]{1,0:T(8,128)(2,1)S(1)}, u32[]{:S(2)}, u32[]{:S(2)}) %collective-permute-start.23) | collective-permute-done | bytes 524320 | tf_op jit(solution)/shard_map/ppermute | solution.py:180
  318.9 8.5 %fusion.4 = bf16[2048,1024]{1,0:T(8,128)(2,1)} fusion(bf16[1024,1024]{1,0:T(8,128)(2,1)S(1)} %constant_dynamic-update-slice_fusion.9, bf16[512,2048]{1,0:T(8,128)(2,1)} %collective-permute-done.16, bf16[512,2048]{1,0:T(8,128)(2,1)} %pad_maximum_fusion.2), kind=kOutput, calls=%fused_computation.11 | convolution fusion | flops 4305453056 | bytes 10485760 | tf_op jit(solution)/shard_map/td,tf->df/dot_general | solution.py:22
  347.8 7.7 %collective-permute-done.26 = bf16[128,2048]{1,0:T(8,128)(2,1)S(1)} collective-permute-done((bf16[128,2048]{1,0:T(8,128)(2,1)S(1)}, bf16[128,2048]{1,0:T(8,128)(2,1)S(1)}, u32[]{:S(2)}, u32[]{:S(2)}) %collective-permute-start.26) | collective-permute-done | bytes 524320 | tf_op jit(solution)/shard_map/ppermute | solution.py:180
  355.5 10.6 %collective-permute-done.27 = bf16[128,2048]{1,0:T(8,128)(2,1)S(1)} collective-permute-done((bf16[128,2048]{1,0:T(8,128)(2,1)S(1)}, bf16[128,2048]{1,0:T(8,128)(2,1)S(1)}, u32[]{:S(2)}, u32[]{:S(2)}) %collective-permute-start.27) | collective-permute-done | bytes 524320 | tf_op jit(solution)/shard_map/ppermute | solution.py:180
  367.8 5.5 %convert_add_fusion.1 = f32[512,2048]{1,0:T(8,128)S(1)} fusion(bf16[512,2048]{1,0:T(8,128)(2,1)} %collective-permute-done.25, bf16[512,1024]{1,0:T(8,128)(2,1)} %copy-done.19, bf16[1024,2048]{1,0:T(8,128)(2,1)} %all-gather.10.cloned.1.call-done), kind=kOutput, calls=%fused_computation.8 | convolution fusion | flops 2149580800 | bytes 11534336 | tf_op jit(solution)/shard_map/tf,fd->td/dot_general | solution.py:22
  403.7 5.1 add_convert_fusion
  417.4 5.0 convolution_convert_fusion.4
  428.4 7.2 %fusion.58 = (bf16[512,2048]{1,0:T(8,128)(2,1)}, f32[512,2048]{1,0:T(8,128)}) fusion(bf16[512,2048]{1,0:T(8,128)(2,1)} %collective-permute-done.34, bf16[512,768]{1,0:T(8,128)(2,1)S(1)} %copy-done.24, bf16[2048,768]{1,0:T(8,128)(2,1)} %all-gather.6.cloned.1.call-done), kind=kOutput, calls=%fused_computation.162 | convolution fusion | flops 1613758464 | bytes 12320768 | tf_op jit(solution)/shard_map/te,de->td/dot_general | solution.py:22
  448.6 16.7 %collective-permute-done.35 = bf16[128,2048]{1,0:T(8,128)(2,1)S(1)} collective-permute-done((bf16[128,2048]{1,0:T(8,128)(2,1)S(1)}, bf16[128,2048]{1,0:T(8,128)(2,1)S(1)}, u32[]{:S(2)}, u32[]{:S(2)}) %collective-permute-start.35) | collective-permute-done | bytes 524320 | tf_op jit(solution)/shard_map/ppermute | solution.py:180
  466.1 11.0 %collective-permute-done.37 = bf16[128,2048]{1,0:T(8,128)(2,1)} collective-permute-done((bf16[128,2048]{1,0:T(8,128)(2,1)S(1)}, bf16[128,2048]{1,0:T(8,128)(2,1)}, u32[]{:S(2)}, u32[]{:S(2)}) %collective-permute-start.37) | collective-permute-done | bytes 524320 | tf_op jit(solution)/shard_map/ppermute | solution.py:180
  484.5 6.6 %reduce-scatter.9.cloned.1.call-done = bf16[512,1024]{0,1:T(8,128)(2,1)} async-done(((bf16[2048,1024]{0,1:T(8,128)(2,1)}), bf16[512,1024]{0,1:T(8,128)(2,1)}) %reduce-scatter.9.cloned.1.call-update) | async-done | bytes 1048592 | tf_op jit(solution)/shard_map/reduce_scatter | solution.py:331
  (368 shorter events, 222.3 us)
Async XLA Ops:
  7.2 33.1 %all-gather.12.cloned.1.call-start = ((), (), s32[]{:S(2)}) async-start(), calls=%async_computation.16 | async-start | bytes 1310720 | tf_op jit(solution)/shard_map/all_gather | solution.py:244
  7.9 96.9 %all-gather.6.cloned.1.call-start = ((), (), s32[]{:S(2)}) async-start(), calls=%async_computation.9 | async-start | bytes 3932160 | tf_op jit(solution)/shard_map/all_gather | solution.py:245
  58.5 26.1 %collective-permute-start.4 = (bf16[128,2048]{1,0:T(8,128)(2,1)}, bf16[128,2048]{1,0:T(8,128)(2,1)}, u32[]{:S(2)}, u32[]{:S(2)}) collective-permute-start(bf16[128,2048]{1,0:T(8,128)(2,1)} %shard_map.314), channel_id=1, source_target_pairs={{0,16},{8,24},{16,0},{24,8},{1,17},{9,25},{17,1},{25,9},{2,18},{10... | collective-permute-start | bytes 1572872 | tf_op jit(solution)/shard_map/ppermute | solution.py:180
  59.2 25.5 %collective-permute-start.5 = (bf16[128,2048]{1,0:T(8,128)(2,1)}, bf16[128,2048]{1,0:T(8,128)(2,1)}, u32[]{:S(2)}, u32[]{:S(2)}) collective-permute-start(bf16[128,2048]{1,0:T(8,128)(2,1)} %shard_map.314), channel_id=1, source_target_pairs={{0,24},{8,16},{16,8},{24,0},{1,25},{9,17},{17,9},{25,1},{2,26},{10... | collective-permute-start | bytes 1572872 | tf_op jit(solution)/shard_map/ppermute | solution.py:180
  64.2 30.4 %all-to-all-start.2 = ((bf16[8,64,1024]{2,1,0:T(8,128)(2,1)}), bf16[8,64,1024]{2,1,0:T(8,128)(2,1)S(1)}, u32[]{:S(2)}, u32[]{:S(2)}) async-start(bf16[8,64,1024]{2,1,0:T(8,128)(2,1)} %reshape.284), calls=%async_computation.2 | async-start | bytes 2097152 | tf_op jit(solution)/shard_map/all_to_all | solution.py:207
  67.8 118.7 %all-gather.8.cloned.1.call-start = ((), (), s32[]{:S(2)}) async-start(), calls=%async_computation.10 | async-start | bytes 5242880 | tf_op jit(solution)/shard_map/all_gather | solution.py:248
  87.6 20.9 %collective-permute-start.8 = (bf16[512,2048]{1,0:T(8,128)(2,1)}, bf16[512,2048]{1,0:T(8,128)(2,1)}, u32[]{:S(2)}, u32[]{:S(2)}) collective-permute-start(bf16[512,2048]{1,0:T(8,128)(2,1)} %pad_maximum_fusion.1), channel_id=1, source_target_pairs={{0,1},{1,0},{2,3},{3,2},{4,5},{5,4},{6,7},{7,6},{8,9},{9,8},{10,11... | collective-permute-start | bytes 6291464 | tf_op jit(solution)/shard_map/ppermute | solution.py:180
  104.9 166.6 %all-gather.10.cloned.1.call-start = ((), (), s32[]{:S(2)}) async-start(), calls=%async_computation.11 | async-start | bytes 5242880 | tf_op jit(solution)/shard_map/all_gather | solution.py:249
  137.2 25.2 %collective-permute-start.11 = (bf16[128,2048]{1,0:T(8,128)(2,1)}, bf16[128,2048]{1,0:T(8,128)(2,1)S(1)}, u32[]{:S(2)}, u32[]{:S(2)}) collective-permute-start(bf16[128,2048]{1,0:T(8,128)(2,1)} %get-tuple-element.129), channel_id=1, source_target_pairs={{0,16},{8,24},{16,0},{24,8},{1,17},{9,25},{17,1},{25,9},{2,18},{10... | collective-permute-start | bytes 1572872 | tf_op jit(solution)/shard_map/ppermute | solution.py:180
  138.7 23.7 %collective-permute-start.12 = (bf16[128,2048]{1,0:T(8,128)(2,1)}, bf16[128,2048]{1,0:T(8,128)(2,1)S(1)}, u32[]{:S(2)}, u32[]{:S(2)}) collective-permute-start(bf16[128,2048]{1,0:T(8,128)(2,1)} %get-tuple-element.128), channel_id=1, source_target_pairs={{0,24},{8,16},{16,8},{24,0},{1,25},{9,17},{17,9},{25,1},{2,26},{10... | collective-permute-start | bytes 1572872 | tf_op jit(solution)/shard_map/ppermute | solution.py:180
  186.5 146.1 %reduce-scatter.5.cloned.1.call-start = ((), (), s32[]{:S(2)}) async-start(), calls=%async_computation.12 | async-start | bytes 3932160 | tf_op jit(solution)/shard_map/reduce_scatter | solution.py:294
  193.1 24.8 %collective-permute-start.14 = (bf16[128,2048]{1,0:T(8,128)(2,1)}, bf16[128,2048]{1,0:T(8,128)(2,1)S(1)}, u32[]{:S(2)}, u32[]{:S(2)}) collective-permute-start(bf16[128,2048]{1,0:T(8,128)(2,1)} %shard_map.317), channel_id=1, source_target_pairs={{0,16},{8,24},{16,0},{24,8},{1,17},{9,25},{17,1},{25,9},{2,18},{10... | collective-permute-start | bytes 1572872 | tf_op jit(solution)/shard_map/ppermute | solution.py:180
  194.6 23.3 %collective-permute-start.15 = (bf16[128,2048]{1,0:T(8,128)(2,1)}, bf16[128,2048]{1,0:T(8,128)(2,1)S(1)}, u32[]{:S(2)}, u32[]{:S(2)}) collective-permute-start(bf16[128,2048]{1,0:T(8,128)(2,1)} %shard_map.317), channel_id=1, source_target_pairs={{0,24},{8,16},{16,8},{24,0},{1,25},{9,17},{17,9},{25,1},{2,26},{10... | collective-permute-start | bytes 1572872 | tf_op jit(solution)/shard_map/ppermute | solution.py:180
  222.0 23.8 %collective-permute-start.18 = (bf16[128,2048]{1,0:T(8,128)(2,1)S(1)}, bf16[128,2048]{1,0:T(8,128)(2,1)S(1)}, u32[]{:S(2)}, u32[]{:S(2)}) collective-permute-start(bf16[128,2048]{1,0:T(8,128)(2,1)S(1)} %bitcast.162), channel_id=1, source_target_pairs={{0,16},{8,24},{16,0},{24,8},{1,17},{9,25},{17,1},{25,9},{2,18},{10... | collective-permute-start | bytes 1572872 | tf_op jit(solution)/shard_map/ppermute | solution.py:180
  223.0 23.7 %collective-permute-start.19 = (bf16[128,2048]{1,0:T(8,128)(2,1)S(1)}, bf16[128,2048]{1,0:T(8,128)(2,1)S(1)}, u32[]{:S(2)}, u32[]{:S(2)}) collective-permute-start(bf16[128,2048]{1,0:T(8,128)(2,1)S(1)} %bitcast.163), channel_id=1, source_target_pairs={{0,24},{8,16},{16,8},{24,0},{1,25},{9,17},{17,9},{25,1},{2,26},{10... | collective-permute-start | bytes 1572872 | tf_op jit(solution)/shard_map/ppermute | solution.py:180
  224.5 30.7 %collective-permute-start.16 = (bf16[512,2048]{1,0:T(8,128)(2,1)}, bf16[512,2048]{1,0:T(8,128)(2,1)}, u32[]{:S(2)}, u32[]{:S(2)}) collective-permute-start(bf16[512,2048]{1,0:T(8,128)(2,1)} %pad_maximum_fusion.2), channel_id=1, source_target_pairs={{0,1},{1,0},{2,3},{3,2},{4,5},{5,4},{6,7},{7,6},{8,9},{9,8},{10,11... | collective-permute-start | bytes 6291464 | tf_op jit(solution)/shard_map/ppermute | solution.py:180
  271.5 144.8 %reduce-scatter.7.cloned.1.call-start = ((), (), s32[]{:S(2)}) async-start(), calls=%async_computation.13 | async-start | bytes 5242880 | tf_op jit(solution)/shard_map/reduce_scatter | solution.py:308
  291.4 25.1 %collective-permute-start.23 = (bf16[128,2048]{1,0:T(8,128)(2,1)S(1)}, bf16[128,2048]{1,0:T(8,128)(2,1)S(1)}, u32[]{:S(2)}, u32[]{:S(2)}) collective-permute-start(bf16[128,2048]{1,0:T(8,128)(2,1)S(1)} %get-tuple-element.126), channel_id=1, source_target_pairs={{0,16},{8,24},{16,0},{24,8},{1,17},{9,25},{17,1},{25,9},{2,18},{10... | collective-permute-start | bytes 1572872 | tf_op jit(solution)/shard_map/ppermute | solution.py:180
  291.6 24.9 %collective-permute-start.24 = (bf16[128,2048]{1,0:T(8,128)(2,1)S(1)}, bf16[128,2048]{1,0:T(8,128)(2,1)S(1)}, u32[]{:S(2)}, u32[]{:S(2)}) collective-permute-start(bf16[128,2048]{1,0:T(8,128)(2,1)S(1)} %get-tuple-element.125), channel_id=1, source_target_pairs={{0,24},{8,16},{16,8},{24,0},{1,25},{9,17},{17,9},{25,1},{2,26},{10... | collective-permute-start | bytes 1572872 | tf_op jit(solution)/shard_map/ppermute | solution.py:180
  332.7 158.4 %reduce-scatter.9.cloned.1.call-start = ((), (), s32[]{:S(2)}) async-start(), calls=%async_computation.14 | async-start | bytes 5242880 | tf_op jit(solution)/shard_map/reduce_scatter | solution.py:331
  342.0 24.2 %collective-permute-start.27 = (bf16[128,2048]{1,0:T(8,128)(2,1)S(1)}, bf16[128,2048]{1,0:T(8,128)(2,1)S(1)}, u32[]{:S(2)}, u32[]{:S(2)}) collective-permute-start(bf16[128,2048]{1,0:T(8,128)(2,1)S(1)} %get-tuple-element.108), channel_id=1, source_target_pairs={{0,16},{8,24},{16,0},{24,8},{1,17},{9,25},{17,1},{25,9},{2,18},{10... | collective-permute-start | bytes 1572872 | tf_op jit(solution)/shard_map/ppermute | solution.py:180
  342.6 23.6 %collective-permute-start.28 = (bf16[128,2048]{1,0:T(8,128)(2,1)S(1)}, bf16[128,2048]{1,0:T(8,128)(2,1)S(1)}, u32[]{:S(2)}, u32[]{:S(2)}) collective-permute-start(bf16[128,2048]{1,0:T(8,128)(2,1)S(1)} %get-tuple-element.108), channel_id=1, source_target_pairs={{0,24},{8,16},{16,8},{24,0},{1,25},{9,17},{17,9},{25,1},{2,26},{10... | collective-permute-start | bytes 1572872 | tf_op jit(solution)/shard_map/ppermute | solution.py:180
  347.8 20.0 %collective-permute-start.25 = (bf16[512,2048]{1,0:T(8,128)(2,1)}, bf16[512,2048]{1,0:T(8,128)(2,1)}, u32[]{:S(2)}, u32[]{:S(2)}) collective-permute-start(bf16[512,2048]{1,0:T(8,128)(2,1)} %convolution_convert_fusion.1), channel_id=1, source_target_pairs={{0,1},{1,0},{2,3},{3,2},{4,5},{5,4},{6,7},{7,6},{8,9},{9,8},{10,11... | collective-permute-start | bytes 6291464 | tf_op jit(solution)/shard_map/ppermute | solution.py:180
  378.2 30.5 %collective-permute-start.33 = (bf16[2,64,2048]{2,1,0:T(8,128)(2,1)S(1)}, bf16[2,64,2048]{2,1,0:T(8,128)(2,1)S(1)}, u32[]{:S(2)}, u32[]{:S(2)}) collective-permute-start(bf16[2,64,2048]{2,1,0:T(8,128)(2,1)S(1)} %get-tuple-element.131), channel_id=1, source_target_pairs={{0,1},{1,0},{2,3},{3,2},{4,5},{5,4},{6,7},{7,6},{8,9},{9,8},{10,11... | collective-permute-start | bytes 1572872 | tf_op jit(solution)/shard_map/ppermute | solution.py:180
  380.3 36.0 %collective-permute-start.30 = (bf16[128,2048]{1,0:T(8,128)(2,1)}, bf16[128,2048]{1,0:T(8,128)(2,1)}, u32[]{:S(2)}, u32[]{:S(2)}) collective-permute-start(bf16[128,2048]{1,0:T(8,128)(2,1)} %get-tuple-element.123), channel_id=1, source_target_pairs={{0,8},{8,0},{16,24},{24,16},{1,9},{9,1},{17,25},{25,17},{2,10},{10... | collective-permute-start | bytes 1572872 | tf_op jit(solution)/shard_map/ppermute | solution.py:180
  380.8 35.5 %collective-permute-start.31 = (bf16[128,2048]{1,0:T(8,128)(2,1)}, bf16[128,2048]{1,0:T(8,128)(2,1)}, u32[]{:S(2)}, u32[]{:S(2)}) collective-permute-start(bf16[128,2048]{1,0:T(8,128)(2,1)} %get-tuple-element.122), channel_id=1, source_target_pairs={{0,16},{8,24},{16,0},{24,8},{1,17},{9,25},{17,1},{25,9},{2,18},{10... | collective-permute-start | bytes 1572872 | tf_op jit(solution)/shard_map/ppermute | solution.py:180
  382.2 34.0 %collective-permute-start.32 = (bf16[128,2048]{1,0:T(8,128)(2,1)}, bf16[128,2048]{1,0:T(8,128)(2,1)}, u32[]{:S(2)}, u32[]{:S(2)}) collective-permute-start(bf16[128,2048]{1,0:T(8,128)(2,1)} %get-tuple-element.121), channel_id=1, source_target_pairs={{0,24},{8,16},{16,8},{24,0},{1,25},{9,17},{17,9},{25,1},{2,26},{10... | collective-permute-start | bytes 1572872 | tf_op jit(solution)/shard_map/ppermute | solution.py:180
  435.6 41.5 %all-to-all-start.3 = ((bf16[8,64,1024]{2,1,0:T(8,128)(2,1)}), bf16[8,64,1024]{2,1,0:T(8,128)(2,1)S(1)}, u32[]{:S(2)}, u32[]{:S(2)}) async-start(bf16[8,64,1024]{2,1,0:T(8,128)(2,1)} %bitcast.165), calls=%async_computation.5 | async-start | bytes 2097152 | tf_op jit(solution)/shard_map/all_to_all | solution.py:207
  439.1 83.1 %reduce-scatter.11.cloned.1.call-start = ((), (), s32[]{:S(2)}) async-start(), calls=%async_computation.15 | async-start | bytes 1310720 | tf_op jit(solution)/shard_map/reduce_scatter | solution.py:343
  440.9 24.4 %collective-permute-start.35 = (bf16[128,2048]{1,0:T(8,128)(2,1)S(1)}, bf16[128,2048]{1,0:T(8,128)(2,1)S(1)}, u32[]{:S(2)}, u32[]{:S(2)}) collective-permute-start(bf16[128,2048]{1,0:T(8,128)(2,1)S(1)} %get-tuple-element.120), channel_id=1, source_target_pairs={{0,8},{8,0},{16,24},{24,16},{1,9},{9,1},{17,25},{25,17},{2,10},{10... | collective-permute-start | bytes 1572872 | tf_op jit(solution)/shard_map/ppermute | solution.py:180
  442.9 22.4 %collective-permute-start.36 = (bf16[128,2048]{1,0:T(8,128)(2,1)S(1)}, bf16[128,2048]{1,0:T(8,128)(2,1)S(1)}, u32[]{:S(2)}, u32[]{:S(2)}) collective-permute-start(bf16[128,2048]{1,0:T(8,128)(2,1)S(1)} %get-tuple-element.119), channel_id=1, source_target_pairs={{0,16},{8,24},{16,0},{24,8},{1,17},{9,25},{17,1},{25,9},{2,18},{10... | collective-permute-start | bytes 1572872 | tf_op jit(solution)/shard_map/ppermute | solution.py:180
  444.4 32.7 %collective-permute-start.37 = (bf16[128,2048]{1,0:T(8,128)(2,1)S(1)}, bf16[128,2048]{1,0:T(8,128)(2,1)}, u32[]{:S(2)}, u32[]{:S(2)}) collective-permute-start(bf16[128,2048]{1,0:T(8,128)(2,1)S(1)} %get-tuple-element.118), channel_id=1, source_target_pairs={{0,24},{8,16},{16,8},{24,0},{1,25},{9,17},{17,9},{25,1},{2,26},{10... | collective-permute-start | bytes 1572872 | tf_op jit(solution)/shard_map/ppermute | solution.py:180
  (86 other events, 1010.8 us)
Sparse Core Ops, SparseCore 0:
  9.6 30.6 all-gather.11
  41.8 62.9 all-gather.5
  107.0 79.4 all-gather.7
  187.9 79.2 all-gather.9
  271.6 58.5 reduce-scatter.4
  332.8 76.3 reduce-scatter.6
  416.5 74.5 reduce-scatter.8
  493.4 27.8 reduce-scatter.10

commit v8 on v7

--- a/solution.py
+++ b/solution.py
@@ -303,11 +303,9 @@
         dhidden_join = join(fill_dhidden)
         up_grad = dot("td,tf->df", join(fill_second), dhidden_join).astype(BF)
         up_mm = up_grad
-        active_join, dy_join = after((active_join, dy_join), up_mm)
-        down_rest = dot("tf,td->fd", active_join, dy_join[:, early:]).astype(BF)
         up_grad = lax.psum_scatter(after(up_grad, down_early), "z", scatter_dimension=0, tiled=True)
         dsecond = lane_blocks(add_up(mine, got), back)
-        dsecond = after(dsecond, down_early, up_mm, down_rest)
+        dsecond = after(dsecond, down_early, up_mm)
         dmiddle = dyf + norm_back(xhat2, inv2, g2 * dsecond)
         dbranch = (dmiddle * keep).astype(BF)
         dbranch_all = plane_gather(dbranch)
@@ -328,6 +326,8 @@
         result = add_up(rows(result, 0, t), after(result_got, qkv_grad))
         mixed = jnp.concatenate([qkv_grad, wo_grad.reshape(D, -1)], axis=1)
         dqkv = after(dqkv, mixed)
+        active_join, dy_join = after((active_join, dy_join), mixed)
+        down_rest = dot("tf,td->fd", active_join, dy_join[:, early:]).astype(BF)
         mixed = lax.psum_scatter(after(mixed, up_grad, result_got), "z", scatter_dimension=0, tiled=True)
         mixed_sum = mixed
         qkv_grad = exchange(mixed[:, : 3 * cols].reshape(tp, R, 3 * cols), ("seq", "core"))

time: 537 us -> 537 us (level)
    unnamed x132 -> x124, local copies, waits for them, and re-layouts: 16 us -> 15.6 us
  transfers between devices with their start and end apart: 57 -> 57, of which waited for: 22 -> 23; matrix products, arithmetic and copies ran while one was open for 34% -> 34% of each run, Pallas kernels for 6% -> 6%
where the time goes in v8:
time: 537 us; the launch traced here: 531 us
  waiting for transfers between devices  213 us (40%)
  matrix products  106 us (20%)
  starting transfers between devices  61 us (11%)
  other arithmetic  42.3 us (8%)
  local copies, waits for them, and re-layouts  40.7 us (8%)
  Pallas kernels  35.2 us (7%)
  blocking collectives  17.8 us (3%)
  between operations  15.5 us (3%)
    ppermute x45, waiting for transfers between devices, flip(): return lax.ppermute(v, axis, [(i, i ^ q) for i in range(size)])  151 us
    dot_general x23, matrix products, dot(): return jnp.einsum(form, left, right, preferred_element_type=F32)  106 us
    ppermute x45, starting transfers between devices, flip(): return lax.ppermute(v, axis, [(i, i ^ q) for i in range(size)])  44.6 us
    all_gather x1, waiting for transfers between devices, body(): wup = lax.all_gather(up, 'z', axis=0, tiled=True)  21.7 us
    all_to_all x1, blocking collectives, exchange(): return lax.all_to_all(v, axes, split_axis=0, concat_axis=0, tiled=True)  17.8 us
    pallas_call x4, Pallas kernels, attend_call(): pl.pallas_call(functools.partial(kernel, heads), out_shape=jax.ShapeDtype...  17 us
    unnamed x124, local copies, waits for them, and re-layouts  15.6 us
    all_to_all x4, starting transfers between devices, exchange(): return lax.all_to_all(v, axes, split_axis=0, concat_axis=0, tiled=True)  14.8 us
  transfers between devices with their start and end apart: 57, of which 23 were waited for; matrix products, arithmetic and copies ran while one was open for 34% of the time, Pallas kernels for 6%

profile of v8, /device:TPU:0, one launch (start us, length us, event | category | flops | bytes accessed | tf_op | source)
XLA Modules:
  0.0 531.3 jit_solution(5009513195699656055)
XLA Ops:
  11.3 17.8 %all_to_all.29 = bf16[8,64,768]{2,1,0:T(8,128)(2,1)} all-to-all(bf16[8,64,768]{2,1,0:T(8,128)(2,1)S(1)} %copy.55), channel_id=1, replica_groups=mesh['seq'=4,'z'=4,'core'=2] {'seq','core'}, dimensions={0} | all-to-all | bytes 1572864 | tf_op jit(solution)/shard_map/all_to_all | solution.py:207
  29.1 11.2 %all-gather.12.cloned.1.call-done = bf16[256,2048]{1,0:T(8,128)(2,1)} async-done(((bf16[64,2048]{1,0:T(8,128)(2,1)}), bf16[256,2048]{1,0:T(8,128)(2,1)}) %all-gather.12.cloned.1.call-update) | async-done | bytes 1048592 | tf_op jit(solution)/shard_map/all_gather | solution.py:244
  47.2 7.3 %all-to-all-done.1 = bf16[32,2,384]{2,1,0:T(2,128)(2,1)S(1)} async-done(((bf16[32,2,384]{2,1,0:T(2,128)(2,1)}), bf16[32,2,384]{2,1,0:T(2,128)(2,1)S(1)}, u32[]{:S(2)}, u32[]{:S(2)}) %all-to-all-start.1) | async-done | bytes 49184 | tf_op jit(solution)/shard_map/all_to_all | solution.py:207
  67.8 5.2 collective-permute-done.3
  73.0 11.7 %collective-permute-done.4 = bf16[128,2048]{1,0:T(8,128)(2,1)} collective-permute-done((bf16[128,2048]{1,0:T(8,128)(2,1)}, bf16[128,2048]{1,0:T(8,128)(2,1)}, u32[]{:S(2)}, u32[]{:S(2)}) %collective-permute-start.4) | collective-permute-done | bytes 524320 | tf_op jit(solution)/shard_map/ppermute | solution.py:180
  94.6 10.2 %all-gather.6.cloned.1.call-done = bf16[2048,768]{1,0:T(8,128)(2,1)} async-done(((bf16[512,768]{1,0:T(8,128)(2,1)}), bf16[2048,768]{1,0:T(8,128)(2,1)}) %all-gather.6.cloned.1.call-update) | async-done | bytes 3145744 | tf_op jit(solution)/shard_map/all_gather | solution.py:245
  108.5 5.2 add_convert_fusion.1.qkv_ref
  121.5 5.1 add_convert_fusion.2.qkv_ref
  139.5 11.3 %collective-permute-done.10 = bf16[128,2048]{1,0:T(8,128)(2,1)S(1)} collective-permute-done((bf16[128,2048]{1,0:T(8,128)(2,1)}, bf16[128,2048]{1,0:T(8,128)(2,1)S(1)}, u32[]{:S(2)}, u32[]{:S(2)}) %collective-permute-start.10) | collective-permute-done | bytes 524320 | tf_op jit(solution)/shard_map/ppermute | solution.py:180
  150.7 11.7 %collective-permute-done.11 = bf16[128,2048]{1,0:T(8,128)(2,1)S(1)} collective-permute-done((bf16[128,2048]{1,0:T(8,128)(2,1)}, bf16[128,2048]{1,0:T(8,128)(2,1)S(1)}, u32[]{:S(2)}, u32[]{:S(2)}) %collective-permute-start.11) | collective-permute-done | bytes 524320 | tf_op jit(solution)/shard_map/ppermute | solution.py:180
  164.9 21.7 %all-gather.8.cloned.1.call-done = bf16[2048,1024]{1,0:T(8,128)(2,1)} async-done(((bf16[512,1024]{1,0:T(8,128)(2,1)}), bf16[2048,1024]{1,0:T(8,128)(2,1)}) %all-gather.8.cloned.1.call-update) | async-done | bytes 4194320 | tf_op jit(solution)/shard_map/all_gather | solution.py:248
  195.1 11.5 %collective-permute-done.13 = bf16[128,2048]{1,0:T(8,128)(2,1)S(1)} collective-permute-done((bf16[128,2048]{1,0:T(8,128)(2,1)}, bf16[128,2048]{1,0:T(8,128)(2,1)S(1)}, u32[]{:S(2)}, u32[]{:S(2)}) %collective-permute-start.13) | collective-permute-done | bytes 524320 | tf_op jit(solution)/shard_map/ppermute | solution.py:180
  206.6 11.3 %collective-permute-done.14 = bf16[128,2048]{1,0:T(8,128)(2,1)S(1)} collective-permute-done((bf16[128,2048]{1,0:T(8,128)(2,1)}, bf16[128,2048]{1,0:T(8,128)(2,1)S(1)}, u32[]{:S(2)}, u32[]{:S(2)}) %collective-permute-start.14) | collective-permute-done | bytes 524320 | tf_op jit(solution)/shard_map/ppermute | solution.py:180
  225.4 10.5 %collective-permute-done.17 = bf16[128,2048]{1,0:T(8,128)(2,1)S(1)} collective-permute-done((bf16[128,2048]{1,0:T(8,128)(2,1)S(1)}, bf16[128,2048]{1,0:T(8,128)(2,1)S(1)}, u32[]{:S(2)}, u32[]{:S(2)}) %collective-permute-start.17) | collective-permute-done | bytes 524320 | tf_op jit(solution)/shard_map/ppermute | solution.py:180
  236.8 9.0 %collective-permute-done.18 = bf16[128,2048]{1,0:T(8,128)(2,1)S(1)} collective-permute-done((bf16[128,2048]{1,0:T(8,128)(2,1)S(1)}, bf16[128,2048]{1,0:T(8,128)(2,1)S(1)}, u32[]{:S(2)}, u32[]{:S(2)}) %collective-permute-start.18) | collective-permute-done | bytes 524320 | tf_op jit(solution)/shard_map/ppermute | solution.py:180
  249.7 5.3 fusion.57
  255.1 6.5 %multiply_convert_fusion = (bf16[512,1024]{1,0:T(8,128)(2,1)S(1)}, bf16[512,1024]{1,0:T(8,128)(2,1)S(1)}, f32[512,1024]{1,0:T(8,128)}) fusion(f32[1024]{0:T(1024)S(1)} %bitcast.181, f32[512,1024]{1,0:T(8,128)S(1)} %fusion.57, bf16[512,2048]{1,0:T(8,128)(2,1)} %collective-permute-done.16, bf16[2048,1024]{1,0:T(8,128)(2,1)S(1)} %copy-done.50), kind=kOutput, calls=%fused_computation.38 | convolution fusion | flops 2153775104 | bytes 12587008 | tf_op jit(solution)/shard_map/td,df->tf/dot_general | solution.py:22
  266.2 5.1 convolution_convert_fusion
  271.8 6.5 %fusion.20 = bf16[512,1024]{1,0:T(8,128)(2,1)S(1)} fusion(f32[512,1024]{1,0:T(8,128)} %get-tuple-element.180, bf16[512,2048]{1,0:T(8,128)(2,1)} %collective-permute-done.20, bf16[1024,2048]{1,0:T(8,128)(2,1)} %all-gather.10.cloned.1.call-done, f32[1024]{0:T(1024)S(1)} %bitcast.182), kind=kOutput, calls=%fused_computation.33 | convolution fusion | flops 2153250816 | bytes 9441280 | tf_op jit(solution)/shard_map/td,fd->tf/dot_general | solution.py:22
  294.0 11.2 %collective-permute-done.22 = bf16[128,2048]{1,0:T(8,128)(2,1)S(1)} collective-permute-done((bf16[128,2048]{1,0:T(8,128)(2,1)S(1)}, bf16[128,2048]{1,0:T(8,128)(2,1)S(1)}, u32[]{:S(2)}, u32[]{:S(2)}) %collective-permute-start.22) | collective-permute-done | bytes 524320 | tf_op jit(solution)/shard_map/ppermute | solution.py:180
  305.3 11.0 %collective-permute-done.23 = bf16[128,2048]{1,0:T(8,128)(2,1)S(1)} collective-permute-done((bf16[128,2048]{1,0:T(8,128)(2,1)S(1)}, bf16[128,2048]{1,0:T(8,128)(2,1)S(1)}, u32[]{:S(2)}, u32[]{:S(2)}) %collective-permute-start.23) | collective-permute-done | bytes 524320 | tf_op jit(solution)/shard_map/ppermute | solution.py:180
  318.5 8.4 %fusion.4 = bf16[2048,1024]{1,0:T(8,128)(2,1)} fusion(bf16[1024,1024]{1,0:T(8,128)(2,1)S(1)} %constant_dynamic-update-slice_fusion.9, bf16[512,2048]{1,0:T(8,128)(2,1)} %collective-permute-done.16, bf16[512,2048]{1,0:T(8,128)(2,1)} %pad_maximum_fusion.2), kind=kOutput, calls=%fused_computation.11 | convolution fusion | flops 4305453056 | bytes 10485760 | tf_op jit(solution)/shard_map/td,tf->df/dot_general | solution.py:22
  346.2 7.7 %collective-permute-done.26 = bf16[128,2048]{1,0:T(8,128)(2,1)S(1)} collective-permute-done((bf16[128,2048]{1,0:T(8,128)(2,1)S(1)}, bf16[128,2048]{1,0:T(8,128)(2,1)S(1)}, u32[]{:S(2)}, u32[]{:S(2)}) %collective-permute-start.26) | collective-permute-done | bytes 524320 | tf_op jit(solution)/shard_map/ppermute | solution.py:180
  353.9 11.1 %collective-permute-done.27 = bf16[128,2048]{1,0:T(8,128)(2,1)S(1)} collective-permute-done((bf16[128,2048]{1,0:T(8,128)(2,1)S(1)}, bf16[128,2048]{1,0:T(8,128)(2,1)S(1)}, u32[]{:S(2)}, u32[]{:S(2)}) %collective-permute-start.27) | collective-permute-done | bytes 524320 | tf_op jit(solution)/shard_map/ppermute | solution.py:180
  366.6 5.6 %convert_add_fusion.1 = f32[512,2048]{1,0:T(8,128)S(1)} fusion(bf16[512,2048]{1,0:T(8,128)(2,1)} %collective-permute-done.25, bf16[512,1024]{1,0:T(8,128)(2,1)} %copy-done.23, bf16[1024,2048]{1,0:T(8,128)(2,1)} %all-gather.10.cloned.1.call-done), kind=kOutput, calls=%fused_computation.8 | convolution fusion | flops 2149580800 | bytes 11534336 | tf_op jit(solution)/shard_map/tf,fd->td/dot_general | solution.py:22
  385.6 4.9 shard_map.319
  393.5 5.0 shard_map.320
  402.4 5.2 add_convert_fusion
  416.0 5.1 convolution_convert_fusion.4
  432.8 7.1 %fusion.58 = (bf16[512,2048]{1,0:T(8,128)(2,1)}, f32[512,2048]{1,0:T(8,128)}) fusion(bf16[512,2048]{1,0:T(8,128)(2,1)} %collective-permute-done.34, bf16[512,768]{1,0:T(8,128)(2,1)S(1)} %copy-done.25, bf16[2048,768]{1,0:T(8,128)(2,1)} %all-gather.6.cloned.1.call-done), kind=kOutput, calls=%fused_computation.162 | convolution fusion | flops 1613758464 | bytes 12320768 | tf_op jit(solution)/shard_map/te,de->td/dot_general | solution.py:22
  453.0 16.6 %collective-permute-done.35 = bf16[128,2048]{1,0:T(8,128)(2,1)S(1)} collective-permute-done((bf16[128,2048]{1,0:T(8,128)(2,1)S(1)}, bf16[128,2048]{1,0:T(8,128)(2,1)S(1)}, u32[]{:S(2)}, u32[]{:S(2)}) %collective-permute-start.35) | collective-permute-done | bytes 524320 | tf_op jit(solution)/shard_map/ppermute | solution.py:180
  470.4 11.0 %collective-permute-done.37 = bf16[128,2048]{1,0:T(8,128)(2,1)} collective-permute-done((bf16[128,2048]{1,0:T(8,128)(2,1)S(1)}, bf16[128,2048]{1,0:T(8,128)(2,1)}, u32[]{:S(2)}, u32[]{:S(2)}) %collective-permute-start.37) | collective-permute-done | bytes 524320 | tf_op jit(solution)/shard_map/ppermute | solution.py:180
  (360 shorter events, 222.1 us)
Async XLA Ops:
  7.2 33.1 %all-gather.12.cloned.1.call-start = ((), (), s32[]{:S(2)}) async-start(), calls=%async_computation.16 | async-start | bytes 1310720 | tf_op jit(solution)/shard_map/all_gather | solution.py:244
  7.9 96.9 %all-gather.6.cloned.1.call-start = ((), (), s32[]{:S(2)}) async-start(), calls=%async_computation.9 | async-start | bytes 3932160 | tf_op jit(solution)/shard_map/all_gather | solution.py:245
  58.5 26.2 %collective-permute-start.4 = (bf16[128,2048]{1,0:T(8,128)(2,1)}, bf16[128,2048]{1,0:T(8,128)(2,1)}, u32[]{:S(2)}, u32[]{:S(2)}) collective-permute-start(bf16[128,2048]{1,0:T(8,128)(2,1)} %shard_map.314), channel_id=1, source_target_pairs={{0,16},{8,24},{16,0},{24,8},{1,17},{9,25},{17,1},{25,9},{2,18},{10... | collective-permute-start | bytes 1572872 | tf_op jit(solution)/shard_map/ppermute | solution.py:180
  59.2 25.5 %collective-permute-start.5 = (bf16[128,2048]{1,0:T(8,128)(2,1)}, bf16[128,2048]{1,0:T(8,128)(2,1)}, u32[]{:S(2)}, u32[]{:S(2)}) collective-permute-start(bf16[128,2048]{1,0:T(8,128)(2,1)} %shard_map.314), channel_id=1, source_target_pairs={{0,24},{8,16},{16,8},{24,0},{1,25},{9,17},{17,9},{25,1},{2,26},{10... | collective-permute-start | bytes 1572872 | tf_op jit(solution)/shard_map/ppermute | solution.py:180
  64.1 30.5 %all-to-all-start.2 = ((bf16[8,64,1024]{2,1,0:T(8,128)(2,1)}), bf16[8,64,1024]{2,1,0:T(8,128)(2,1)S(1)}, u32[]{:S(2)}, u32[]{:S(2)}) async-start(bf16[8,64,1024]{2,1,0:T(8,128)(2,1)} %reshape.284), calls=%async_computation.2 | async-start | bytes 2097152 | tf_op jit(solution)/shard_map/all_to_all | solution.py:207
  67.7 118.8 %all-gather.8.cloned.1.call-start = ((), (), s32[]{:S(2)}) async-start(), calls=%async_computation.10 | async-start | bytes 5242880 | tf_op jit(solution)/shard_map/all_gather | solution.py:248
  87.6 20.9 %collective-permute-start.8 = (bf16[512,2048]{1,0:T(8,128)(2,1)}, bf16[512,2048]{1,0:T(8,128)(2,1)}, u32[]{:S(2)}, u32[]{:S(2)}) collective-permute-start(bf16[512,2048]{1,0:T(8,128)(2,1)} %pad_maximum_fusion.1), channel_id=1, source_target_pairs={{0,1},{1,0},{2,3},{3,2},{4,5},{5,4},{6,7},{7,6},{8,9},{9,8},{10,11... | collective-permute-start | bytes 6291464 | tf_op jit(solution)/shard_map/ppermute | solution.py:180
  104.9 166.4 %all-gather.10.cloned.1.call-start = ((), (), s32[]{:S(2)}) async-start(), calls=%async_computation.11 | async-start | bytes 5242880 | tf_op jit(solution)/shard_map/all_gather | solution.py:249
  137.2 25.2 %collective-permute-start.11 = (bf16[128,2048]{1,0:T(8,128)(2,1)}, bf16[128,2048]{1,0:T(8,128)(2,1)S(1)}, u32[]{:S(2)}, u32[]{:S(2)}) collective-permute-start(bf16[128,2048]{1,0:T(8,128)(2,1)} %get-tuple-element.129), channel_id=1, source_target_pairs={{0,16},{8,24},{16,0},{24,8},{1,17},{9,25},{17,1},{25,9},{2,18},{10... | collective-permute-start | bytes 1572872 | tf_op jit(solution)/shard_map/ppermute | solution.py:180
  138.7 23.7 %collective-permute-start.12 = (bf16[128,2048]{1,0:T(8,128)(2,1)}, bf16[128,2048]{1,0:T(8,128)(2,1)S(1)}, u32[]{:S(2)}, u32[]{:S(2)}) collective-permute-start(bf16[128,2048]{1,0:T(8,128)(2,1)} %get-tuple-element.128), channel_id=1, source_target_pairs={{0,24},{8,16},{16,8},{24,0},{1,25},{9,17},{17,9},{25,1},{2,26},{10... | collective-permute-start | bytes 1572872 | tf_op jit(solution)/shard_map/ppermute | solution.py:180
  186.5 143.5 %reduce-scatter.5.cloned.1.call-start = ((), (), s32[]{:S(2)}) async-start(), calls=%async_computation.12 | async-start | bytes 3932160 | tf_op jit(solution)/shard_map/reduce_scatter | solution.py:294
  193.1 24.8 %collective-permute-start.14 = (bf16[128,2048]{1,0:T(8,128)(2,1)}, bf16[128,2048]{1,0:T(8,128)(2,1)S(1)}, u32[]{:S(2)}, u32[]{:S(2)}) collective-permute-start(bf16[128,2048]{1,0:T(8,128)(2,1)} %shard_map.317), channel_id=1, source_target_pairs={{0,16},{8,24},{16,0},{24,8},{1,17},{9,25},{17,1},{25,9},{2,18},{10... | collective-permute-start | bytes 1572872 | tf_op jit(solution)/shard_map/ppermute | solution.py:180
  194.6 23.3 %collective-permute-start.15 = (bf16[128,2048]{1,0:T(8,128)(2,1)}, bf16[128,2048]{1,0:T(8,128)(2,1)S(1)}, u32[]{:S(2)}, u32[]{:S(2)}) collective-permute-start(bf16[128,2048]{1,0:T(8,128)(2,1)} %shard_map.317), channel_id=1, source_target_pairs={{0,24},{8,16},{16,8},{24,0},{1,25},{9,17},{17,9},{25,1},{2,26},{10... | collective-permute-start | bytes 1572872 | tf_op jit(solution)/shard_map/ppermute | solution.py:180
  222.0 23.8 %collective-permute-start.18 = (bf16[128,2048]{1,0:T(8,128)(2,1)S(1)}, bf16[128,2048]{1,0:T(8,128)(2,1)S(1)}, u32[]{:S(2)}, u32[]{:S(2)}) collective-permute-start(bf16[128,2048]{1,0:T(8,128)(2,1)S(1)} %bitcast.162), channel_id=1, source_target_pairs={{0,16},{8,24},{16,0},{24,8},{1,17},{9,25},{17,1},{25,9},{2,18},{10... | collective-permute-start | bytes 1572872 | tf_op jit(solution)/shard_map/ppermute | solution.py:180
  223.0 23.7 %collective-permute-start.19 = (bf16[128,2048]{1,0:T(8,128)(2,1)S(1)}, bf16[128,2048]{1,0:T(8,128)(2,1)S(1)}, u32[]{:S(2)}, u32[]{:S(2)}) collective-permute-start(bf16[128,2048]{1,0:T(8,128)(2,1)S(1)} %bitcast.163), channel_id=1, source_target_pairs={{0,24},{8,16},{16,8},{24,0},{1,25},{9,17},{17,9},{25,1},{2,26},{10... | collective-permute-start | bytes 1572872 | tf_op jit(solution)/shard_map/ppermute | solution.py:180
  224.5 30.6 %collective-permute-start.16 = (bf16[512,2048]{1,0:T(8,128)(2,1)}, bf16[512,2048]{1,0:T(8,128)(2,1)}, u32[]{:S(2)}, u32[]{:S(2)}) collective-permute-start(bf16[512,2048]{1,0:T(8,128)(2,1)} %pad_maximum_fusion.2), channel_id=1, source_target_pairs={{0,1},{1,0},{2,3},{3,2},{4,5},{5,4},{6,7},{7,6},{8,9},{9,8},{10,11... | collective-permute-start | bytes 6291464 | tf_op jit(solution)/shard_map/ppermute | solution.py:180
  271.3 143.6 %reduce-scatter.7.cloned.1.call-start = ((), (), s32[]{:S(2)}) async-start(), calls=%async_computation.13 | async-start | bytes 5242880 | tf_op jit(solution)/shard_map/reduce_scatter | solution.py:306
  291.1 25.1 %collective-permute-start.23 = (bf16[128,2048]{1,0:T(8,128)(2,1)S(1)}, bf16[128,2048]{1,0:T(8,128)(2,1)S(1)}, u32[]{:S(2)}, u32[]{:S(2)}) collective-permute-start(bf16[128,2048]{1,0:T(8,128)(2,1)S(1)} %get-tuple-element.126), channel_id=1, source_target_pairs={{0,16},{8,24},{16,0},{24,8},{1,17},{9,25},{17,1},{25,9},{2,18},{10... | collective-permute-start | bytes 1572872 | tf_op jit(solution)/shard_map/ppermute | solution.py:180
  291.3 25.7 %collective-permute-start.24 = (bf16[128,2048]{1,0:T(8,128)(2,1)S(1)}, bf16[128,2048]{1,0:T(8,128)(2,1)}, u32[]{:S(2)}, u32[]{:S(2)}) collective-permute-start(bf16[128,2048]{1,0:T(8,128)(2,1)S(1)} %get-tuple-element.125), channel_id=1, source_target_pairs={{0,24},{8,16},{16,8},{24,0},{1,25},{9,17},{17,9},{25,1},{2,26},{10... | collective-permute-start | bytes 1572872 | tf_op jit(solution)/shard_map/ppermute | solution.py:180
  330.1 161.2 %reduce-scatter.9.cloned.1.call-start = ((), (), s32[]{:S(2)}) async-start(), calls=%async_computation.14 | async-start | bytes 5242880 | tf_op jit(solution)/shard_map/reduce_scatter | solution.py:331
  340.5 24.5 %collective-permute-start.27 = (bf16[128,2048]{1,0:T(8,128)(2,1)S(1)}, bf16[128,2048]{1,0:T(8,128)(2,1)S(1)}, u32[]{:S(2)}, u32[]{:S(2)}) collective-permute-start(bf16[128,2048]{1,0:T(8,128)(2,1)S(1)} %get-tuple-element.108), channel_id=1, source_target_pairs={{0,16},{8,24},{16,0},{24,8},{1,17},{9,25},{17,1},{25,9},{2,18},{10... | collective-permute-start | bytes 1572872 | tf_op jit(solution)/shard_map/ppermute | solution.py:180
  342.0 23.0 %collective-permute-start.28 = (bf16[128,2048]{1,0:T(8,128)(2,1)S(1)}, bf16[128,2048]{1,0:T(8,128)(2,1)S(1)}, u32[]{:S(2)}, u32[]{:S(2)}) collective-permute-start(bf16[128,2048]{1,0:T(8,128)(2,1)S(1)} %get-tuple-element.108), channel_id=1, source_target_pairs={{0,24},{8,16},{16,8},{24,0},{1,25},{9,17},{17,9},{25,1},{2,26},{10... | collective-permute-start | bytes 1572872 | tf_op jit(solution)/shard_map/ppermute | solution.py:180
  346.2 20.4 %collective-permute-start.25 = (bf16[512,2048]{1,0:T(8,128)(2,1)}, bf16[512,2048]{1,0:T(8,128)(2,1)}, u32[]{:S(2)}, u32[]{:S(2)}) collective-permute-start(bf16[512,2048]{1,0:T(8,128)(2,1)} %convolution_convert_fusion.1), channel_id=1, source_target_pairs={{0,1},{1,0},{2,3},{3,2},{4,5},{5,4},{6,7},{7,6},{8,9},{9,8},{10,11... | collective-permute-start | bytes 6291464 | tf_op jit(solution)/shard_map/ppermute | solution.py:180
  377.1 30.4 %collective-permute-start.33 = (bf16[2,64,2048]{2,1,0:T(8,128)(2,1)S(1)}, bf16[2,64,2048]{2,1,0:T(8,128)(2,1)S(1)}, u32[]{:S(2)}, u32[]{:S(2)}) collective-permute-start(bf16[2,64,2048]{2,1,0:T(8,128)(2,1)S(1)} %get-tuple-element.131), channel_id=1, source_target_pairs={{0,1},{1,0},{2,3},{3,2},{4,5},{5,4},{6,7},{7,6},{8,9},{9,8},{10,11... | collective-permute-start | bytes 1572872 | tf_op jit(solution)/shard_map/ppermute | solution.py:180
  379.1 35.8 %collective-permute-start.30 = (bf16[128,2048]{1,0:T(8,128)(2,1)}, bf16[128,2048]{1,0:T(8,128)(2,1)}, u32[]{:S(2)}, u32[]{:S(2)}) collective-permute-start(bf16[128,2048]{1,0:T(8,128)(2,1)} %get-tuple-element.123), channel_id=1, source_target_pairs={{0,8},{8,0},{16,24},{24,16},{1,9},{9,1},{17,25},{25,17},{2,10},{10... | collective-permute-start | bytes 1572872 | tf_op jit(solution)/shard_map/ppermute | solution.py:180
  380.2 34.7 %collective-permute-start.31 = (bf16[128,2048]{1,0:T(8,128)(2,1)}, bf16[128,2048]{1,0:T(8,128)(2,1)}, u32[]{:S(2)}, u32[]{:S(2)}) collective-permute-start(bf16[128,2048]{1,0:T(8,128)(2,1)} %get-tuple-element.122), channel_id=1, source_target_pairs={{0,16},{8,24},{16,0},{24,8},{1,17},{9,25},{17,1},{25,9},{2,18},{10... | collective-permute-start | bytes 1572872 | tf_op jit(solution)/shard_map/ppermute | solution.py:180
  381.2 33.7 %collective-permute-start.32 = (bf16[128,2048]{1,0:T(8,128)(2,1)S(1)}, bf16[128,2048]{1,0:T(8,128)(2,1)}, u32[]{:S(2)}, u32[]{:S(2)}) collective-permute-start(bf16[128,2048]{1,0:T(8,128)(2,1)S(1)} %get-tuple-element.121), channel_id=1, source_target_pairs={{0,24},{8,16},{16,8},{24,0},{1,25},{9,17},{17,9},{25,1},{2,26},{10... | collective-permute-start | bytes 1572872 | tf_op jit(solution)/shard_map/ppermute | solution.py:180
  439.8 41.5 %all-to-all-start.3 = ((bf16[8,64,1024]{2,1,0:T(8,128)(2,1)}), bf16[8,64,1024]{2,1,0:T(8,128)(2,1)S(1)}, u32[]{:S(2)}, u32[]{:S(2)}) async-start(bf16[8,64,1024]{2,1,0:T(8,128)(2,1)} %bitcast.165), calls=%async_computation.5 | async-start | bytes 2097152 | tf_op jit(solution)/shard_map/all_to_all | solution.py:207
  443.4 79.0 %reduce-scatter.11.cloned.1.call-start = ((), (), s32[]{:S(2)}) async-start(), calls=%async_computation.15 | async-start | bytes 1310720 | tf_op jit(solution)/shard_map/reduce_scatter | solution.py:343
  445.2 24.4 %collective-permute-start.35 = (bf16[128,2048]{1,0:T(8,128)(2,1)S(1)}, bf16[128,2048]{1,0:T(8,128)(2,1)S(1)}, u32[]{:S(2)}, u32[]{:S(2)}) collective-permute-start(bf16[128,2048]{1,0:T(8,128)(2,1)S(1)} %get-tuple-element.120), channel_id=1, source_target_pairs={{0,8},{8,0},{16,24},{24,16},{1,9},{9,1},{17,25},{25,17},{2,10},{10... | collective-permute-start | bytes 1572872 | tf_op jit(solution)/shard_map/ppermute | solution.py:180
  447.1 22.4 %collective-permute-start.36 = (bf16[128,2048]{1,0:T(8,128)(2,1)S(1)}, bf16[128,2048]{1,0:T(8,128)(2,1)S(1)}, u32[]{:S(2)}, u32[]{:S(2)}) collective-permute-start(bf16[128,2048]{1,0:T(8,128)(2,1)S(1)} %get-tuple-element.119), channel_id=1, source_target_pairs={{0,16},{8,24},{16,0},{24,8},{1,17},{9,25},{17,1},{25,9},{2,18},{10... | collective-permute-start | bytes 1572872 | tf_op jit(solution)/shard_map/ppermute | solution.py:180
  448.6 32.8 %collective-permute-start.37 = (bf16[128,2048]{1,0:T(8,128)(2,1)S(1)}, bf16[128,2048]{1,0:T(8,128)(2,1)}, u32[]{:S(2)}, u32[]{:S(2)}) collective-permute-start(bf16[128,2048]{1,0:T(8,128)(2,1)S(1)} %get-tuple-element.118), channel_id=1, source_target_pairs={{0,24},{8,16},{16,8},{24,0},{1,25},{9,17},{17,9},{25,1},{2,26},{10... | collective-permute-start | bytes 1572872 | tf_op jit(solution)/shard_map/ppermute | solution.py:180
  (82 other events, 912.1 us)
Sparse Core Ops, SparseCore 0:
  9.6 30.6 all-gather.11
  41.8 62.9 all-gather.5
  107.0 79.4 all-gather.7
  187.9 79.2 all-gather.9
  271.4 58.5 reduce-scatter.4
  332.2 76.7 reduce-scatter.6
  415.1 76.1 reduce-scatter.8
  493.6 27.8 reduce-scatter.10
